TPU v7x, 256 devices: a whole 4x4x8 slice. The times are simulated.
256 devices in a mesh: grp: 16 (over z_hi, x, core), gz: 16 (over z_lo, y).
Axes of the slice: x: 4, y: 4, z: 8 (z_hi: 2, z_lo: 4; z = z_hi * 4 + z_lo), core: 2. Of those that a mesh axis runs over, the one named last changes fastest.
Arguments:
- pet_image: float32 [128, 32, 480], P('gz'), may hold values from 0.5 to 2
- mr_image: float32 [128, 32, 960], P('gz'), may hold values from -6 to 6
- coil_sens: bfloat16 [32, 128, 32, 960], P('grp', 'gz'), may hold values from -0.8984375 to 0.8984375
- kspace_data: bfloat16 [32, 128, 32, 960], P('grp', None, 'gz'), may hold values from -1.1953125 to 1.1953125
- kspace_mask: int32 [128, 480], replicated, may hold values 0 or 1
- system_tiles: bfloat16 [4096, 128, 480], P(('grp', 'gz')), may hold values from 0.0099487305 to 4
- tile_subset_block: int32 [4096], P(('grp', 'gz')), may hold values from 0 to 15
- tile_col: int32 [4096], P(('grp', 'gz')), may hold values from 0 to 255
- measured: float32 [1024, 128], P('grp'), may hold values from 0 to 24
- background: float32 [1024, 128], P('grp'), may hold values from 0.5 to 2
- subset_view_blocks: int32 [256], P('grp'), may hold values from 0 to 63
Outputs:
- grad_pet: float32 [128, 32, 480], P('gz', 'grp')
- grad_mr: float32 [128, 32, 960], P('gz', 'grp')
All inputs are finite; a program needn't handle non-finite values.
Results may differ from a plain program's by a relative error of at most 0.0036.
Values may be sent and summed in bfloat16 or wider, within the bound.
No kernel may reach another device: no remote copies, remote signals or barrier semaphores. Data moves between devices by JAX's collectives and lax.ppermute only.
A program may use at most 64 MiB of HBM per device.

v0:
```python
import math

import jax
import jax.numpy as jnp
from jax import lax
from jax.sharding import PartitionSpec as P

coupling_weight = 0.1
mag_smooth = 0.3
eta_smooth = 0.3


def with_halo(cells, sides, width):
    for axis, dim in sides:
        count = lax.axis_size(axis)
        ends = count - 1
        head = lax.slice_in_dim(cells, 0, width, axis=dim)
        tail = lax.slice_in_dim(cells, cells.shape[dim] - width, cells.shape[dim], axis=dim)
        cells = jnp.concatenate(
            [
                lax.ppermute(tail, axis, [(i, (i + 1) % count) for i in range(ends)]),
                cells,
                lax.ppermute(head, axis, [((i + 1) % count, i) for i in range(ends)]),
            ],
            axis=dim,
        )
    return cells


def dft_parts(length):
    indices = jnp.arange(length, dtype=jnp.int32)
    product = indices[:, None] * indices[None, :] % length
    angles = product.astype(jnp.float32) * (2.0 * math.pi / length)
    scaling = 1.0 / math.sqrt(length)
    return (
        (jnp.cos(angles) * scaling).astype(jnp.bfloat16),
        (-jnp.sin(angles) * scaling).astype(jnp.bfloat16),
    )


def y_table(length):
    real_part, imag_part = dft_parts(length)
    upper_half = jnp.concatenate([real_part, imag_part], 1)
    lower_half = jnp.concatenate([-imag_part, real_part], 1)
    return jnp.concatenate([upper_half, lower_half], 0)


def z_table(length):
    real_part, imag_part = dft_parts(length)
    return jnp.concatenate([real_part, imag_part], 0)


def complex_mul(left_part, right_part, width):
    left_re, left_im = (left_part[..., :width], left_part[..., width:])
    right_re, right_im = (right_part[..., :width], right_part[..., width:])
    return jnp.concatenate(
        [left_re * right_re - left_im * right_im, left_re * right_im + left_im * right_re], -1
    )


def complex_mul_conj(left_part, right_part, width):
    left_re, left_im = (left_part[..., :width], left_part[..., width:])
    right_re, right_im = (right_part[..., :width], right_part[..., width:])
    return jnp.concatenate(
        [left_re * right_re + left_im * right_im, left_re * right_im - left_im * right_re], -1
    )


def z_apply(dft_table, volume, depth, width, inverse):
    product = jnp.einsum("kz,czxn->ckxn", dft_table, volume, preferred_element_type=jnp.float32)
    upper_half, lower_half = (product[:, :depth], product[:, depth:])
    if inverse:
        real_part = upper_half[..., :width] + lower_half[..., width:]
        imag_part = upper_half[..., width:] - lower_half[..., :width]
    else:
        real_part = upper_half[..., :width] - lower_half[..., width:]
        imag_part = upper_half[..., width:] + lower_half[..., :width]
    return jnp.concatenate([real_part, imag_part], -1)


def forward_diff(volume, dim_index):
    extent = volume.shape[dim_index]
    ahead_part = lax.slice_in_dim(volume, 1, extent, axis=dim_index)
    here_part = lax.slice_in_dim(volume, 0, extent - 1, axis=dim_index)
    closing = jnp.zeros_like(lax.slice_in_dim(volume, 0, 1, axis=dim_index))
    return jnp.concatenate([ahead_part - here_part, closing], dim_index)


def local_coupling(extended, z_start, nz_all):
    width = extended.shape[-1] // 3
    slices = extended.shape[0] - 1
    pet_ext = extended[..., :width]
    magnitude = jnp.sqrt(
        extended[..., width : 2 * width] ** 2 + extended[..., 2 * width :] ** 2 + mag_smooth**2
    )
    level_values = z_start - 1 + jnp.arange(slices, dtype=jnp.int32)
    keep_term = (level_values >= 0).astype(jnp.float32)[:, None, None]
    keep_step = (level_values < nz_all - 1).astype(jnp.float32)[:, None, None]

    def differences(volume):
        step_z = (volume[1:] - volume[:-1]) * keep_step
        head_part = volume[:-1]
        return (step_z, forward_diff(head_part, 1), forward_diff(head_part, 2))

    pet_diffs = differences(pet_ext)
    mag_diffs = differences(magnitude)
    pet_sq = pet_diffs[0] ** 2 + pet_diffs[1] ** 2 + pet_diffs[2] ** 2
    mag_sq = mag_diffs[0] ** 2 + mag_diffs[1] ** 2 + mag_diffs[2] ** 2
    cross = pet_diffs[0] * mag_diffs[0] + pet_diffs[1] * mag_diffs[1] + pet_diffs[2] * mag_diffs[2]
    level_terms = jnp.sqrt(eta_smooth**2 + pet_sq * mag_sq - cross * cross)
    return jnp.sum(level_terms * keep_term)


def pet_ratio(projection, measured, background, view_numbers):
    selected_counts = jnp.take(measured, view_numbers, axis=0)
    back_sel = jnp.take(background, view_numbers, axis=0)
    return (1.0 - selected_counts / (projection + back_sel)).astype(jnp.bfloat16)


def on_device(
    pet_image,
    mr_image,
    coil_sens,
    kspace_data,
    kspace_mask,
    system_tiles,
    tile_subset_block,
    tile_col,
    measured,
    background,
    subset_view_blocks,
):
    slab_len, row_len, width = pet_image.shape
    groups_z = lax.axis_size("gz")
    depth = slab_len * groups_z
    coils_here = coil_sens.shape[0]
    ky_table = y_table(width)
    kz_table = z_table(depth)
    mask_float = kspace_mask.astype(jnp.float32)
    mask_wide = jnp.concatenate([mask_float, mask_float], -1)[None, :, None, :]
    joined = jnp.concatenate([pet_image, mr_image], -1)
    extended = with_halo(joined, (("gz", 0),), 1)
    voxel_rows = slab_len * row_len
    sub_count = subset_view_blocks.shape[0]
    pet_rows = pet_image.astype(jnp.bfloat16).reshape(voxel_rows, width)
    col_hot = tile_col[:, None] == jnp.arange(voxel_rows, dtype=jnp.int32)[None, :]
    row_hot = tile_subset_block[:, None] == jnp.arange(sub_count, dtype=jnp.int32)[None, :]
    picked = jnp.dot(
        col_hot.astype(jnp.bfloat16), pet_rows, preferred_element_type=jnp.float32
    ).astype(jnp.bfloat16)
    projected = jnp.einsum("kbn,kn->kb", system_tiles, picked, preferred_element_type=jnp.float32)
    partial_bins = jnp.dot(
        row_hot.astype(jnp.float32).T, projected, precision=lax.Precision.HIGHEST
    )
    whole_bins = lax.psum(partial_bins, "gz") / width
    ratio_all = pet_ratio(whole_bins, measured, background, subset_view_blocks)
    picked_ratio = jnp.dot(
        row_hot.astype(jnp.bfloat16), ratio_all, preferred_element_type=jnp.float32
    ).astype(jnp.bfloat16)
    spread = jnp.einsum(
        "kbn,kb->kn", system_tiles, picked_ratio, preferred_element_type=jnp.float32
    )
    pet_fit = (
        jnp.dot(col_hot.astype(jnp.float32).T, spread, precision=lax.Precision.HIGHEST) / width
    )
    pet_fit = pet_fit.reshape(slab_len, row_len, width)
    mr_fit = jnp.zeros(mr_image.shape, jnp.float32)
    for coil_index in range(coils_here):
        sens_part = coil_sens[coil_index : coil_index + 1]
        coil_image = complex_mul(sens_part.astype(jnp.float32), mr_image, width).astype(
            jnp.bfloat16
        )
        flat_part = jnp.dot(
            coil_image.reshape(-1, 2 * width), ky_table, preferred_element_type=jnp.float32
        )
        slab_one = flat_part.astype(jnp.bfloat16).reshape(coil_image.shape)
        pencil = lax.all_to_all(slab_one, "gz", split_axis=2, concat_axis=1, tiled=True)
        kspace = z_apply(kz_table, pencil, depth, width, False)
        misfit = (
            mask_wide * (kspace - kspace_data[coil_index : coil_index + 1].astype(jnp.float32))
        ).astype(jnp.bfloat16)
        back_pencil = z_apply(kz_table, misfit, depth, width, True).astype(jnp.bfloat16)
        returned = lax.all_to_all(back_pencil, "gz", split_axis=1, concat_axis=2, tiled=True)
        image_back = jnp.dot(
            returned.reshape(-1, 2 * width), ky_table.T, preferred_element_type=jnp.float32
        )
        image_back = image_back.reshape(returned.shape)
        mr_fit = mr_fit + jnp.sum(
            complex_mul_conj(sens_part.astype(jnp.float32), image_back, width), axis=0
        )
    z_start = lax.axis_index("gz") * slab_len
    value_out, pullback = jax.vjp(
        lambda ext_values: local_coupling(ext_values, z_start, depth), extended
    )
    grad_ext = pullback(jnp.ones((), jnp.float32))[0]
    grad_own = grad_ext[1:-1]
    group_fits = jnp.concatenate([pet_fit, mr_fit], -1)
    group_amounts = row_len // lax.axis_size("grp")
    row_start = lax.axis_index("grp") * group_amounts
    summed = lax.psum(group_fits, "grp")
    own_fit = lax.dynamic_slice_in_dim(summed, row_start, group_amounts, 1)
    own_couple = lax.dynamic_slice_in_dim(grad_own, row_start, group_amounts, 1)
    combined = own_fit + coupling_weight * own_couple
    return (combined[..., :width], combined[..., width:])


def solution(mesh):
    placed = (
        P("gz", None, None),
        P("gz", None, None),
        P("grp", "gz", None, None),
        P("grp", None, "gz", None),
        P(),
        P(("grp", "gz"), None, None),
        P(("grp", "gz")),
        P(("grp", "gz")),
        P("grp", None),
        P("grp", None),
        P("grp"),
    )
    return jax.shard_map(
        on_device,
        mesh=mesh,
        in_specs=placed,
        out_specs=(P("gz", "grp", None), P("gz", "grp", None)),
        check_vma=False,
    )
```

profile of v0, /device:TPU:6, one launch (start us, length us, event | category | flops | bytes accessed | tf_op | source)
XLA Modules:
  0.0 371.2 jit_solution(94410011626286174)
XLA Ops:
  7.2 2.1 fusion.66
  9.2 4.2 %collective-permute-start = (f32[1,32,1440]{2,1,0:T(8,128)}, f32[1,32,1440]{2,1,0:T(8,128)}, u32[]{:S(2)}, u32[]{:S(2)}) collective-permute-start(f32[1,32,1440]{2,1,0:T(8,128)} %get-tuple-element.46), channel_id=1, source_target_pairs={{0,1},{1,2},{2,3},{3,4},{4,5},{5,6},{6,7},{7,8},{8,9},{9,10},{10,1... | collective-permute-start | bytes 552968 | tf_op jit(solution)/shard_map/ppermute | solution.py:21
  13.4 1.3 collective-permute-start.1
  14.7 3.9 %fusion.67 = bf16[480,480]{1,0:T(8,128)(2,1)S(1)} fusion(), kind=kLoop, calls=%fused_computation.150 | loop fusion | flops 3456000 | bytes 460800 | tf_op jit(solution)/shard_map/neg | solution.py:44
  18.6 3.9 %multiply_convert_fusion = bf16[480,480]{1,0:T(8,128)(2,1)S(1)} fusion(), kind=kLoop, calls=%fused_computation.48 | loop fusion | flops 2764800 | bytes 460800 | tf_op jit(solution)/shard_map/convert_element_type | solution.py:37
  22.5 3.8 %multiply_convert_fusion.1 = bf16[480,480]{1,0:T(8,128)(2,1)S(1)} fusion(), kind=kLoop, calls=%fused_computation.49 | loop fusion | flops 2534400 | bytes 460800 | tf_op jit(solution)/shard_map/convert_element_type | solution.py:36
  26.7 1.5 fusion.48
  28.1 1.7 convolution_convert_fusion.1
  31.2 9.6 %all-to-all-start = ((bf16[1,8,32,960]{3,1,0,2:T(8,128)(2,1)}), bf16[1,8,32,960]{3,1,0,2:T(8,128)(2,1)}, u32[]{:S(2)}, u32[]{:S(2)}) async-start(bf16[1,8,32,960]{3,1,0,2:T(8,128)(2,1)} %copy.33), calls=%async_computation | async-start | bytes 1048576 | tf_op jit(solution)/shard_map/all_to_all | solution.py:177
  40.8 1.8 pad_maximum_fusion
  44.8 1.6 convert_element_type.118
  46.5 4.1 %convolution_convert_fusion = bf16[256,960]{0,1:T(8,128)(2,1)} fusion(bf16[256,480]{1,0:T(8,128)(2,1)} %bitcast.128, bf16[256,480]{1,0:T(8,128)(2,1)} %bitcast.127, bf16[480,480]{1,0:T(8,128)(2,1)} %copy-done.31, bf16[480,480]{1,0:T(8,128)(2,1)} %copy-done.29, bf16[480,480]{1,0:T(8,128)(2,1)} %copy-done.30), kind=kOutput, calls=%fused_computation.31 | convolution fusion | flops 480460800 | bytes 2365440 | tf_op jit(solution)/shard_map/dot_general | solution.py:173
  50.6 2.0 copy.39
  52.6 2.1 copy.40
  55.4 1.3 gather_fusion
  56.7 1.4 gather_fusion.1
  58.1 1.2 fusion.10
  60.7 45.0 %psum.14 = f32[16,128]{1,0:T(8,128)} all-reduce(f32[16,128]{1,0:T(8,128)} %fusion.85), channel_id=1, replica_groups=mesh['grp'=16,'gz'=16] {'gz'}, use_global_device_ids=true, to_apply=%region_0.2 | all-reduce | flops 2048 | bytes 16384 | tf_op jit(solution)/shard_map/psum | solution.py:155
  107.4 1.3 convolution_multiply_fusion
  108.6 2.0 copy.31
  111.5 1.9 pad_maximum_fusion.7
  113.4 1.8 fusion.23
  115.2 1.4 add_sqrt_fusion
  118.6 4.3 %all-to-all-start.2 = ((bf16[1,8,32,960]{3,1,0,2:T(8,128)(2,1)}), bf16[1,8,32,960]{3,1,0,2:T(8,128)(2,1)}, u32[]{:S(2)}, u32[]{:S(2)}) async-start(bf16[1,8,32,960]{3,1,0,2:T(8,128)(2,1)} %copy.40), calls=%async_computation.2 | async-start | bytes 1048576 | tf_op jit(solution)/shard_map/all_to_all | solution.py:177
  122.8 1.5 convolution_bitcast_fusion.3
  127.1 2.0 copy.36
  129.1 6.1 %all-to-all-done.2 = bf16[1,8,32,960]{3,1,0,2:T(8,128)(2,1)} async-done(((bf16[1,8,32,960]{3,1,0,2:T(8,128)(2,1)}), bf16[1,8,32,960]{3,1,0,2:T(8,128)(2,1)}, u32[]{:S(2)}, u32[]{:S(2)}) %all-to-all-start.2) | async-done | bytes 491552 | tf_op jit(solution)/shard_map/all_to_all | solution.py:177
  135.2 4.3 %all-to-all-start.1 = ((bf16[1,128,2,960]{3,2,0,1:T(2,128)(2,1)}), bf16[1,128,2,960]{3,2,0,1:T(2,128)(2,1)}, u32[]{:S(2)}, u32[]{:S(2)}) async-start(bf16[1,128,2,960]{3,2,0,1:T(2,128)(2,1)} %copy.36), calls=%async_computation.1 | async-start | bytes 1048576 | tf_op jit(solution)/shard_map/all_to_all | solution.py:183
  139.4 1.5 convolution_bitcast_fusion.1
  143.7 2.0 copy.43
  145.7 6.2 %all-to-all-done.1 = bf16[1,128,2,960]{3,2,0,1:T(2,128)(2,1)} async-done(((bf16[1,128,2,960]{3,2,0,1:T(2,128)(2,1)}), bf16[1,128,2,960]{3,2,0,1:T(2,128)(2,1)}, u32[]{:S(2)}, u32[]{:S(2)}) %all-to-all-start.1) | async-done | bytes 491552 | tf_op jit(solution)/shard_map/all_to_all | solution.py:183
  151.8 6.2 %all-to-all-start.3 = ((bf16[1,128,2,960]{3,2,0,1:T(2,128)(2,1)}), bf16[1,128,2,960]{3,2,0,1:T(2,128)(2,1)}, u32[]{:S(2)}, u32[]{:S(2)}) async-start(bf16[1,128,2,960]{3,2,0,1:T(2,128)(2,1)} %copy.43), calls=%async_computation.3 | async-start | bytes 1048576 | tf_op jit(solution)/shard_map/all_to_all | solution.py:183
  158.1 1.2 fusion.25
  159.6 3.1 fusion.98
  162.7 1.2 copy.71
  163.8 1.3 copy.38
  165.2 2.2 reshape.166
  167.4 3.4 fusion.4
  170.8 1.1 copy.70
  172.0 1.4 copy.45
  173.3 2.2 reshape.170
  175.6 2.6 fusion.7
  179.9 1.5 pad_maximum_fusion.1
  181.5 3.2 fusion.106
  186.9 2.8 multiply_multiply_fusion.1
  189.7 2.1 multiply_multiply_fusion
  191.7 170.0 %all-reduce.23.cloned.1.call-done = f32[8,32,1440]{2,1,0:T(8,128)} async-done(((f32[8,32,1440]{2,1,0:T(8,128)}), f32[8,32,1440]{2,1,0:T(8,128)}) %all-reduce.23.cloned.1.call-update) | async-done | bytes 1474576 | tf_op jit(solution)/shard_map/psum | solution.py:200
  361.7 1.3 multiply_add_fusion.5
  (111 shorter events, 21.3 us)
Async XLA Ops:
  7.2 52.1 %copy-start = (bf16[16,128,480]{1,2,0:T(8,128)(2,1)S(1)}, bf16[16,128,480]{1,2,0:T(8,128)(2,1)}, u32[]{:S(2)}) copy-start(bf16[16,128,480]{1,2,0:T(8,128)(2,1)} %param.18) | copy-start | bytes 5898244
  7.2 19.2 %copy-start.21 = (bf16[2,8,32,960]{3,2,1,0:T(8,128)(2,1)S(1)}, bf16[2,8,32,960]{3,2,1,0:T(8,128)(2,1)}, u32[]{:S(2)}) copy-start(bf16[2,8,32,960]{3,2,1,0:T(8,128)(2,1)} %param.15) | copy-start | bytes 2949124
  9.2 104.2 %collective-permute-start = (f32[1,32,1440]{2,1,0:T(8,128)}, f32[1,32,1440]{2,1,0:T(8,128)}, u32[]{:S(2)}, u32[]{:S(2)}) collective-permute-start(f32[1,32,1440]{2,1,0:T(8,128)} %get-tuple-element.46), channel_id=1, source_target_pairs={{0,1},{1,2},{2,3},{3,4},{4,5},{5,6},{6,7},{7,8},{8,9},{9,10},{10,1... | collective-permute-start | bytes 552968 | tf_op jit(solution)/shard_map/ppermute | solution.py:21
  13.4 101.8 %collective-permute-start.1 = (f32[1,32,1440]{2,1,0:T(8,128)}, f32[1,32,1440]{2,1,0:T(8,128)}, u32[]{:S(2)}, u32[]{:S(2)}) collective-permute-start(f32[1,32,1440]{2,1,0:T(8,128)} %get-tuple-element.45), channel_id=1, source_target_pairs={{1,0},{2,1},{3,2},{4,3},{5,4},{6,5},{7,6},{8,7},{9,8},{10,9},{11,1... | collective-permute-start | bytes 552968 | tf_op jit(solution)/shard_map/ppermute | solution.py:23
  18.6 9.5 %copy-start.29 = (bf16[480,480]{1,0:T(8,128)(2,1)}, bf16[480,480]{1,0:T(8,128)(2,1)S(1)}, u32[]{:S(2)}) copy-start(bf16[480,480]{1,0:T(8,128)(2,1)S(1)} %fusion.67) | copy-start | bytes 1382404
  18.6 8.1 %copy-start.11 = (f32[8,32,960]{2,1,0:T(8,128)S(1)}, f32[8,32,960]{2,1,0:T(8,128)}, u32[]{:S(2)}) copy-start(f32[8,32,960]{2,1,0:T(8,128)} %param.14) | copy-start | bytes 2949124
  22.5 5.6 %copy-start.30 = (bf16[480,480]{1,0:T(8,128)(2,1)}, bf16[480,480]{1,0:T(8,128)(2,1)S(1)}, u32[]{:S(2)}) copy-start(bf16[480,480]{1,0:T(8,128)(2,1)S(1)} %multiply_convert_fusion) | copy-start | bytes 1382404
  26.4 1.8 copy-start.31
  26.6 1.5 copy-start.12
  26.6 1.5 copy-start.14
  31.2 87.4 %all-to-all-start = ((bf16[1,8,32,960]{3,1,0,2:T(8,128)(2,1)}), bf16[1,8,32,960]{3,1,0,2:T(8,128)(2,1)}, u32[]{:S(2)}, u32[]{:S(2)}) async-start(bf16[1,8,32,960]{3,1,0,2:T(8,128)(2,1)} %copy.33), calls=%async_computation | async-start | bytes 1048576 | tf_op jit(solution)/shard_map/all_to_all | solution.py:177
  40.8 2.7 copy-start.17
  40.8 3.4 copy-start.34
  54.8 0.6 copy-start.32
  58.1 1.7 copy-start.35
  105.6 1.8 copy-start.33
  116.7 0.8 copy-start.1
  118.6 16.6 %all-to-all-start.2 = ((bf16[1,8,32,960]{3,1,0,2:T(8,128)(2,1)}), bf16[1,8,32,960]{3,1,0,2:T(8,128)(2,1)}, u32[]{:S(2)}, u32[]{:S(2)}) async-start(bf16[1,8,32,960]{3,1,0,2:T(8,128)(2,1)} %copy.40), calls=%async_computation.2 | async-start | bytes 1048576 | tf_op jit(solution)/shard_map/all_to_all | solution.py:177
  124.3 1.0 copy-start.18
  124.3 1.3 copy-start.23
  124.3 1.3 copy-start.25
  124.4 1.3 copy-start.27
  135.2 16.6 %all-to-all-start.1 = ((bf16[1,128,2,960]{3,2,0,1:T(2,128)(2,1)}), bf16[1,128,2,960]{3,2,0,1:T(2,128)(2,1)}, u32[]{:S(2)}, u32[]{:S(2)}) async-start(bf16[1,128,2,960]{3,2,0,1:T(2,128)(2,1)} %copy.36), calls=%async_computation.1 | async-start | bytes 1048576 | tf_op jit(solution)/shard_map/all_to_all | solution.py:183
  140.9 1.0 copy-start.19
  140.9 1.3 copy-start.24
  140.9 1.3 copy-start.26
  140.9 1.3 copy-start.28
  151.8 19.0 %all-to-all-start.3 = ((bf16[1,128,2,960]{3,2,0,1:T(2,128)(2,1)}), bf16[1,128,2,960]{3,2,0,1:T(2,128)(2,1)}, u32[]{:S(2)}, u32[]{:S(2)}) async-start(bf16[1,128,2,960]{3,2,0,1:T(2,128)(2,1)} %copy.43), calls=%async_computation.3 | async-start | bytes 1048576 | tf_op jit(solution)/shard_map/all_to_all | solution.py:183
  158.0 203.7 %all-reduce.23.cloned.1.call-start = ((), (), s32[]{:S(2)}) async-start(), calls=%async_computation.4 | async-start | bytes 3145728 | tf_op jit(solution)/shard_map/psum | solution.py:200
  158.1 1.3 copy-start.2
  158.1 1.4 copy-start.3
  158.1 1.5 copy-start.7
  159.4 3.3 copy-start.9
  159.6 3.1 copy-start.5
  175.6 2.6 copy-start.13
  175.6 2.6 copy-start.15
  175.6 2.6 copy-start.22
  178.9 1.0 copy-start.20
  181.5 3.2 copy-start.4
  181.5 3.2 copy-start.10
  181.5 3.2 copy-start.16
  184.7 1.1 copy-start.6
  184.8 1.2 copy-start.8
Sparse Core Ops, SparseCore 0:
  181.6 180.0 all-reduce.22
where the time goes:
time: 376 us; the launch traced here: 371 us
  waiting for transfers between devices  182 us (48%)
  other arithmetic  47.8 us (13%)
  blocking collectives  45 us (12%)
  local copies, waits for them, and re-layouts  30.7 us (8%)
  starting transfers between devices  29.8 us (8%)
  matrix products  21.1 us (6%)
  between operations  14.6 us (4%)
    psum x1, waiting for transfers between devices, on_device(): summed = lax.psum(group_fits, 'grp')  170 us
    psum x1, blocking collectives, on_device(): whole_bins = lax.psum(partial_bins, 'gz') / width  45 us
    all_to_all x2, starting transfers between devices, on_device(): lax.all_to_all(slab_one, 'gz', split_axis=2, concat_axis=1, tiled=True)  13.8 us
    all_to_all x2, starting transfers between devices, on_device(): lax.all_to_all(back_pencil, 'gz', split_axis=1, concat_axis=2, tiled=True)  10.5 us
  transfers between devices with their start and end apart: 7, of which 3 were waited for; matrix products, arithmetic and copies ran while one was open for 21% of the time, Pallas kernels for 0%

commit v1 on v0

v1 whole, which is shorter than its diff:
```python
import math

import jax
import jax.numpy as jnp
import numpy as np
from jax import lax
from jax.experimental import pallas as pl
from jax.experimental.pallas import tpu as pltpu
from jax.sharding import Mesh, PartitionSpec as P

coupling_weight = 0.1
mag_smooth = 0.3
eta_smooth = 0.3

ZS, NX, NY, NZ = 8, 32, 480, 128
HALF = 512
ROW = 2 * HALF
CHUNK = ROW + HALF // 2
GRP = ("zh", "x", "c")
GZ = ("zl", "y")
f32, bf16 = jnp.float32, jnp.bfloat16

SMEM = pl.BlockSpec(memory_space=pltpu.SMEM)
VMEM = pl.BlockSpec(memory_space=pltpu.VMEM)


def dft_parts(length):
    indices = np.arange(length)
    angles = (indices[:, None] * indices[None, :] % length) * (2.0 * math.pi / length)
    scaling = 1.0 / math.sqrt(length)
    return np.cos(angles) * scaling, -np.sin(angles) * scaling


def y_table():
    real_part, imag_part = dft_parts(NY)
    table = np.zeros((2, HALF, 2, HALF), np.float64)
    table[0, :NY, 0, :NY] = real_part
    table[0, :NY, 1, :NY] = imag_part
    table[1, :NY, 0, :NY] = -imag_part
    table[1, :NY, 1, :NY] = real_part
    return jnp.asarray(table.reshape(ROW, ROW).astype(jnp.bfloat16))


def z_table():
    real_part, imag_part = dft_parts(NZ)
    table = np.block([[real_part, -imag_part], [imag_part, real_part]])
    return jnp.asarray(table.astype(jnp.bfloat16))


def call(kernel, out_shape, in_specs, scratch, flops, moved, name):
    return pl.pallas_call(
        kernel,
        out_shape=out_shape,
        in_specs=in_specs,
        out_specs=jax.tree.map(lambda _: VMEM, out_shape),
        scratch_shapes=scratch,
        compiler_params=pltpu.CompilerParams(vmem_limit_bytes=40 * 1024 * 1024),
        cost_estimate=pl.CostEstimate(flops=flops, bytes_accessed=moved, transcendentals=0),
        name=name,
    )


def pack_kernel(core_ref, sens_ref, mr_ref, out_ref, sens_rows, mr_rows):
    imag = core_ref[0] == 1
    last = NY - 3 * 128
    for part in range(2):
        sens_rows[4 * part + 3, :, last:] = jnp.zeros((2 * ZS * NX, 128 - last), f32)
    mr_rows[3, :, last:] = jnp.zeros((ZS * NX, 128 - last), f32)
    for q in range(2 * ZS):
        rows = pl.ds(q * NX, NX)
        for part in range(2):
            values = sens_ref[rows, part * NY : (part + 1) * NY].astype(f32)
            for b in range(4):
                block = values[:, 128 * b : min(128 * (b + 1), NY)]
                sens_rows[4 * part + b, rows, : block.shape[1]] = block
    for q in range(ZS):
        rows = pl.ds(q * NX, NX)
        values = jnp.where(imag, mr_ref[rows, NY:], mr_ref[rows, :NY])
        for b in range(4):
            block = values[:, 128 * b : min(128 * (b + 1), NY)]
            mr_rows[b, rows, : block.shape[1]] = block
    for x in range(NX):
        place = (x % 2) * (NX // 2) + x // 2
        for b in range(8):
            block = sens_rows[b, pl.ds(x, 2 * ZS, stride=NX), :]
            out_ref[place, :, 128 * b : 128 * (b + 1)] = block.astype(bf16)
        for b in range(2):
            block = jnp.concatenate(
                [mr_rows[b, pl.ds(x, ZS, stride=NX), :], mr_rows[b + 2, pl.ds(x, ZS, stride=NX), :]], 0
            )
            out_ref[place, :, ROW + 128 * b : ROW + 128 * (b + 1)] = block.astype(bf16)


def project_kernel(
    col_ref, block_ref, xs_ref, pet_ref, mr_ref, tiles_ref,
    bins_ref, win_ref, low_ref, high_ref, picked,
):
    for t in range(16):
        picked[pl.ds(t, 1), :] = pet_ref[pl.ds(col_ref[t], 1), :]
    rows = picked[...].astype(bf16)
    bins_ref[...] = jnp.zeros((16, 128), f32)
    for t in range(16):
        product = lax.dot_general(
            rows, tiles_ref[t], (((1,), (1,)), ((), ())), preferred_element_type=f32
        )
        place = pl.ds(block_ref[t], 1)
        bins_ref[place, :] = bins_ref[place, :] + product[t : t + 1, :]
    win_ref[...] = jnp.zeros((12, ZS, HALF), f32)
    low_ref[...] = jnp.zeros((16, HALF), f32)
    high_ref[...] = jnp.zeros((16, HALF), f32)
    for r in range(4):
        for z in range(ZS):
            place = pl.ds(xs_ref[r] + z * NX, 1)
            win_ref[r, z : z + 1, :NY] = pet_ref[place, :]
            win_ref[4 + r, z : z + 1, :NY] = mr_ref[place, :NY]
            win_ref[8 + r, z : z + 1, :NY] = mr_ref[place, NY:]
    for r in range(12):
        low_ref[pl.ds(r, 1), :] = win_ref[r, 0:1, :]
        high_ref[pl.ds(r, 1), :] = win_ref[r, ZS - 1 : ZS, :]


def backproject_kernel(
    col_ref, block_ref, view_ref, bins_ref, measured_ref, background_ref, tiles_ref,
    out_ref, ratio, gathered, acc,
):
    for j in range(16):
        counts = measured_ref[pl.ds(view_ref[j], 1), :]
        back = background_ref[pl.ds(view_ref[j], 1), :]
        projection = bins_ref[j : j + 1, :] / NY
        ratio[j : j + 1, :] = 1.0 - counts / (projection + back)
    for t in range(16):
        gathered[t : t + 1, :] = ratio[pl.ds(block_ref[t], 1), :]
    rows = gathered[...].astype(bf16)
    acc[...] = jnp.zeros((4, ZS * NX, 128), f32)
    for t in range(16):
        spread = jnp.dot(rows, tiles_ref[t], preferred_element_type=f32)
        place = pl.ds(col_ref[t], 1)
        for b in range(4):
            block = spread[t : t + 1, 128 * b : min(128 * (b + 1), NY)]
            lanes = slice(0, block.shape[1])
            acc[b, place, lanes] = acc[b, place, lanes] + block
    for p in range(16):
        for k in range(2):
            for b in range(4):
                block = acc[b, pl.ds(2 * p + k, ZS, stride=NX), :] / NY
                first = k * HALF + 128 * b
                out_ref[p, :, first : first + 128] = block.astype(bf16)


def coupling_kernel(
    info_ref, win_ref, prev_ref, next_ref, pet_out, mr_out, planes, mags, moved
):
    z_start, x_first = info_ref[0], info_ref[1]
    planes[...] = jnp.zeros((12, 24, HALF), f32)
    for r in range(12):
        planes[r, 0:1, :] = prev_ref[r : r + 1, :]
        planes[r, 1 : ZS + 1, :] = win_ref[r]
        planes[r, ZS + 1 : ZS + 2, :] = next_ref[r : r + 1, :]
    for r in range(4):
        mags[r] = jnp.sqrt(planes[4 + r] ** 2 + planes[8 + r] ** 2 + mag_smooth**2)
    shape = (16, HALF)
    level = z_start - 1 + lax.broadcasted_iota(jnp.int32, shape, 0)
    lane = lax.broadcasted_iota(jnp.int32, shape, 1)
    step_z = level < NZ - 1
    step_y = lane < NY - 1
    term_z = (level >= 0) & (lane < NY)

    def differences(ref, r, step_x):
        here = ref[r, 0:16, :]
        along_z = jnp.where(step_z, ref[r, 1:17, :] - here, 0.0)
        along_x = jnp.where(step_x, ref[r + 1, 0:16, :] - here, 0.0)
        along_y = jnp.where(step_y, pltpu.roll(here, HALF - 1, 1) - here, 0.0)
        return along_z, along_x, along_y

    grads = []
    for r in range(3):
        place = x_first - 1 + r
        step_x = place < NX - 1
        a = differences(planes, r, step_x)
        b = differences(mags, r, step_x)
        a_sq = a[0] ** 2 + a[1] ** 2 + a[2] ** 2
        b_sq = b[0] ** 2 + b[1] ** 2 + b[2] ** 2
        cross = a[0] * b[0] + a[1] * b[1] + a[2] * b[2]
        weight = lax.rsqrt(eta_smooth**2 + a_sq * b_sq - cross * cross)
        weight = jnp.where(term_z & (place >= 0), weight, 0.0)
        grads.append(
            (
                [(p * b_sq - q * cross) * weight for p, q in zip(a, b)],
                [(q * a_sq - p * cross) * weight for p, q in zip(a, b)],
            )
        )

    for k in range(2):
        found = []
        for which in range(2):
            here, before = grads[k + 1][which], grads[k][which]
            total = before[1] - here[0] - here[1] - here[2]
            total = total + pltpu.roll(here[0], 1, 0) + pltpu.roll(here[2], 1, 1)
            found.append(coupling_weight * total)
        moved[0] = found[0]
        scaled = found[1] / mags[k + 1, 0:16, :]
        moved[1] = scaled * planes[5 + k, 0:16, :]
        moved[2] = scaled * planes[9 + k, 0:16, :]
        pet_out[k] = moved[0, 1 : ZS + 1, :]
        mr_out[k, :, :HALF] = moved[1, 1 : ZS + 1, :]
        mr_out[k, :, HALF:] = moved[2, 1 : ZS + 1, :]


def coil_kernel(recv_ref, data_own_ref, data_got_ref, mask_ref, ytab_ref, ztab_ref, core_ref,
                out_ref, sens, images, kyrows):
    def image_part(c):
        part = recv_ref[c * 16 : (c + 1) * 16, :, ROW:].astype(f32)
        left = part[:, :ZS].reshape(NZ, HALF // 2)
        right = part[:, ZS:].reshape(NZ, HALF // 2)
        return jnp.concatenate([left, right], -1)

    mr_re, mr_im = image_part(0), image_part(1)
    for c in range(2):
        block = recv_ref[c * 16 : (c + 1) * 16, :, :ROW].astype(f32)
        for k in range(2):
            q = 2 * c + k
            rows = pl.ds(q * NZ, NZ)
            one = block[:, k * ZS : (k + 1) * ZS].reshape(NZ, ROW)
            s_re, s_im = one[:, :HALF], one[:, HALF:]
            sens[rows, :] = one
            images[rows, :HALF] = (s_re * mr_re - s_im * mr_im).astype(bf16)
            images[rows, HALF:] = (s_re * mr_im + s_im * mr_re).astype(bf16)
    kyrows[...] = jnp.dot(images[...], ytab_ref[...], preferred_element_type=f32).astype(bf16)
    mask = mask_ref[...].astype(f32)
    on_first = core_ref[0] == 0
    ztab = ztab_ref[...]
    for q in range(4):
        rows = pl.ds(q * NZ, NZ)
        volume = jnp.concatenate([kyrows[rows, :HALF], kyrows[rows, HALF:]], 0)
        kspace = jnp.dot(ztab, volume, preferred_element_type=f32)
        k = q % 2
        own_first = on_first if q < 2 else jnp.logical_not(on_first)
        data = jnp.where(own_first, data_own_ref[k].astype(f32), data_got_ref[k].astype(f32))
        misfit = jnp.concatenate(
            [mask * (kspace[:NZ] - data[:NZ]), mask * (data[NZ:] - kspace[NZ:])], 0
        ).astype(bf16)
        back = jnp.dot(ztab, misfit, preferred_element_type=f32).astype(bf16)
        images[rows, :HALF] = back[:NZ]
        images[rows, HALF:] = back[NZ:]
    total_re = jnp.zeros((NZ, HALF), f32)
    total_im = jnp.zeros((NZ, HALF), f32)
    for q in range(4):
        rows = pl.ds(q * NZ, NZ)
        image = jnp.dot(images[rows, :], ytab_ref[...], preferred_element_type=f32)
        i_re, i_im = image[:, :HALF], image[:, HALF:]
        s_re, s_im = sens[rows, :HALF], sens[rows, HALF:]
        total_re = total_re + (s_re * i_re - s_im * i_im)
        total_im = total_im - (s_re * i_im + s_im * i_re)
    out_ref[:, :, :HALF] = total_re.reshape(16, ZS, HALF).astype(bf16)
    out_ref[:, :, HALF:] = total_im.reshape(16, ZS, HALF).astype(bf16)


def sum_kernel(recv_ref, mr_out, pet_out):
    pet = jnp.zeros((ZS, ROW), f32)
    for c in range(2):
        mr = jnp.zeros((ZS, ROW), f32)
        for g in range(8):
            block = recv_ref[2 * g + c].astype(f32)
            mr = mr + block[:ZS]
            pet = pet + block[ZS:]
        mr_out[c * ZS : (c + 1) * ZS, :] = mr
    pet_out[...] = pet


def final_kernel(mr_ref, pet_ref, couple_pet_ref, couple_mr_ref, pet_out, mr_out):
    for k in range(2):
        rows = pl.ds(k * ZS, ZS)
        pet = pet_ref[:, k * HALF : (k + 1) * HALF] + couple_pet_ref[k]
        mr = mr_ref[rows, :] + couple_mr_ref[k]
        pet_out[:, k, :] = pet[:, :NY]
        mr_out[:, k, :NY] = mr[:, :NY]
        mr_out[:, k, NY:] = mr[:, HALF : HALF + NY]


def sds(shape, dtype):
    return jax.ShapeDtypeStruct(shape, dtype)


def on_device(
    pet_image, mr_image, coil_sens, kspace_data, kspace_mask, system_tiles,
    tile_subset_block, tile_col, measured, background, subset_view_blocks,
):
    core = lax.axis_index("c")
    grp = lax.axis_index(GRP)
    gz = lax.axis_index(GZ)
    core_arr = core.astype(jnp.int32).reshape(1)
    pet_rows = pet_image.reshape(ZS * NX, NY)
    mr_rows = mr_image.reshape(ZS * NX, 2 * NY)

    sent = call(
        pack_kernel, sds((32, 16, CHUNK), bf16), [SMEM, VMEM, VMEM],
        [pltpu.VMEM((8, 2 * ZS * NX, 128), f32), pltpu.VMEM((4, ZS * NX, 128), f32)],
        10**6, 4 * 10**6, "pack",
    )(core_arr, coil_sens.reshape(2 * ZS * NX, 2 * NY), mr_rows)
    recv = lax.all_to_all(sent, ("c",) + GZ, split_axis=0, concat_axis=0, tiled=True)

    data = kspace_data.reshape(2, NZ, 2, 2, NY).transpose(2, 0, 3, 1, 4)
    data = jnp.pad(data, ((0, 0),) * 4 + ((0, HALF - NY),)).reshape(2, 2, 2 * NZ, HALF)
    data_own = lax.dynamic_index_in_dim(data, core, 0, keepdims=False)
    data_out = lax.dynamic_index_in_dim(data, 1 - core, 0, keepdims=False)
    data_got = lax.ppermute(data_out, "c", [(0, 1), (1, 0)])
    mask = jnp.pad(kspace_mask, ((0, 0), (0, HALF - NY)))

    xs = jnp.clip(2 * grp - 1 + jnp.arange(4, dtype=jnp.int32), 0, NX - 1)
    bins, win, low, high = call(
        project_kernel,
        (sds((16, 128), f32), sds((12, ZS, HALF), f32), sds((16, HALF), f32), sds((16, HALF), f32)),
        [SMEM, SMEM, SMEM, VMEM, VMEM, VMEM],
        [pltpu.VMEM((16, NY), f32)],
        10**7, 4 * 10**6, "project",
    )(tile_col, tile_subset_block, xs, pet_rows, mr_rows, system_tiles)
    from_prev = lax.ppermute(high, GZ, [(i, i + 1) for i in range(15)])
    from_next = lax.ppermute(low, GZ, [(i + 1, i) for i in range(15)])
    for k in (1, 2, 4, 8):
        bins = bins + lax.ppermute(bins, GZ, [(i, i ^ k) for i in range(16)])
    pet_part = call(
        backproject_kernel, sds((16, ZS, ROW), bf16), [SMEM, SMEM, SMEM, VMEM, VMEM, VMEM, VMEM],
        [pltpu.VMEM((16, 128), f32), pltpu.VMEM((16, 128), f32), pltpu.VMEM((4, ZS * NX, 128), f32)],
        10**7, 3 * 10**6, "backproject",
    )(tile_col, tile_subset_block, subset_view_blocks, bins, measured, background, system_tiles)
    info = jnp.stack([gz * ZS, 2 * grp]).astype(jnp.int32)
    couple_pet, couple_mr = call(
        coupling_kernel, (sds((2, ZS, HALF), f32), sds((2, ZS, ROW), f32)),
        [SMEM, VMEM, VMEM, VMEM],
        [pltpu.VMEM((12, 24, HALF), f32), pltpu.VMEM((4, 24, HALF), f32),
         pltpu.VMEM((3, 16, HALF), f32)],
        10**6, 10**6, "coupling",
    )(info, win, from_prev, from_next)

    mr_part = call(
        coil_kernel, sds((16, ZS, ROW), bf16), [VMEM] * 6 + [SMEM],
        [pltpu.VMEM((4 * NZ, ROW), f32), pltpu.VMEM((4 * NZ, ROW), bf16),
         pltpu.VMEM((4 * NZ, ROW), bf16)],
        5 * 10**9, 6 * 10**6, "coils",
    )(recv, data_own, data_got, mask, y_table(), z_table(), core_arr)

    both = lax.all_to_all(
        jnp.concatenate([mr_part, pet_part], 1), GRP, split_axis=0, concat_axis=0, tiled=True
    )
    mr_sum, pet_sum = call(
        sum_kernel, (sds((2 * ZS, ROW), f32), sds((ZS, ROW), f32)), [VMEM], [],
        10**6, 10**6, "sums",
    )(both)
    mr_here = lax.ppermute(
        mr_sum, GRP + GZ, [(g * 16 + j, j * 16 + g) for g in range(16) for j in range(16)]
    )
    return call(
        final_kernel, (sds((ZS, 2, NY), f32), sds((ZS, 2, 2 * NY), f32)), [VMEM] * 4, [],
        10**5, 10**6, "final",
    )(mr_here, pet_sum, couple_pet, couple_mr)


def solution(mesh):
    fine = Mesh(mesh.devices.reshape(2, 4, 2, 4, 4), ("zh", "x", "c", "zl", "y"))
    placed = (
        P(GZ, None, None),
        P(GZ, None, None),
        P(GRP, GZ, None, None),
        P(GRP, None, GZ, None),
        P(),
        P(GRP + GZ, None, None),
        P(GRP + GZ),
        P(GRP + GZ),
        P(GRP, None),
        P(GRP, None),
        P(GRP),
    )
    return jax.shard_map(
        on_device,
        mesh=fine,
        in_specs=placed,
        out_specs=(P(GZ, GRP, None), P(GZ, GRP, None)),
        check_vma=False,
    )
```

time: 376 us -> 96.6 us (0.26)
  waiting for transfers between devices: 182 us -> 32.7 us
  other arithmetic: 47.8 us -> 0.95 us
  blocking collectives: 45 us -> 0 us
  matrix products: 21.1 us -> 0 us
  local copies, waits for them, and re-layouts: 30.7 us -> 11.7 us
  between operations: 14.6 us -> 0.84 us
  Pallas kernels: 0 us -> 13.3 us
  starting transfers between devices: 29.8 us -> 35.6 us
    psum x1 -> x0, waiting for transfers between devices: 170 us -> none  [on_device(): summed = lax.psum(group_fits, 'grp')]
    psum x1 -> x0, blocking collectives: 45 us -> none  [on_device(): whole_bins = lax.psum(partial_bins, 'gz') / width]
    dot_general x14 -> x0, matrix products: 21.1 us -> none  [the longest x2 5.95 us: on_device(): jnp.dot(returned.reshape(-1, 2 * width), ky_table.T, preferred_element_ty...]
    ppermute x2 -> x8, waiting for transfers between devices: 0.01 us -> 20.5 us  [the longest x4 13.7 us: on_device(): bins = bins + lax.ppermute(bins, GZ, [(i, i ^ k) for i in range(16)])]
    pallas_call x0 -> x7, Pallas kernels: none -> 13.3 us  [the longest x1 5.21 us: on_device(): call(coil_kernel, sds((16, ZS, ROW), bf16), [VMEM] * 6 + [SMEM], [pltpu.V...]
    ppermute x2 -> x8, starting transfers between devices: 5.44 us -> 17.7 us  [the longest x4 10.1 us: on_device(): bins = bins + lax.ppermute(bins, GZ, [(i, i ^ k) for i in range(16)])]
    convert_element_type x8 -> x0, other arithmetic: 12.1 us -> none  [the longest x2 4.77 us: dft_parts(): (-jnp.sin(angles) * scaling).astype(jnp.bfloat16)]
    concatenate x6 -> x1, other arithmetic: 8.95 us -> 0.85 us  [on_device(): jnp.concatenate([mr_part, pet_part], 1)]
  transfers between devices with their start and end apart: 7 -> 10, of which waited for: 3 -> 7; matrix products, arithmetic and copies ran while one was open for 21% -> 6% of each run, Pallas kernels for 0% -> 4%
where the time goes in v1:
time: 96.6 us; the launch traced here: 95.1 us
  starting transfers between devices  35.6 us (37%)
  waiting for transfers between devices  32.7 us (34%)
  Pallas kernels  13.3 us (14%)
  local copies, waits for them, and re-layouts  11.7 us (12%)
    ppermute x4, waiting for transfers between devices, on_device(): bins = bins + lax.ppermute(bins, GZ, [(i, i ^ k) for i in range(16)])  13.7 us
    all_to_all x1, waiting for transfers between devices, on_device(): lax.all_to_all(jnp.concatenate([mr_part, pet_part], 1), GRP, split_axis=0...  11.3 us
    unnamed x29, local copies, waits for them, and re-layouts  10.5 us
    ppermute x4, starting transfers between devices, on_device(): bins = bins + lax.ppermute(bins, GZ, [(i, i ^ k) for i in range(16)])  10.1 us
    all_to_all x1, starting transfers between devices, on_device(): lax.all_to_all(sent, ('c',) + GZ, split_axis=0, concat_axis=0, tiled=True)  9.16 us
    all_to_all x1, starting transfers between devices, on_device(): lax.all_to_all(jnp.concatenate([mr_part, pet_part], 1), GRP, split_axis=0...  8.73 us
    ppermute x1, waiting for transfers between devices, on_device(): lax.ppermute(mr_sum, GRP + GZ, [(g * 16 + j, j * 16 + g) for g in range(1...  6.82 us
    pallas_call x1, Pallas kernels, on_device(): call(coil_kernel, sds((16, ZS, ROW), bf16), [VMEM] * 6 + [SMEM], [pltpu.V...  5.21 us
  transfers between devices with their start and end apart: 10, of which 7 were waited for; matrix products, arithmetic and copies ran while one was open for 6% of the time, Pallas kernels for 4%

profile of v1, /device:TPU:6, one launch (start us, length us, event | category | flops | bytes accessed | tf_op | source)
XLA Modules:
  0.0 95.1 jit_solution(17600843617151385468)
XLA Ops:
  0.6 0.0 copy-start
  0.6 1.2 %copy-done = f32[8,32,960]{2,1,0:T(8,128)S(1)} copy-done((f32[8,32,960]{2,1,0:T(8,128)S(1)}, f32[8,32,960]{2,1,0:T(8,128)}, u32[]{:S(2)}) %copy-start) | copy-done | bytes 983064
  1.9 1.2 %copy-done.2 = bf16[2,8,32,960]{3,2,1,0:T(8,128)(2,1)S(1)} copy-done((bf16[2,8,32,960]{3,2,1,0:T(8,128)(2,1)S(1)}, bf16[2,8,32,960]{3,2,1,0:T(8,128)(2,1)}, u32[]{:S(2)}) %copy-start.2) | copy-done | bytes 983064
  3.1 3.8 %pack.1 = bf16[32,16,1280]{2,1,0:T(8,128)(2,1)} custom-call(s32[1]{0:T(128)} %bitcast.core_ref, bf16[512,960]{1,0:T(8,128)(2,1)S(1)} %bitcast.16, f32[256,960]{1,0:T(8,128)S(1)} %bitcast.14), custom_call_target="tpu_custom_call" | custom-call | flops 1000000 | bytes 4000000 | tf_op jit(solution)/shard_map/pack/pallas_call | solution.py:295
  6.9 9.2 %all-to-all-start = ((bf16[32,16,1280]{2,1,0:T(8,128)(2,1)}), bf16[32,16,1280]{2,1,0:T(8,128)(2,1)}, u32[]{:S(2)}, u32[]{:S(2)}) async-start(bf16[32,16,1280]{2,1,0:T(8,128)(2,1)} %pack.1), calls=%async_computation | async-start | bytes 2621440 | tf_op jit(solution)/shard_map/all_to_all | solution.py:300
  16.1 0.0 copy-done.12
  16.1 0.5 copy.19
  16.6 0.1 pad.8.clone
  16.8 1.1 %dynamic-slice_bitcast_fusion = (bf16[2,256,512]{2,1,0:T(8,128)(2,1)}, bf16[2,256,512]{2,1,0:T(8,128)(2,1)}) fusion(bf16[2,2,256,512]{3,2,1,0:T(8,128)(2,1)S(1)} %bitcast.18, s32[]{:T(128)S(6)} %select_n.8, s32[]{:T(128)S(6)} %select_n.7), kind=kLoop, calls=%fused_computation.1 | loop fusion | bytes 2097160 | tf_op jit(solution)/shard_map/jit(dynamic_index_in_dim)/squeeze | solution.py:305
  17.8 0.2 collective-permute-start
  18.0 2.9 %copy.17.tiles_ref = bf16[16,128,480]{2,1,0:T(8,128)(2,1)S(1)} copy(bf16[16,128,480]{1,2,0:T(8,128)(2,1)} %param.18) | data formatting | bytes 3932160 | tf_op args[5]
  21.0 0.0 copy-done.1
  21.0 0.0 copy-done.7
  21.0 0.0 copy-done.8
  21.0 0.0 copy-start.3
  21.0 1.0 %copy-done.3 = f32[8,32,480]{2,1,0:T(8,128)S(1)} copy-done((f32[8,32,480]{2,1,0:T(8,128)S(1)}, f32[8,32,480]{2,1,0:T(8,128)}, u32[]{:S(2)}) %copy-start.3) | copy-done | bytes 491544
  22.1 1.2 %project.1 = (f32[16,128]{1,0:T(8,128)S(1)}, f32[12,8,512]{2,1,0:T(8,128)S(1)}, f32[16,512]{1,0:T(8,128)S(1)}, f32[16,512]{1,0:T(8,128)S(1)}) custom-call(s32[16]{0:T(128)S(1)} %copy-done.7, s32[16]{0:T(128)S(1)} %copy-done.8, s32[4]{0:T(128)S(1)} %add_clamp_fusion.xs_ref, f32[256,480]{1,0:T(8,128)S(1)} %bitcast.17, f32[256,960]{1,0:T(8,128)S(1)} %bitcast.15, ...), custom_call_target="tpu_custom_call" | custom-call | flops 10000000 | bytes 4000000 | tf_op jit(solution)/shard_map/project/pallas_call | solution.py:310
  23.3 0.0 copy-start.4
  23.3 1.8 %collective-permute-start.1 = (f32[16,128]{1,0:T(8,128)S(1)}, f32[16,128]{1,0:T(8,128)S(1)}, u32[]{:S(2)}, u32[]{:S(2)}) collective-permute-start(f32[16,128]{1,0:T(8,128)S(1)} %get-tuple-element.10), channel_id=1, source_target_pairs={{0,1},{1,0},{2,3},{3,2},{4,5},{5,4},{6,7},{7,6},{8,9},{9,8},{10,11... | collective-permute-start | bytes 24584 | tf_op jit(solution)/shard_map/ppermute | solution.py:320
  25.1 2.7 %collective-permute-done.1 = f32[16,128]{1,0:T(8,128)S(1)} collective-permute-done((f32[16,128]{1,0:T(8,128)S(1)}, f32[16,128]{1,0:T(8,128)S(1)}, u32[]{:S(2)}, u32[]{:S(2)}) %collective-permute-start.1) | collective-permute-done | bytes 8224 | tf_op jit(solution)/shard_map/ppermute | solution.py:320
  27.8 2.4 %collective-permute-start.2 = (f32[16,128]{1,0:T(8,128)S(1)}, f32[16,128]{1,0:T(8,128)S(1)}, u32[]{:S(2)}, u32[]{:S(2)}) collective-permute-start(f32[16,128]{1,0:T(8,128)S(1)} %add.46), channel_id=1, source_target_pairs={{0,2},{1,3},{2,0},{3,1},{4,6},{5,7},{6,4},{7,5},{8,10},{9,11},{10,... | collective-permute-start | bytes 24584 | tf_op jit(solution)/shard_map/ppermute | solution.py:320
  30.2 2.7 %collective-permute-done.2 = f32[16,128]{1,0:T(8,128)S(1)} collective-permute-done((f32[16,128]{1,0:T(8,128)S(1)}, f32[16,128]{1,0:T(8,128)S(1)}, u32[]{:S(2)}, u32[]{:S(2)}) %collective-permute-start.2) | collective-permute-done | bytes 8224 | tf_op jit(solution)/shard_map/ppermute | solution.py:320
  33.0 1.4 %collective-permute-start.3 = (f32[16,128]{1,0:T(8,128)S(1)}, f32[16,128]{1,0:T(8,128)S(1)}, u32[]{:S(2)}, u32[]{:S(2)}) collective-permute-start(f32[16,128]{1,0:T(8,128)S(1)} %add.47), channel_id=1, source_target_pairs={{0,4},{1,5},{2,6},{3,7},{4,0},{5,1},{6,2},{7,3},{8,12},{9,13},{10,... | collective-permute-start | bytes 24584 | tf_op jit(solution)/shard_map/ppermute | solution.py:320
  34.4 3.7 %collective-permute-done.3 = f32[16,128]{1,0:T(8,128)S(1)} collective-permute-done((f32[16,128]{1,0:T(8,128)S(1)}, f32[16,128]{1,0:T(8,128)S(1)}, u32[]{:S(2)}, u32[]{:S(2)}) %collective-permute-start.3) | collective-permute-done | bytes 8224 | tf_op jit(solution)/shard_map/ppermute | solution.py:320
  38.1 4.5 %collective-permute-start.4 = (f32[16,128]{1,0:T(8,128)S(1)}, f32[16,128]{1,0:T(8,128)S(1)}, u32[]{:S(2)}, u32[]{:S(2)}) collective-permute-start(f32[16,128]{1,0:T(8,128)S(1)} %add.48), channel_id=1, source_target_pairs={{0,8},{1,9},{2,10},{3,11},{4,12},{5,13},{6,14},{7,15},{8,0},{9,1},... | collective-permute-start | bytes 24584 | tf_op jit(solution)/shard_map/ppermute | solution.py:320
  42.6 1.1 %copy.16 = s32[128,480]{1,0:T(8,128)S(1)} copy(s32[128,480]{0,1:T(8,128)} %param.17) | data formatting | bytes 491520 | tf_op args[4]
  43.7 4.5 %collective-permute-done.4 = f32[16,128]{1,0:T(8,128)S(1)} collective-permute-done((f32[16,128]{1,0:T(8,128)S(1)}, f32[16,128]{1,0:T(8,128)S(1)}, u32[]{:S(2)}, u32[]{:S(2)}) %collective-permute-start.4) | collective-permute-done | bytes 8224 | tf_op jit(solution)/shard_map/ppermute | solution.py:320
  48.2 0.0 copy-done.5
  48.2 0.0 copy-done.6
  48.2 1.3 %backproject.1 = bf16[16,8,1024]{2,1,0:T(8,128)(2,1)S(1)} custom-call(s32[16]{0:T(128)S(1)} %copy-done.7, s32[16]{0:T(128)S(1)} %copy-done.8, s32[16]{0:T(128)S(1)} %copy-done.9, f32[16,128]{1,0:T(8,128)S(1)} %add.49.bins_ref, f32[64,128]{1,0:T(8,128)S(1)} %copy-done.5, f32[64,128]{1,0:T(8,128)S(1)} %copy-done.6, bf16[16,128,480]{2,1,0:T(8,128)(2,1)S(1)} %copy.17.tiles_ref), custom_call_target="tpu_custom_call" | custom-call | flops 10000000 | bytes 3000000 | tf_op jit(solution)/shard_map/backproject/pallas_call | solution.py:321
  49.5 0.0 collective-permute-done.data_got_ref
  49.5 0.8 all-to-all-done.recv_ref
  50.4 1.6 %copy-done.10 = bf16[1024,1024]{1,0:T(8,128)(2,1)S(1)} copy-done((bf16[1024,1024]{1,0:T(8,128)(2,1)S(1)}, bf16[1024,1024]{1,0:T(8,128)(2,1)}, u32[]{:S(2)}) %copy-start.10) | copy-done | bytes 2097176
  52.0 0.9 copy-done.11
  52.9 5.2 %coils.1 = bf16[16,8,1024]{2,1,0:T(8,128)(2,1)S(1)} custom-call(bf16[32,16,1280]{2,1,0:T(8,128)(2,1)} %all-to-all-done.recv_ref, bf16[2,256,512]{2,1,0:T(8,128)(2,1)S(1)} %copy-done.4, bf16[2,256,512]{2,1,0:T(8,128)(2,1)} %collective-permute-done.data_got_ref, s32[128,512]{1,0:T(8,128)S(1)} %pad.9.mask_ref, bf16[1024,1024]{1,0:T(8,128)(2,1)S(1)} %copy-done.10, ...), custom_call_target="tpu_custom_call" | custom-call | flops 5000000000 | bytes 6000000 | tf_op jit(solution)/shard_map/coils/pallas_call | solution.py:335
  58.1 0.9 pad_maximum_fusion
  58.9 8.7 %all-to-all-start.1 = ((bf16[16,16,1024]{2,1,0:T(8,128)(2,1)}), bf16[16,16,1024]{2,1,0:T(8,128)(2,1)S(1)}, u32[]{:S(2)}, u32[]{:S(2)}) async-start(bf16[16,16,1024]{2,1,0:T(8,128)(2,1)} %pad_maximum_fusion), calls=%async_computation.1 | async-start | bytes 1048576 | tf_op jit(solution)/shard_map/all_to_all | solution.py:342
  67.7 2.6 %collective-permute-start.6 = (f32[16,512]{1,0:T(8,128)S(1)}, f32[16,512]{1,0:T(8,128)S(1)}, u32[]{:S(2)}, u32[]{:S(2)}) collective-permute-start(f32[16,512]{1,0:T(8,128)S(1)} %get-tuple-element.14), channel_id=1, source_target_pairs={{0,1},{1,2},{2,3},{3,4},{4,5},{5,6},{6,7},{7,8},{8,9},{9,10},{10,1... | collective-permute-start | bytes 98312 | tf_op jit(solution)/shard_map/ppermute | solution.py:317
  70.3 1.3 %collective-permute-start.7 = (f32[16,512]{1,0:T(8,128)S(1)}, f32[16,512]{1,0:T(8,128)S(1)}, u32[]{:S(2)}, u32[]{:S(2)}) collective-permute-start(f32[16,512]{1,0:T(8,128)S(1)} %get-tuple-element.15), channel_id=1, source_target_pairs={{1,0},{2,1},{3,2},{4,3},{5,4},{6,5},{7,6},{8,7},{9,8},{10,9},{11,1... | collective-permute-start | bytes 98312 | tf_op jit(solution)/shard_map/ppermute | solution.py:318
  71.6 11.3 %all-to-all-done.1.recv_ref = bf16[16,16,1024]{2,1,0:T(8,128)(2,1)S(1)} async-done(((bf16[16,16,1024]{2,1,0:T(8,128)(2,1)}), bf16[16,16,1024]{2,1,0:T(8,128)(2,1)S(1)}, u32[]{:S(2)}, u32[]{:S(2)}) %all-to-all-start.1) | async-done | bytes 524320 | tf_op jit(solution)/shard_map/all_to_all | solution.py:342
  83.0 0.1 sums.1
  83.0 3.5 %collective-permute-start.5 = (f32[16,1024]{1,0:T(8,128)S(1)}, f32[16,1024]{1,0:T(8,128)S(1)}, u32[]{:S(2)}, u32[]{:S(2)}) collective-permute-start(f32[16,1024]{1,0:T(8,128)S(1)} %get-tuple-element.11), channel_id=1, source_target_pairs={{0,0},{1,16},{2,32},{3,48},{4,64},{5,80},{6,96},{7,112},{8,128},{9... | collective-permute-start | bytes 196616 | tf_op jit(solution)/shard_map/ppermute | solution.py:349
  86.5 0.1 pad_add_fusion.info_ref
  86.6 0.0 collective-permute-done.6.prev_ref
  86.6 0.0 collective-permute-done.7.next_ref
  86.6 1.0 %coupling.1 = (f32[2,8,512]{2,1,0:T(8,128)S(1)}, f32[2,8,1024]{2,1,0:T(8,128)S(1)}) custom-call(s32[2]{0:T(128)S(1)} %pad_add_fusion.info_ref, f32[12,8,512]{2,1,0:T(8,128)S(1)} %get-tuple-element.13.win_ref, f32[16,512]{1,0:T(8,128)S(1)} %collective-permute-done.6.prev_ref, f32[16,512]{1,0:T(8,128)S(1)} %collective-permute-done.7.next_ref), custom_call_target="tpu_custom_call" | custom-call | flops 1000000 | bytes 1000000 | tf_op jit(solution)/shard_map/coupling/pallas_call | solution.py:327
  87.6 6.8 %collective-permute-done.5.mr_ref = f32[16,1024]{1,0:T(8,128)S(1)} collective-permute-done((f32[16,1024]{1,0:T(8,128)S(1)}, f32[16,1024]{1,0:T(8,128)S(1)}, u32[]{:S(2)}, u32[]{:S(2)}) %collective-permute-start.5) | collective-permute-done | bytes 65568 | tf_op jit(solution)/shard_map/ppermute | solution.py:349
  94.4 0.7 final.1
  (18 shorter events, 0.1 us)
Async XLA Ops:
  0.6 1.2 %copy-start = (f32[8,32,960]{2,1,0:T(8,128)S(1)}, f32[8,32,960]{2,1,0:T(8,128)}, u32[]{:S(2)}) copy-start(f32[8,32,960]{2,1,0:T(8,128)} %param.14) | copy-start | bytes 2949124
  1.9 1.2 %copy-start.2 = (bf16[2,8,32,960]{3,2,1,0:T(8,128)(2,1)S(1)}, bf16[2,8,32,960]{3,2,1,0:T(8,128)(2,1)}, u32[]{:S(2)}) copy-start(bf16[2,8,32,960]{3,2,1,0:T(8,128)(2,1)} %param.15) | copy-start | bytes 2949124
  6.9 9.2 %copy-start.12 = (bf16[2,128,2,960]{1,3,2,0:T(8,128)(2,1)S(1)}, bf16[2,128,2,960]{1,3,2,0:T(8,128)(2,1)}, u32[]{:S(2)}) copy-start(bf16[2,128,2,960]{1,3,2,0:T(8,128)(2,1)} %param.16) | copy-start | bytes 2949124
  6.9 43.5 %all-to-all-start = ((bf16[32,16,1280]{2,1,0:T(8,128)(2,1)}), bf16[32,16,1280]{2,1,0:T(8,128)(2,1)}, u32[]{:S(2)}, u32[]{:S(2)}) async-start(bf16[32,16,1280]{2,1,0:T(8,128)(2,1)} %pack.1), calls=%async_computation | async-start | bytes 2621440 | tf_op jit(solution)/shard_map/all_to_all | solution.py:300
  17.8 31.7 %collective-permute-start = (bf16[2,256,512]{2,1,0:T(8,128)(2,1)}, bf16[2,256,512]{2,1,0:T(8,128)(2,1)}, u32[]{:S(2)}, u32[]{:S(2)}) collective-permute-start(bf16[2,256,512]{2,1,0:T(8,128)(2,1)} %get-tuple-element.18), channel_id=1, source_target_pairs={{0,16},{16,0},{1,17},{17,1},{2,18},{18,2},{3,19},{19,3},{4,20},{20... | collective-permute-start | bytes 1572872 | tf_op jit(solution)/shard_map/ppermute | solution.py:306
  18.0 2.9 %copy-start.1 = (f32[8,32,960]{2,1,0:T(8,128)S(1)}, f32[8,32,960]{2,1,0:T(8,128)}, u32[]{:S(2)}) copy-start(f32[8,32,960]{2,1,0:T(8,128)} %param.14) | copy-start | bytes 2949124
  18.0 3.0 %copy-start.7 = (s32[16]{0:T(128)S(1)}, s32[16]{0:T(128)}, u32[]{:S(2)}) copy-start(s32[16]{0:T(128)} %col_ref.3) | copy-start | bytes 196
  18.0 3.0 %copy-start.8 = (s32[16]{0:T(128)S(1)}, s32[16]{0:T(128)}, u32[]{:S(2)}) copy-start(s32[16]{0:T(128)} %block_ref.3) | copy-start | bytes 196
  21.0 1.0 %copy-start.3 = (f32[8,32,480]{2,1,0:T(8,128)S(1)}, f32[8,32,480]{2,1,0:T(8,128)}, u32[]{:S(2)}) copy-start(f32[8,32,480]{2,1,0:T(8,128)} %param.13) | copy-start | bytes 1474564
  22.1 26.1 %copy-start.5 = (f32[64,128]{1,0:T(8,128)S(1)}, f32[64,128]{1,0:T(8,128)}, u32[]{:S(2)}) copy-start(f32[64,128]{1,0:T(8,128)} %measured_ref.1) | copy-start | bytes 98308
  22.1 26.1 %copy-start.6 = (f32[64,128]{1,0:T(8,128)S(1)}, f32[64,128]{1,0:T(8,128)}, u32[]{:S(2)}) copy-start(f32[64,128]{1,0:T(8,128)} %background_ref.1) | copy-start | bytes 98308
  22.1 26.1 %copy-start.9 = (s32[16]{0:T(128)S(1)}, s32[16]{0:T(128)}, u32[]{:S(2)}) copy-start(s32[16]{0:T(128)} %view_ref.1) | copy-start | bytes 196
  23.3 27.1 %copy-start.4 = (bf16[2,256,512]{2,1,0:T(8,128)(2,1)S(1)}, bf16[2,256,512]{2,1,0:T(8,128)(2,1)}, u32[]{:S(2)}) copy-start(bf16[2,256,512]{2,1,0:T(8,128)(2,1)} %get-tuple-element.19.data_own_ref) | copy-start | bytes 1572868
  23.3 4.5 %collective-permute-start.1 = (f32[16,128]{1,0:T(8,128)S(1)}, f32[16,128]{1,0:T(8,128)S(1)}, u32[]{:S(2)}, u32[]{:S(2)}) collective-permute-start(f32[16,128]{1,0:T(8,128)S(1)} %get-tuple-element.10), channel_id=1, source_target_pairs={{0,1},{1,0},{2,3},{3,2},{4,5},{5,4},{6,7},{7,6},{8,9},{9,8},{10,11... | collective-permute-start | bytes 24584 | tf_op jit(solution)/shard_map/ppermute | solution.py:320
  27.8 5.2 %collective-permute-start.2 = (f32[16,128]{1,0:T(8,128)S(1)}, f32[16,128]{1,0:T(8,128)S(1)}, u32[]{:S(2)}, u32[]{:S(2)}) collective-permute-start(f32[16,128]{1,0:T(8,128)S(1)} %add.46), channel_id=1, source_target_pairs={{0,2},{1,3},{2,0},{3,1},{4,6},{5,7},{6,4},{7,5},{8,10},{9,11},{10,... | collective-permute-start | bytes 24584 | tf_op jit(solution)/shard_map/ppermute | solution.py:320
  33.0 5.1 %collective-permute-start.3 = (f32[16,128]{1,0:T(8,128)S(1)}, f32[16,128]{1,0:T(8,128)S(1)}, u32[]{:S(2)}, u32[]{:S(2)}) collective-permute-start(f32[16,128]{1,0:T(8,128)S(1)} %add.47), channel_id=1, source_target_pairs={{0,4},{1,5},{2,6},{3,7},{4,0},{5,1},{6,2},{7,3},{8,12},{9,13},{10,... | collective-permute-start | bytes 24584 | tf_op jit(solution)/shard_map/ppermute | solution.py:320
  38.1 10.1 %collective-permute-start.4 = (f32[16,128]{1,0:T(8,128)S(1)}, f32[16,128]{1,0:T(8,128)S(1)}, u32[]{:S(2)}, u32[]{:S(2)}) collective-permute-start(f32[16,128]{1,0:T(8,128)S(1)} %add.48), channel_id=1, source_target_pairs={{0,8},{1,9},{2,10},{3,11},{4,12},{5,13},{6,14},{7,15},{8,0},{9,1},... | collective-permute-start | bytes 24584 | tf_op jit(solution)/shard_map/ppermute | solution.py:320
  50.4 1.6 %copy-start.10 = (bf16[1024,1024]{1,0:T(8,128)(2,1)S(1)}, bf16[1024,1024]{1,0:T(8,128)(2,1)}, u32[]{:S(2)}) copy-start(bf16[1024,1024]{1,0:T(8,128)(2,1)} %constant.49.clone.ytab_ref) | copy-start | bytes 6291460
  52.0 0.9 copy-start.11
  58.9 24.0 %all-to-all-start.1 = ((bf16[16,16,1024]{2,1,0:T(8,128)(2,1)}), bf16[16,16,1024]{2,1,0:T(8,128)(2,1)S(1)}, u32[]{:S(2)}, u32[]{:S(2)}) async-start(bf16[16,16,1024]{2,1,0:T(8,128)(2,1)} %pad_maximum_fusion), calls=%async_computation.1 | async-start | bytes 1048576 | tf_op jit(solution)/shard_map/all_to_all | solution.py:342
  67.7 18.9 %collective-permute-start.6 = (f32[16,512]{1,0:T(8,128)S(1)}, f32[16,512]{1,0:T(8,128)S(1)}, u32[]{:S(2)}, u32[]{:S(2)}) collective-permute-start(f32[16,512]{1,0:T(8,128)S(1)} %get-tuple-element.14), channel_id=1, source_target_pairs={{0,1},{1,2},{2,3},{3,4},{4,5},{5,6},{6,7},{7,8},{8,9},{9,10},{10,1... | collective-permute-start | bytes 98312 | tf_op jit(solution)/shard_map/ppermute | solution.py:317
  70.3 16.3 %collective-permute-start.7 = (f32[16,512]{1,0:T(8,128)S(1)}, f32[16,512]{1,0:T(8,128)S(1)}, u32[]{:S(2)}, u32[]{:S(2)}) collective-permute-start(f32[16,512]{1,0:T(8,128)S(1)} %get-tuple-element.15), channel_id=1, source_target_pairs={{1,0},{2,1},{3,2},{4,3},{5,4},{6,5},{7,6},{8,7},{9,8},{10,9},{11,1... | collective-permute-start | bytes 98312 | tf_op jit(solution)/shard_map/ppermute | solution.py:318
  83.0 11.4 %collective-permute-start.5 = (f32[16,1024]{1,0:T(8,128)S(1)}, f32[16,1024]{1,0:T(8,128)S(1)}, u32[]{:S(2)}, u32[]{:S(2)}) collective-permute-start(f32[16,1024]{1,0:T(8,128)S(1)} %get-tuple-element.11), channel_id=1, source_target_pairs={{0,0},{1,16},{2,32},{3,48},{4,64},{5,80},{6,96},{7,112},{8,128},{9... | collective-permute-start | bytes 196616 | tf_op jit(solution)/shard_map/ppermute | solution.py:349

commit v2 on v1

--- a/solution.py
+++ b/solution.py
@@ -22,6 +22,7 @@
 
 SMEM = pl.BlockSpec(memory_space=pltpu.SMEM)
 VMEM = pl.BlockSpec(memory_space=pltpu.VMEM)
+HBM = pl.BlockSpec(memory_space=pltpu.HBM)
 
 
 def dft_parts(length):
@@ -47,26 +48,39 @@
     return jnp.asarray(table.astype(jnp.bfloat16))
 
 
-def call(kernel, out_shape, in_specs, scratch, flops, moved, name):
+def call(kernel, out_shape, in_specs, scratch, flops, moved, name, out_spec=VMEM, grant=40):
     return pl.pallas_call(
         kernel,
         out_shape=out_shape,
         in_specs=in_specs,
-        out_specs=jax.tree.map(lambda _: VMEM, out_shape),
+        out_specs=jax.tree.map(lambda _: out_spec, out_shape),
         scratch_shapes=scratch,
-        compiler_params=pltpu.CompilerParams(vmem_limit_bytes=40 * 1024 * 1024),
+        compiler_params=pltpu.CompilerParams(vmem_limit_bytes=grant * 1024 * 1024),
         cost_estimate=pl.CostEstimate(flops=flops, bytes_accessed=moved, transcendentals=0),
         name=name,
     )
 
 
-def pack_kernel(core_ref, sens_ref, mr_ref, out_ref, sens_rows, mr_rows):
+def pack_kernel(core_ref, sens_hbm, mr_hbm, out_hbm, sens_ref, mr_ref, sens_rows, mr_rows, out_ref,
+                sens_sems, mr_sems, out_sems):
+    sens_copies = [
+        pltpu.make_async_copy(sens_hbm.at[pl.ds(128 * n, 128)], sens_ref.at[pl.ds(128 * n, 128)], sens_sems.at[n])
+        for n in range(4)
+    ]
+    mr_copies = [
+        pltpu.make_async_copy(mr_hbm.at[pl.ds(128 * n, 128)], mr_ref.at[pl.ds(128 * n, 128)], mr_sems.at[n])
+        for n in range(2)
+    ]
+    for copy in sens_copies + mr_copies:
+        copy.start()
     imag = core_ref[0] == 1
     last = NY - 3 * 128
     for part in range(2):
         sens_rows[4 * part + 3, :, last:] = jnp.zeros((2 * ZS * NX, 128 - last), f32)
     mr_rows[3, :, last:] = jnp.zeros((ZS * NX, 128 - last), f32)
     for q in range(2 * ZS):
+        if q % 4 == 0:
+            sens_copies[q // 4].wait()
         rows = pl.ds(q * NX, NX)
         for part in range(2):
             values = sens_ref[rows, part * NY : (part + 1) * NY].astype(f32)
@@ -74,13 +88,16 @@
                 block = values[:, 128 * b : min(128 * (b + 1), NY)]
                 sens_rows[4 * part + b, rows, : block.shape[1]] = block
     for q in range(ZS):
+        if q % 4 == 0:
+            mr_copies[q // 4].wait()
         rows = pl.ds(q * NX, NX)
         values = jnp.where(imag, mr_ref[rows, NY:], mr_ref[rows, :NY])
         for b in range(4):
             block = values[:, 128 * b : min(128 * (b + 1), NY)]
             mr_rows[b, rows, : block.shape[1]] = block
-    for x in range(NX):
-        place = (x % 2) * (NX // 2) + x // 2
+    out_copies = []
+    for place in range(NX):
+        x = 2 * (place % 16) + place // 16
         for b in range(8):
             block = sens_rows[b, pl.ds(x, 2 * ZS, stride=NX), :]
             out_ref[place, :, 128 * b : 128 * (b + 1)] = block.astype(bf16)
@@ -89,6 +106,13 @@
                 [mr_rows[b, pl.ds(x, ZS, stride=NX), :], mr_rows[b + 2, pl.ds(x, ZS, stride=NX), :]], 0
             )
             out_ref[place, :, ROW + 128 * b : ROW + 128 * (b + 1)] = block.astype(bf16)
+        if place % 4 == 3:
+            part = pl.ds(place - 3, 4)
+            copy = pltpu.make_async_copy(out_ref.at[part], out_hbm.at[part], out_sems.at[place // 4])
+            copy.start()
+            out_copies.append(copy)
+    for copy in out_copies:
+        copy.wait()
 
 
 def project_kernel(
@@ -100,9 +124,7 @@
     rows = picked[...].astype(bf16)
     bins_ref[...] = jnp.zeros((16, 128), f32)
     for t in range(16):
-        product = lax.dot_general(
-            rows, tiles_ref[t], (((1,), (1,)), ((), ())), preferred_element_type=f32
-        )
+        product = jnp.dot(rows, tiles_ref[t], preferred_element_type=f32)
         place = pl.ds(block_ref[t], 1)
         bins_ref[place, :] = bins_ref[place, :] + product[t : t + 1, :]
     win_ref[...] = jnp.zeros((12, ZS, HALF), f32)
@@ -133,7 +155,9 @@
     rows = gathered[...].astype(bf16)
     acc[...] = jnp.zeros((4, ZS * NX, 128), f32)
     for t in range(16):
-        spread = jnp.dot(rows, tiles_ref[t], preferred_element_type=f32)
+        spread = lax.dot_general(
+            rows, tiles_ref[t], (((1,), (1,)), ((), ())), preferred_element_type=f32
+        )
         place = pl.ds(col_ref[t], 1)
         for b in range(4):
             block = spread[t : t + 1, 128 * b : min(128 * (b + 1), NY)]
@@ -144,7 +168,8 @@
             for b in range(4):
                 block = acc[b, pl.ds(2 * p + k, ZS, stride=NX), :] / NY
                 first = k * HALF + 128 * b
-                out_ref[p, :, first : first + 128] = block.astype(bf16)
+                rows = slice(p // 8 * ZS, (p // 8 + 1) * ZS)
+                out_ref[p % 8, rows, first : first + 128] = block.astype(bf16)
 
 
 def coupling_kernel(
@@ -206,72 +231,106 @@
         mr_out[k, :, HALF:] = moved[2, 1 : ZS + 1, :]
 
 
-def coil_kernel(recv_ref, data_own_ref, data_got_ref, mask_ref, ytab_ref, ztab_ref, core_ref,
-                out_ref, sens, images, kyrows):
+def coil_kernel(core_ref, recv_hbm, ytab_hbm, data_own_ref, data_got_ref, mask_ref, ztab_ref, pet_ref,
+                out_ref, recv_ref, ytab_ref, sens, images, kyrows, recv_sems, ytab_sems):
+    def received(n, c, lanes):
+        place = (pl.ds(16 * c, 16), slice(None), lanes)
+        return pltpu.make_async_copy(recv_hbm.at[place], recv_ref.at[place], recv_sems.at[n])
+
+    copies = [
+        received(0, 0, pl.ds(ROW, HALF // 2)),
+        received(1, 1, pl.ds(ROW, HALF // 2)),
+        received(2, 0, pl.ds(0, ROW)),
+        received(3, 1, pl.ds(0, ROW)),
+    ]
+    tables = [
+        pltpu.make_async_copy(
+            ytab_hbm.at[pl.ds(256 * n, 256)], ytab_ref.at[pl.ds(256 * n, 256)], ytab_sems.at[n]
+        )
+        for n in range(4)
+    ]
+    for copy in copies + tables:
+        copy.start()
+    out_ref[:, 2 * ZS :] = pet_ref[...]
+
     def image_part(c):
         part = recv_ref[c * 16 : (c + 1) * 16, :, ROW:].astype(f32)
         left = part[:, :ZS].reshape(NZ, HALF // 2)
         right = part[:, ZS:].reshape(NZ, HALF // 2)
         return jnp.concatenate([left, right], -1)
 
+    copies[0].wait()
+    copies[1].wait()
     mr_re, mr_im = image_part(0), image_part(1)
+    mask = mask_ref[...].astype(f32)
+    on_first = core_ref[0] == 0
+    ztab = ztab_ref[...]
     for c in range(2):
+        copies[2 + c].wait()
         block = recv_ref[c * 16 : (c + 1) * 16, :, :ROW].astype(f32)
         for k in range(2):
-            q = 2 * c + k
-            rows = pl.ds(q * NZ, NZ)
+            rows = pl.ds((2 * c + k) * NZ, NZ)
             one = block[:, k * ZS : (k + 1) * ZS].reshape(NZ, ROW)
             s_re, s_im = one[:, :HALF], one[:, HALF:]
             sens[rows, :] = one
             images[rows, :HALF] = (s_re * mr_re - s_im * mr_im).astype(bf16)
             images[rows, HALF:] = (s_re * mr_im + s_im * mr_re).astype(bf16)
-    kyrows[...] = jnp.dot(images[...], ytab_ref[...], preferred_element_type=f32).astype(bf16)
-    mask = mask_ref[...].astype(f32)
-    on_first = core_ref[0] == 0
-    ztab = ztab_ref[...]
-    for q in range(4):
-        rows = pl.ds(q * NZ, NZ)
-        volume = jnp.concatenate([kyrows[rows, :HALF], kyrows[rows, HALF:]], 0)
-        kspace = jnp.dot(ztab, volume, preferred_element_type=f32)
-        k = q % 2
-        own_first = on_first if q < 2 else jnp.logical_not(on_first)
-        data = jnp.where(own_first, data_own_ref[k].astype(f32), data_got_ref[k].astype(f32))
-        misfit = jnp.concatenate(
-            [mask * (kspace[:NZ] - data[:NZ]), mask * (data[NZ:] - kspace[NZ:])], 0
-        ).astype(bf16)
-        back = jnp.dot(ztab, misfit, preferred_element_type=f32).astype(bf16)
-        images[rows, :HALF] = back[:NZ]
-        images[rows, HALF:] = back[NZ:]
+    for copy in tables:
+        copy.wait()
+    for c in range(2):
+        pair = pl.ds(2 * c * NZ, 2 * NZ)
+        kyrows[pair, :] = jnp.dot(images[pair, :], ytab_ref[...], preferred_element_type=f32).astype(bf16)
+        own = on_first if c == 0 else jnp.logical_not(on_first)
+        for k in range(2):
+            rows = pl.ds((2 * c + k) * NZ, NZ)
+            volume = jnp.concatenate([kyrows[rows, :HALF], kyrows[rows, HALF:]], 0)
+            kspace = jnp.dot(ztab, volume, preferred_element_type=f32)
+            data = jnp.where(own, data_own_ref[k].astype(f32), data_got_ref[k].astype(f32))
+            misfit = jnp.concatenate(
+                [mask * (kspace[:NZ] - data[:NZ]), mask * (data[NZ:] - kspace[NZ:])], 0
+            ).astype(bf16)
+            back = jnp.dot(ztab, misfit, preferred_element_type=f32).astype(bf16)
+            images[rows, :HALF] = back[:NZ]
+            images[rows, HALF:] = back[NZ:]
     total_re = jnp.zeros((NZ, HALF), f32)
     total_im = jnp.zeros((NZ, HALF), f32)
-    for q in range(4):
-        rows = pl.ds(q * NZ, NZ)
-        image = jnp.dot(images[rows, :], ytab_ref[...], preferred_element_type=f32)
-        i_re, i_im = image[:, :HALF], image[:, HALF:]
-        s_re, s_im = sens[rows, :HALF], sens[rows, HALF:]
-        total_re = total_re + (s_re * i_re - s_im * i_im)
-        total_im = total_im - (s_re * i_im + s_im * i_re)
-    out_ref[:, :, :HALF] = total_re.reshape(16, ZS, HALF).astype(bf16)
-    out_ref[:, :, HALF:] = total_im.reshape(16, ZS, HALF).astype(bf16)
-
-
-def sum_kernel(recv_ref, mr_out, pet_out):
-    pet = jnp.zeros((ZS, ROW), f32)
     for c in range(2):
-        mr = jnp.zeros((ZS, ROW), f32)
-        for g in range(8):
-            block = recv_ref[2 * g + c].astype(f32)
-            mr = mr + block[:ZS]
-            pet = pet + block[ZS:]
-        mr_out[c * ZS : (c + 1) * ZS, :] = mr
-    pet_out[...] = pet
-
-
-def final_kernel(mr_ref, pet_ref, couple_pet_ref, couple_mr_ref, pet_out, mr_out):
+        pair = pl.ds(2 * c * NZ, 2 * NZ)
+        image = jnp.dot(images[pair, :], ytab_ref[...], preferred_element_type=f32)
+        for k in range(2):
+            rows = pl.ds((2 * c + k) * NZ, NZ)
+            i_re, i_im = image[k * NZ : (k + 1) * NZ, :HALF], image[k * NZ : (k + 1) * NZ, HALF:]
+            s_re, s_im = sens[rows, :HALF], sens[rows, HALF:]
+            total_re = total_re + (s_re * i_re - s_im * i_im)
+            total_im = total_im - (s_re * i_im + s_im * i_re)
+    for part, total in enumerate((total_re, total_im)):
+        slabs = total.reshape(2, 8, ZS, HALF)
+        both = jnp.concatenate([slabs[0], slabs[1]], 1)
+        out_ref[:, : 2 * ZS, part * HALF : (part + 1) * HALF] = both.astype(bf16)
+
+
+def sum_kernel(half_ref, recv_ref, mr_own, mr_other, pet_own, pet_other):
+    upper = half_ref[0] == 1
+    pet = jnp.zeros((2 * ZS, ROW), f32)
+    for c in range(2):
+        mr = jnp.zeros((2 * ZS, ROW), f32)
+        for x in range(4):
+            block = recv_ref[2 * x + c].astype(f32)
+            mr = mr + block[: 2 * ZS]
+            pet = pet + block[2 * ZS :]
+        rows = pl.ds(c * ZS, ZS)
+        mr_own[rows, :] = jnp.where(upper, mr[ZS:], mr[:ZS])
+        mr_other[rows, :] = jnp.where(upper, mr[:ZS], mr[ZS:])
+    pet_own[...] = jnp.where(upper, pet[ZS:], pet[:ZS])
+    pet_other[...] = jnp.where(upper, pet[:ZS], pet[ZS:])
+
+
+def final_kernel(mr_a, mr_b, pet_a, pet_b, couple_pet_ref, couple_mr_ref, pet_out, mr_out):
     for k in range(2):
         rows = pl.ds(k * ZS, ZS)
-        pet = pet_ref[:, k * HALF : (k + 1) * HALF] + couple_pet_ref[k]
-        mr = mr_ref[rows, :] + couple_mr_ref[k]
+        lanes = pl.ds(k * HALF, HALF)
+        pet = pet_a[:, lanes] + pet_b[:, lanes] + couple_pet_ref[k]
+        mr = mr_a[rows, :] + mr_b[rows, :] + couple_mr_ref[k]
         pet_out[:, k, :] = pet[:, :NY]
         mr_out[:, k, :NY] = mr[:, :NY]
         mr_out[:, k, NY:] = mr[:, HALF : HALF + NY]
@@ -291,12 +350,17 @@
     core_arr = core.astype(jnp.int32).reshape(1)
     pet_rows = pet_image.reshape(ZS * NX, NY)
     mr_rows = mr_image.reshape(ZS * NX, 2 * NY)
+    tiles = system_tiles.swapaxes(1, 2)
 
     sent = call(
-        pack_kernel, sds((32, 16, CHUNK), bf16), [SMEM, VMEM, VMEM],
-        [pltpu.VMEM((8, 2 * ZS * NX, 128), f32), pltpu.VMEM((4, ZS * NX, 128), f32)],
-        10**6, 4 * 10**6, "pack",
+        pack_kernel, sds((32, 16, CHUNK), bf16), [SMEM, HBM, HBM],
+        [pltpu.VMEM((2 * ZS * NX, 2 * NY), bf16), pltpu.VMEM((ZS * NX, 2 * NY), f32),
+         pltpu.VMEM((8, 2 * ZS * NX, 128), f32), pltpu.VMEM((4, ZS * NX, 128), f32),
+         pltpu.VMEM((32, 16, CHUNK), bf16), pltpu.SemaphoreType.DMA((4,)),
+         pltpu.SemaphoreType.DMA((2,)), pltpu.SemaphoreType.DMA((8,))],
+        10**6, 4 * 10**6, "pack", HBM, 60,
     )(core_arr, coil_sens.reshape(2 * ZS * NX, 2 * NY), mr_rows)
+    sent, tile_col = lax.optimization_barrier((sent, tile_col))
     recv = lax.all_to_all(sent, ("c",) + GZ, split_axis=0, concat_axis=0, tiled=True)
 
     data = kspace_data.reshape(2, NZ, 2, 2, NY).transpose(2, 0, 3, 1, 4)
@@ -313,16 +377,16 @@
         [SMEM, SMEM, SMEM, VMEM, VMEM, VMEM],
         [pltpu.VMEM((16, NY), f32)],
         10**7, 4 * 10**6, "project",
-    )(tile_col, tile_subset_block, xs, pet_rows, mr_rows, system_tiles)
+    )(tile_col, tile_subset_block, xs, pet_rows, mr_rows, tiles)
     from_prev = lax.ppermute(high, GZ, [(i, i + 1) for i in range(15)])
     from_next = lax.ppermute(low, GZ, [(i + 1, i) for i in range(15)])
     for k in (1, 2, 4, 8):
         bins = bins + lax.ppermute(bins, GZ, [(i, i ^ k) for i in range(16)])
     pet_part = call(
-        backproject_kernel, sds((16, ZS, ROW), bf16), [SMEM, SMEM, SMEM, VMEM, VMEM, VMEM, VMEM],
+        backproject_kernel, sds((8, 2 * ZS, ROW), bf16), [SMEM, SMEM, SMEM, VMEM, VMEM, VMEM, VMEM],
         [pltpu.VMEM((16, 128), f32), pltpu.VMEM((16, 128), f32), pltpu.VMEM((4, ZS * NX, 128), f32)],
         10**7, 3 * 10**6, "backproject",
-    )(tile_col, tile_subset_block, subset_view_blocks, bins, measured, background, system_tiles)
+    )(tile_col, tile_subset_block, subset_view_blocks, bins, measured, background, tiles)
     info = jnp.stack([gz * ZS, 2 * grp]).astype(jnp.int32)
     couple_pet, couple_mr = call(
         coupling_kernel, (sds((2, ZS, HALF), f32), sds((2, ZS, ROW), f32)),
@@ -332,27 +396,36 @@
         10**6, 10**6, "coupling",
     )(info, win, from_prev, from_next)
 
-    mr_part = call(
-        coil_kernel, sds((16, ZS, ROW), bf16), [VMEM] * 6 + [SMEM],
-        [pltpu.VMEM((4 * NZ, ROW), f32), pltpu.VMEM((4 * NZ, ROW), bf16),
-         pltpu.VMEM((4 * NZ, ROW), bf16)],
+    recv, pet_part, couple_pet, couple_mr = lax.optimization_barrier(
+        (recv, pet_part, couple_pet, couple_mr)
+    )
+    parts = call(
+        coil_kernel, sds((8, 4 * ZS, ROW), bf16), [SMEM, HBM, HBM] + [VMEM] * 5,
+        [pltpu.VMEM((32, 16, CHUNK), bf16), pltpu.VMEM((ROW, ROW), bf16),
+         pltpu.VMEM((4 * NZ, ROW), f32), pltpu.VMEM((4 * NZ, ROW), bf16),
+         pltpu.VMEM((4 * NZ, ROW), bf16), pltpu.SemaphoreType.DMA((4,)), pltpu.SemaphoreType.DMA((4,))],
         5 * 10**9, 6 * 10**6, "coils",
-    )(recv, data_own, data_got, mask, y_table(), z_table(), core_arr)
-
-    both = lax.all_to_all(
-        jnp.concatenate([mr_part, pet_part], 1), GRP, split_axis=0, concat_axis=0, tiled=True
-    )
-    mr_sum, pet_sum = call(
-        sum_kernel, (sds((2 * ZS, ROW), f32), sds((ZS, ROW), f32)), [VMEM], [],
-        10**6, 10**6, "sums",
-    )(both)
-    mr_here = lax.ppermute(
-        mr_sum, GRP + GZ, [(g * 16 + j, j * 16 + g) for g in range(16) for j in range(16)]
-    )
+    )(core_arr, recv, y_table(), data_own, data_got, mask, z_table(), pet_part)
+
+    both = lax.all_to_all(parts, ("x", "c"), split_axis=0, concat_axis=0, tiled=True)
+    half = lax.axis_index("zh").astype(jnp.int32).reshape(1)
+    mr_own, mr_other, pet_own, pet_other = call(
+        sum_kernel,
+        (sds((2 * ZS, ROW), f32), sds((2 * ZS, ROW), f32), sds((ZS, ROW), f32), sds((ZS, ROW), f32)),
+        [SMEM, VMEM], [], 10**6, 10**6, "sums",
+    )(half, both)
+    places = [(zh, p, j) for zh in range(2) for p in range(8) for j in range(16)]
+    mr_a = lax.ppermute(
+        mr_own, GRP + GZ, [((zh * 8 + p) * 16 + j, j * 16 + zh * 8 + p) for zh, p, j in places]
+    )
+    mr_b = lax.ppermute(
+        mr_other, GRP + GZ, [((zh * 8 + p) * 16 + j, j * 16 + (1 - zh) * 8 + p) for zh, p, j in places]
+    )
+    pet_got = lax.ppermute(pet_other, "zh", [(0, 1), (1, 0)])
     return call(
-        final_kernel, (sds((ZS, 2, NY), f32), sds((ZS, 2, 2 * NY), f32)), [VMEM] * 4, [],
+        final_kernel, (sds((ZS, 2, NY), f32), sds((ZS, 2, 2 * NY), f32)), [VMEM] * 6, [],
         10**5, 10**6, "final",
-    )(mr_here, pet_sum, couple_pet, couple_mr)
+    )(mr_a, mr_b, pet_own, pet_got, couple_pet, couple_mr)
 
 
 def solution(mesh):

time: 96.6 us -> 97 us (level)
  the two profiles are of different devices: /device:TPU:6 before, /device:TPU:7 now
where the time goes in v2:
time: 97 us; the launch traced here: 96.4 us
  starting transfers between devices  34.2 us (35%)
  waiting for transfers between devices  21.9 us (23%)
  Pallas kernels  16.6 us (17%)
  blocking collectives  13 us (13%)
  local copies, waits for them, and re-layouts  9.73 us (10%)
    all_to_all x1, blocking collectives, on_device(): lax.all_to_all(parts, ('x', 'c'), split_axis=0, concat_axis=0, tiled=True)  13 us
    ppermute x4, waiting for transfers between devices, on_device(): bins = bins + lax.ppermute(bins, GZ, [(i, i ^ k) for i in range(16)])  12 us
    ppermute x4, starting transfers between devices, on_device(): bins = bins + lax.ppermute(bins, GZ, [(i, i ^ k) for i in range(16)])  9.59 us
    all_to_all x1, starting transfers between devices, on_device(): lax.all_to_all(sent, ('c',) + GZ, split_axis=0, concat_axis=0, tiled=True)  9.56 us
    unnamed x30, local copies, waits for them, and re-layouts  7.14 us
    pallas_call x1, Pallas kernels, on_device(): call(coil_kernel, sds((8, 4 * ZS, ROW), bf16), [SMEM, HBM, HBM] + [VMEM]...  6.75 us
    ppermute x1, starting transfers between devices, on_device(): lax.ppermute(mr_own, GRP + GZ, [((zh * 8 + p) * 16 + j, j * 16 + zh * 8 +...  6.63 us
    ppermute x1, waiting for transfers between devices, on_device(): pet_got = lax.ppermute(pet_other, 'zh', [(0, 1), (1, 0)])  5.52 us
  transfers between devices with their start and end apart: 11, of which 6 were waited for; matrix products, arithmetic and copies ran while one was open for 5% of the time, Pallas kernels for 5%

profile of v2, /device:TPU:7, one launch (start us, length us, event | category | flops | bytes accessed | tf_op | source)
XLA Modules:
  0.0 96.4 jit_solution(16734120501429139950)
XLA Ops:
  0.6 4.7 %pack.1 = bf16[32,16,1280]{2,1,0:T(8,128)(2,1)} custom-call(s32[1]{0:T(128)} %bitcast.1.core_ref, bf16[512,960]{1,0:T(8,128)(2,1)} %bitcast.22, f32[256,960]{1,0:T(8,128)} %bitcast.18), custom_call_target="tpu_custom_call" | custom-call | flops 1000000 | bytes 4000000 | tf_op jit(solution)/shard_map/pack/pallas_call | solution.py:355
  5.3 0.0 copy-start.13
  5.4 9.6 %all-to-all-start = ((bf16[32,16,1280]{2,1,0:T(8,128)(2,1)}), bf16[32,16,1280]{2,1,0:T(8,128)(2,1)}, u32[]{:S(2)}, u32[]{:S(2)}) async-start(bf16[32,16,1280]{2,1,0:T(8,128)(2,1)} %pack.1), calls=%async_computation | async-start | bytes 2621440 | tf_op jit(solution)/shard_map/all_to_all | solution.py:364
  14.9 1.3 %copy.17 = bf16[2,2,2,128,480]{4,3,2,1,0:T(8,128)(2,1)} copy(bf16[2,2,2,128,480]{3,4,2,0,1:T(8,128)(2,1)S(1)} %bitcast.23) | data formatting | bytes 1966080
  16.3 0.0 copy-start.9
  16.3 1.5 %pad.8.clone = bf16[2,2,2,128,512]{4,3,2,1,0:T(8,128)(2,1)S(1)} pad(bf16[2,2,2,128,480]{4,3,2,1,0:T(8,128)(2,1)} %copy.17, bf16[]{:T(256)} %constant.46.clone.1), padding=0_0x0_0x0_0x0_0x0_32 | pad | bytes 2031618 | tf_op jit(solution)/shard_map/jit(_pad)/pad | solution.py:367
  17.8 1.0 %dynamic-slice_bitcast_fusion = (bf16[2,256,512]{2,1,0:T(8,128)(2,1)}, bf16[2,256,512]{2,1,0:T(8,128)(2,1)}) fusion(bf16[2,2,256,512]{3,2,1,0:T(8,128)(2,1)S(1)} %bitcast.21, s32[]{:T(128)S(6)} %select_n.8, s32[]{:T(128)S(6)} %select_n.7), kind=kLoop, calls=%fused_computation | loop fusion | bytes 2097160 | tf_op jit(solution)/shard_map/jit(dynamic_index_in_dim)/squeeze | solution.py:369
  18.9 0.3 collective-permute-start.6
  19.2 0.0 copy-done.1
  19.2 0.0 copy-start.10
  19.2 1.6 %project.1 = (f32[16,128]{1,0:T(8,128)S(1)}, f32[12,8,512]{2,1,0:T(8,128)S(1)}, f32[16,512]{1,0:T(8,128)}, f32[16,512]{1,0:T(8,128)}) custom-call(s32[16]{0:T(128)S(1)} %copy-done.8, s32[16]{0:T(128)S(1)} %copy-done.9, s32[4]{0:T(128)S(1)} %add_clamp_fusion.xs_ref, f32[256,480]{1,0:T(8,128)S(1)} %bitcast.20, f32[256,960]{1,0:T(8,128)S(1)} %bitcast.19, ...), custom_call_target="tpu_custom_call" | custom-call | flops 10000000 | bytes 4000000 | tf_op jit(solution)/shard_map/project/pallas_call | solution.py:374
  20.9 0.7 copy-done.4
  21.6 1.4 %collective-permute-start = (f32[16,128]{1,0:T(8,128)S(1)}, f32[16,128]{1,0:T(8,128)S(1)}, u32[]{:S(2)}, u32[]{:S(2)}) collective-permute-start(f32[16,128]{1,0:T(8,128)S(1)} %get-tuple-element.20), channel_id=1, source_target_pairs={{0,1},{1,0},{2,3},{3,2},{4,5},{5,4},{6,7},{7,6},{8,9},{9,8},{10,11... | collective-permute-start | bytes 24584 | tf_op jit(solution)/shard_map/ppermute | solution.py:384
  23.0 3.2 %collective-permute-done = f32[16,128]{1,0:T(8,128)S(1)} collective-permute-done((f32[16,128]{1,0:T(8,128)S(1)}, f32[16,128]{1,0:T(8,128)S(1)}, u32[]{:S(2)}, u32[]{:S(2)}) %collective-permute-start) | collective-permute-done | bytes 8224 | tf_op jit(solution)/shard_map/ppermute | solution.py:384
  26.2 1.2 %collective-permute-start.1 = (f32[16,128]{1,0:T(8,128)S(1)}, f32[16,128]{1,0:T(8,128)S(1)}, u32[]{:S(2)}, u32[]{:S(2)}) collective-permute-start(f32[16,128]{1,0:T(8,128)S(1)} %add.44), channel_id=1, source_target_pairs={{0,2},{1,3},{2,0},{3,1},{4,6},{5,7},{6,4},{7,5},{8,10},{9,11},{10,... | collective-permute-start | bytes 24584 | tf_op jit(solution)/shard_map/ppermute | solution.py:384
  27.4 3.5 %collective-permute-done.1 = f32[16,128]{1,0:T(8,128)S(1)} collective-permute-done((f32[16,128]{1,0:T(8,128)S(1)}, f32[16,128]{1,0:T(8,128)S(1)}, u32[]{:S(2)}, u32[]{:S(2)}) %collective-permute-start.1) | collective-permute-done | bytes 8224 | tf_op jit(solution)/shard_map/ppermute | solution.py:384
  30.9 1.6 %collective-permute-start.2 = (f32[16,128]{1,0:T(8,128)S(1)}, f32[16,128]{1,0:T(8,128)S(1)}, u32[]{:S(2)}, u32[]{:S(2)}) collective-permute-start(f32[16,128]{1,0:T(8,128)S(1)} %add.45), channel_id=1, source_target_pairs={{0,4},{1,5},{2,6},{3,7},{4,0},{5,1},{6,2},{7,3},{8,12},{9,13},{10,... | collective-permute-start | bytes 24584 | tf_op jit(solution)/shard_map/ppermute | solution.py:384
  32.5 1.3 %collective-permute-start.4 = (f32[16,512]{1,0:T(8,128)}, f32[16,512]{1,0:T(8,128)S(1)}, u32[]{:S(2)}, u32[]{:S(2)}) collective-permute-start(f32[16,512]{1,0:T(8,128)} %get-tuple-element.22), channel_id=1, source_target_pairs={{0,1},{1,2},{2,3},{3,4},{4,5},{5,6},{6,7},{7,8},{8,9},{9,10},{10,1... | collective-permute-start | bytes 98312 | tf_op jit(solution)/shard_map/ppermute | solution.py:381
  33.8 1.3 %collective-permute-start.5 = (f32[16,512]{1,0:T(8,128)}, f32[16,512]{1,0:T(8,128)S(1)}, u32[]{:S(2)}, u32[]{:S(2)}) collective-permute-start(f32[16,512]{1,0:T(8,128)} %get-tuple-element.23), channel_id=1, source_target_pairs={{1,0},{2,1},{3,2},{4,3},{5,4},{6,5},{7,6},{8,7},{9,8},{10,9},{11,1... | collective-permute-start | bytes 98312 | tf_op jit(solution)/shard_map/ppermute | solution.py:382
  35.1 1.5 %collective-permute-done.2 = f32[16,128]{1,0:T(8,128)S(1)} collective-permute-done((f32[16,128]{1,0:T(8,128)S(1)}, f32[16,128]{1,0:T(8,128)S(1)}, u32[]{:S(2)}, u32[]{:S(2)}) %collective-permute-start.2) | collective-permute-done | bytes 8224 | tf_op jit(solution)/shard_map/ppermute | solution.py:384
  36.6 5.3 %collective-permute-start.3 = (f32[16,128]{1,0:T(8,128)S(1)}, f32[16,128]{1,0:T(8,128)S(1)}, u32[]{:S(2)}, u32[]{:S(2)}) collective-permute-start(f32[16,128]{1,0:T(8,128)S(1)} %add.46), channel_id=1, source_target_pairs={{0,8},{1,9},{2,10},{3,11},{4,12},{5,13},{6,14},{7,15},{8,0},{9,1},... | collective-permute-start | bytes 24584 | tf_op jit(solution)/shard_map/ppermute | solution.py:384
  41.9 0.1 pad_add_fusion.info_ref
  42.0 1.1 %copy.16 = s32[128,480]{1,0:T(8,128)S(1)} copy(s32[128,480]{0,1:T(8,128)} %param.17) | data formatting | bytes 491520 | tf_op args[4]
  43.1 3.8 %collective-permute-done.3 = f32[16,128]{1,0:T(8,128)S(1)} collective-permute-done((f32[16,128]{1,0:T(8,128)S(1)}, f32[16,128]{1,0:T(8,128)S(1)}, u32[]{:S(2)}, u32[]{:S(2)}) %collective-permute-start.3) | collective-permute-done | bytes 8224 | tf_op jit(solution)/shard_map/ppermute | solution.py:384
  46.9 0.0 collective-permute-done.4.prev_ref
  46.9 0.0 collective-permute-done.5.next_ref
  46.9 0.9 copy-done.5
  47.8 1.0 coupling.1
  48.8 0.0 copy-start.6
  48.8 0.7 copy-done.6
  49.6 0.8 copy-done.7
  50.3 1.8 %backproject.1.pet_ref = bf16[8,16,1024]{2,1,0:T(8,128)(2,1)S(1)} custom-call(s32[16]{0:T(128)S(1)} %copy-done.8, s32[16]{0:T(128)S(1)} %copy-done.9, s32[16]{0:T(128)S(1)} %copy-done.10, f32[16,128]{1,0:T(8,128)S(1)} %add.47.bins_ref, f32[64,128]{1,0:T(8,128)S(1)} %copy-done.6, f32[64,128]{1,0:T(8,128)S(1)} %copy-done.7, bf16[16,480,128]{2,1,0:T(8,128)(2,1)S(1)} %bitcast.17), custom_call_target="tpu_custom_call" | custom-call | flops 10000000 | bytes 3000000 | tf_op jit(solution)/shard_map/backproject/pallas_call | solution.py:385
  52.1 0.0 all-to-all-done.recv_hbm
  52.1 0.0 collective-permute-done.6.data_got_ref
  52.1 0.0 copy-done.3
  52.1 0.0 copy-done.12
  52.2 0.0 copy-start.11
  52.2 1.6 %copy-done.11 = bf16[1024,1024]{1,0:T(8,128)(2,1)S(1)} copy-done((bf16[1024,1024]{1,0:T(8,128)(2,1)S(1)}, bf16[1024,1024]{1,0:T(8,128)(2,1)}, u32[]{:S(2)}) %copy-start.11) | copy-done | bytes 2097176
  53.8 6.8 %coils.1 = bf16[8,32,1024]{2,1,0:T(8,128)(2,1)S(1)} custom-call(s32[1]{0:T(128)} %bitcast.1.core_ref, bf16[32,16,1280]{2,1,0:T(8,128)(2,1)} %all-to-all-done.recv_hbm, bf16[1024,1024]{1,0:T(8,128)(2,1)S(1)} %copy-done.11, bf16[2,256,512]{2,1,0:T(8,128)(2,1)S(1)} %copy-done.3, bf16[2,256,512]{2,1,0:T(8,128)(2,1)} %collective-permute-done.6.data_got_ref, ...), custom_call_target="tpu_custom_call" | custom-call | flops 5000000000 | bytes 6000000 | tf_op jit(solution)/shard_map/coils/pallas_call | solution.py:402
  60.5 13.0 %all_to_all.10.recv_ref = bf16[8,32,1024]{2,1,0:T(8,128)(2,1)S(1)} all-to-all(bf16[8,32,1024]{2,1,0:T(8,128)(2,1)S(1)} %coils.1), channel_id=1, replica_groups=mesh['zh'=2,'x'=4,'c'=2,'zl'=4,'y'=4] {'x','c'}, dimensions={0} | all-to-all | bytes 1048576 | tf_op jit(solution)/shard_map/all_to_all | solution.py:410
  73.5 0.1 sums.1
  73.6 6.6 %collective-permute-start.7 = (f32[16,1024]{1,0:T(8,128)S(1)}, f32[16,1024]{1,0:T(8,128)S(1)}, u32[]{:S(2)}, u32[]{:S(2)}) collective-permute-start(f32[16,1024]{1,0:T(8,128)S(1)} %get-tuple-element.28), channel_id=1, source_target_pairs={{0,0},{1,16},{2,32},{3,48},{4,64},{5,80},{6,96},{7,112},{8,128},{9... | collective-permute-start | bytes 196616 | tf_op jit(solution)/shard_map/ppermute | solution.py:418
  80.2 4.4 %collective-permute-start.8 = (f32[16,1024]{1,0:T(8,128)S(1)}, f32[16,1024]{1,0:T(8,128)S(1)}, u32[]{:S(2)}, u32[]{:S(2)}) collective-permute-start(f32[16,1024]{1,0:T(8,128)S(1)} %get-tuple-element.29), channel_id=1, source_target_pairs={{0,8},{1,24},{2,40},{3,56},{4,72},{5,88},{6,104},{7,120},{8,136},{... | collective-permute-start | bytes 196616 | tf_op jit(solution)/shard_map/ppermute | solution.py:421
  84.6 1.2 %collective-permute-start.9 = (f32[8,1024]{1,0:T(8,128)S(1)}, f32[8,1024]{1,0:T(8,128)S(1)}, u32[]{:S(2)}, u32[]{:S(2)}) collective-permute-start(f32[8,1024]{1,0:T(8,128)S(1)} %get-tuple-element.31), channel_id=1, source_target_pairs={{0,128},{128,0},{1,129},{129,1},{2,130},{130,2},{3,131},{131,3},{4... | collective-permute-start | bytes 98312 | tf_op jit(solution)/shard_map/ppermute | solution.py:424
  85.8 5.5 %collective-permute-done.9.pet_b = f32[8,1024]{1,0:T(8,128)S(1)} collective-permute-done((f32[8,1024]{1,0:T(8,128)S(1)}, f32[8,1024]{1,0:T(8,128)S(1)}, u32[]{:S(2)}, u32[]{:S(2)}) %collective-permute-start.9) | collective-permute-done | bytes 32800 | tf_op jit(solution)/shard_map/ppermute | solution.py:424
  91.3 0.0 collective-permute-done.7.mr_a
  91.3 4.4 %collective-permute-done.8.mr_b = f32[16,1024]{1,0:T(8,128)S(1)} collective-permute-done((f32[16,1024]{1,0:T(8,128)S(1)}, f32[16,1024]{1,0:T(8,128)S(1)}, u32[]{:S(2)}, u32[]{:S(2)}) %collective-permute-start.8) | collective-permute-done | bytes 65568 | tf_op jit(solution)/shard_map/ppermute | solution.py:421
  95.7 0.7 final.1
  (21 shorter events, 0.1 us)
Async XLA Ops:
  5.3 9.6 %copy-start.13 = (bf16[2,128,2,960]{1,3,2,0:T(8,128)(2,1)S(1)}, bf16[2,128,2,960]{1,3,2,0:T(8,128)(2,1)}, u32[]{:S(2)}) copy-start(bf16[2,128,2,960]{1,3,2,0:T(8,128)(2,1)} %param.16) | copy-start | bytes 2949124
  5.4 46.8 %all-to-all-start = ((bf16[32,16,1280]{2,1,0:T(8,128)(2,1)}), bf16[32,16,1280]{2,1,0:T(8,128)(2,1)}, u32[]{:S(2)}, u32[]{:S(2)}) async-start(bf16[32,16,1280]{2,1,0:T(8,128)(2,1)} %pack.1), calls=%async_computation | async-start | bytes 2621440 | tf_op jit(solution)/shard_map/all_to_all | solution.py:364
  16.3 2.9 %copy-start = (bf16[16,128,480]{1,2,0:T(8,128)(2,1)S(1)}, bf16[16,128,480]{1,2,0:T(8,128)(2,1)}, u32[]{:S(2)}) copy-start(bf16[16,128,480]{1,2,0:T(8,128)(2,1)} %param.18) | copy-start | bytes 5898244
  16.3 2.9 %copy-start.1 = (f32[8,32,960]{2,1,0:T(8,128)S(1)}, f32[8,32,960]{2,1,0:T(8,128)}, u32[]{:S(2)}) copy-start(f32[8,32,960]{2,1,0:T(8,128)} %param.14) | copy-start | bytes 2949124
  16.3 2.9 %copy-start.2 = (f32[8,32,480]{2,1,0:T(8,128)S(1)}, f32[8,32,480]{2,1,0:T(8,128)}, u32[]{:S(2)}) copy-start(f32[8,32,480]{2,1,0:T(8,128)} %param.13) | copy-start | bytes 1474564
  16.3 2.9 %copy-start.8 = (s32[16]{0:T(128)S(1)}, s32[16]{0:T(128)}, u32[]{:S(2)}) copy-start(s32[16]{0:T(128)} %col_ref.1) | copy-start | bytes 196
  16.3 2.9 %copy-start.9 = (s32[16]{0:T(128)S(1)}, s32[16]{0:T(128)}, u32[]{:S(2)}) copy-start(s32[16]{0:T(128)} %block_ref.3) | copy-start | bytes 196
  18.9 33.3 %collective-permute-start.6 = (bf16[2,256,512]{2,1,0:T(8,128)(2,1)}, bf16[2,256,512]{2,1,0:T(8,128)(2,1)}, u32[]{:S(2)}, u32[]{:S(2)}) collective-permute-start(bf16[2,256,512]{2,1,0:T(8,128)(2,1)} %get-tuple-element.34), channel_id=1, source_target_pairs={{0,16},{16,0},{1,17},{17,1},{2,18},{18,2},{3,19},{19,3},{4,20},{20... | collective-permute-start | bytes 1572872 | tf_op jit(solution)/shard_map/ppermute | solution.py:370
  19.2 29.6 %copy-start.10 = (s32[16]{0:T(128)S(1)}, s32[16]{0:T(128)}, u32[]{:S(2)}) copy-start(s32[16]{0:T(128)} %view_ref.1) | copy-start | bytes 196
  20.9 0.7 copy-start.4
  21.5 30.6 %copy-start.3 = (bf16[2,256,512]{2,1,0:T(8,128)(2,1)S(1)}, bf16[2,256,512]{2,1,0:T(8,128)(2,1)}, u32[]{:S(2)}) copy-start(bf16[2,256,512]{2,1,0:T(8,128)(2,1)} %get-tuple-element.35.data_own_ref) | copy-start | bytes 1572868
  21.5 30.6 %copy-start.12 = (bf16[256,256]{1,0:T(8,128)(2,1)S(1)}, bf16[256,256]{1,0:T(8,128)(2,1)}, u32[]{:S(2)}) copy-start(bf16[256,256]{1,0:T(8,128)(2,1)} %constant.50.clone.ztab_ref) | copy-start | bytes 393220
  21.6 4.6 %collective-permute-start = (f32[16,128]{1,0:T(8,128)S(1)}, f32[16,128]{1,0:T(8,128)S(1)}, u32[]{:S(2)}, u32[]{:S(2)}) collective-permute-start(f32[16,128]{1,0:T(8,128)S(1)} %get-tuple-element.20), channel_id=1, source_target_pairs={{0,1},{1,0},{2,3},{3,2},{4,5},{5,4},{6,7},{7,6},{8,9},{9,8},{10,11... | collective-permute-start | bytes 24584 | tf_op jit(solution)/shard_map/ppermute | solution.py:384
  26.2 4.7 %collective-permute-start.1 = (f32[16,128]{1,0:T(8,128)S(1)}, f32[16,128]{1,0:T(8,128)S(1)}, u32[]{:S(2)}, u32[]{:S(2)}) collective-permute-start(f32[16,128]{1,0:T(8,128)S(1)} %add.44), channel_id=1, source_target_pairs={{0,2},{1,3},{2,0},{3,1},{4,6},{5,7},{6,4},{7,5},{8,10},{9,11},{10,... | collective-permute-start | bytes 24584 | tf_op jit(solution)/shard_map/ppermute | solution.py:384
  30.9 5.7 %collective-permute-start.2 = (f32[16,128]{1,0:T(8,128)S(1)}, f32[16,128]{1,0:T(8,128)S(1)}, u32[]{:S(2)}, u32[]{:S(2)}) collective-permute-start(f32[16,128]{1,0:T(8,128)S(1)} %add.45), channel_id=1, source_target_pairs={{0,4},{1,5},{2,6},{3,7},{4,0},{5,1},{6,2},{7,3},{8,12},{9,13},{10,... | collective-permute-start | bytes 24584 | tf_op jit(solution)/shard_map/ppermute | solution.py:384
  32.5 14.4 %collective-permute-start.4 = (f32[16,512]{1,0:T(8,128)}, f32[16,512]{1,0:T(8,128)S(1)}, u32[]{:S(2)}, u32[]{:S(2)}) collective-permute-start(f32[16,512]{1,0:T(8,128)} %get-tuple-element.22), channel_id=1, source_target_pairs={{0,1},{1,2},{2,3},{3,4},{4,5},{5,6},{6,7},{7,8},{8,9},{9,10},{10,1... | collective-permute-start | bytes 98312 | tf_op jit(solution)/shard_map/ppermute | solution.py:381
  33.8 13.1 %collective-permute-start.5 = (f32[16,512]{1,0:T(8,128)}, f32[16,512]{1,0:T(8,128)S(1)}, u32[]{:S(2)}, u32[]{:S(2)}) collective-permute-start(f32[16,512]{1,0:T(8,128)} %get-tuple-element.23), channel_id=1, source_target_pairs={{1,0},{2,1},{3,2},{4,3},{5,4},{6,5},{7,6},{8,7},{9,8},{10,9},{11,1... | collective-permute-start | bytes 98312 | tf_op jit(solution)/shard_map/ppermute | solution.py:382
  36.6 10.3 %collective-permute-start.3 = (f32[16,128]{1,0:T(8,128)S(1)}, f32[16,128]{1,0:T(8,128)S(1)}, u32[]{:S(2)}, u32[]{:S(2)}) collective-permute-start(f32[16,128]{1,0:T(8,128)S(1)} %add.46), channel_id=1, source_target_pairs={{0,8},{1,9},{2,10},{3,11},{4,12},{5,13},{6,14},{7,15},{8,0},{9,1},... | collective-permute-start | bytes 24584 | tf_op jit(solution)/shard_map/ppermute | solution.py:384
  46.9 0.9 copy-start.5
  48.8 0.8 copy-start.6
  49.6 0.8 copy-start.7
  52.2 1.6 %copy-start.11 = (bf16[1024,1024]{1,0:T(8,128)(2,1)S(1)}, bf16[1024,1024]{1,0:T(8,128)(2,1)}, u32[]{:S(2)}) copy-start(bf16[1024,1024]{1,0:T(8,128)(2,1)} %constant.49.clone.ytab_hbm) | copy-start | bytes 6291460
  73.6 17.7 %collective-permute-start.7 = (f32[16,1024]{1,0:T(8,128)S(1)}, f32[16,1024]{1,0:T(8,128)S(1)}, u32[]{:S(2)}, u32[]{:S(2)}) collective-permute-start(f32[16,1024]{1,0:T(8,128)S(1)} %get-tuple-element.28), channel_id=1, source_target_pairs={{0,0},{1,16},{2,32},{3,48},{4,64},{5,80},{6,96},{7,112},{8,128},{9... | collective-permute-start | bytes 196616 | tf_op jit(solution)/shard_map/ppermute | solution.py:418
  80.2 15.4 %collective-permute-start.8 = (f32[16,1024]{1,0:T(8,128)S(1)}, f32[16,1024]{1,0:T(8,128)S(1)}, u32[]{:S(2)}, u32[]{:S(2)}) collective-permute-start(f32[16,1024]{1,0:T(8,128)S(1)} %get-tuple-element.29), channel_id=1, source_target_pairs={{0,8},{1,24},{2,40},{3,56},{4,72},{5,88},{6,104},{7,120},{8,136},{... | collective-permute-start | bytes 196616 | tf_op jit(solution)/shard_map/ppermute | solution.py:421
  84.6 6.7 %collective-permute-start.9 = (f32[8,1024]{1,0:T(8,128)S(1)}, f32[8,1024]{1,0:T(8,128)S(1)}, u32[]{:S(2)}, u32[]{:S(2)}) collective-permute-start(f32[8,1024]{1,0:T(8,128)S(1)} %get-tuple-element.31), channel_id=1, source_target_pairs={{0,128},{128,0},{1,129},{129,1},{2,130},{130,2},{3,131},{131,3},{4... | collective-permute-start | bytes 98312 | tf_op jit(solution)/shard_map/ppermute | solution.py:424

commit v3 on v2

v3 whole, which is shorter than its diff:
```python
import math

import jax
import jax.numpy as jnp
import numpy as np
from jax import lax
from jax.experimental import pallas as pl
from jax.experimental.pallas import tpu as pltpu
from jax.sharding import Mesh, PartitionSpec as P

coupling_weight = 0.1
mag_smooth = 0.3
eta_smooth = 0.3

ZS, NX, NY, NZ = 8, 32, 480, 128
HALF = 512
ROW = 2 * HALF
CHUNK = 152
GRP = ("zh", "x", "c")
GZ = ("zl", "y")
f32, bf16 = jnp.float32, jnp.bfloat16

SMEM = pl.BlockSpec(memory_space=pltpu.SMEM)
VMEM = pl.BlockSpec(memory_space=pltpu.VMEM)
ANY = pl.BlockSpec(memory_space=pl.ANY)


def dft_parts(length):
    indices = np.arange(length)
    angles = (indices[:, None] * indices[None, :] % length) * (2.0 * math.pi / length)
    scaling = 1.0 / math.sqrt(length)
    return np.cos(angles) * scaling, -np.sin(angles) * scaling


def y_table():
    real_part, imag_part = dft_parts(NY)
    table = np.zeros((2, HALF, 2, HALF), np.float64)
    table[0, :NY, 0, :NY] = real_part
    table[0, :NY, 1, :NY] = imag_part
    table[1, :NY, 0, :NY] = -imag_part
    table[1, :NY, 1, :NY] = real_part
    return jnp.asarray(table.reshape(ROW, ROW).astype(jnp.bfloat16))


def z_table():
    real_part, imag_part = dft_parts(NZ)
    table = np.block([[real_part, -imag_part], [imag_part, real_part]])
    return jnp.asarray(table.astype(jnp.bfloat16))


def call(kernel, out_shape, in_specs, scratch, flops, moved, name, out_spec=VMEM, grant=40):
    return pl.pallas_call(
        kernel,
        out_shape=out_shape,
        in_specs=in_specs,
        out_specs=jax.tree.map(lambda _: out_spec, out_shape),
        scratch_shapes=scratch,
        compiler_params=pltpu.CompilerParams(vmem_limit_bytes=grant * 1024 * 1024),
        cost_estimate=pl.CostEstimate(flops=flops, bytes_accessed=moved, transcendentals=0),
        name=name,
    )


def order_tables():
    tables = []
    for count in (2 * ZS, ZS):
        rows = np.arange(NX * count)
        place, q = rows // count, rows % count
        table = np.zeros((NX * count, NX * count), np.float32)
        table[rows, q * NX + 2 * (place % 16) + place // 16] = 1.0
        tables.append(jnp.asarray(table.astype(jnp.bfloat16)))
    return tables


def pack_kernel(core_ref, sens_hbm, mr_hbm, order_hbm, short_hbm, out_hbm, sens_ref, mr_ref, order_ref,
                short_ref, rows_ref, mr_rows, out_ref, sems, out_sems):
    copies = []
    for n in range(4):
        part = pl.ds(64 * n, 64)
        copies.append(pltpu.make_async_copy(mr_hbm.at[part], mr_ref.at[part], sems.at[n]))
    for n in range(4):
        part = pl.ds(128 * n, 128)
        copies.append(pltpu.make_async_copy(sens_hbm.at[part], sens_ref.at[part], sems.at[4 + n]))
    copies.append(pltpu.make_async_copy(order_hbm, order_ref, sems.at[8]))
    copies.append(pltpu.make_async_copy(short_hbm, short_ref, sems.at[9]))
    for copy in copies:
        copy.start()
    imag = core_ref[0] == 1
    rows_ref[256:, HALF + NY :] = jnp.zeros((256, HALF - NY), bf16)
    for n in range(4):
        copies[n].wait()
        part = pl.ds(64 * n, 64)
        values = jnp.where(imag, mr_ref[part, NY:], mr_ref[part, :NY]).astype(bf16)
        mr_rows[part, :] = values[:, :384]
        rows_ref[part, NY:HALF] = values[:, 384:416]
        rows_ref[pl.ds(256 + 64 * n, 64), NY:HALF] = values[:, 416:448]
        rows_ref[part, HALF + NY :] = values[:, 448:]
    for n in range(4):
        copies[4 + n].wait()
        part = pl.ds(128 * n, 128)
        rows_ref[part, :NY] = sens_ref[part, :NY]
        rows_ref[part, HALF : HALF + NY] = sens_ref[part, NY:]
    copies[8].wait()
    copies[9].wait()
    out_copies = []

    def send(rows):
        place = (slice(None), rows)
        copy = pltpu.make_async_copy(out_ref.at[place], out_hbm.at[place], out_sems.at[len(out_copies)])
        copy.start()
        out_copies.append(copy)

    moved = jnp.dot(short_ref[...], mr_rows[...], preferred_element_type=f32)
    blocks = [moved[:, 128 * b : 128 * (b + 1)].reshape(NX, ZS, 128) for b in range(3)]
    out_ref[:, 128:, :] = jnp.concatenate(blocks, 1).astype(bf16)
    for n in range(4):
        moved = jnp.dot(order_ref[...], rows_ref[:, 256 * n : 256 * (n + 1)], preferred_element_type=f32)
        for b in range(2):
            first = 16 * (2 * n + b)
            block = moved[:, 128 * b : 128 * (b + 1)].astype(bf16)
            out_ref[:, first : first + 16, :] = block.reshape(NX, 16, 128)
        send(pl.ds(32 * n, 32))
    send(pl.ds(128, CHUNK - 128))
    for copy in out_copies:
        copy.wait()


def prepare_kernel(core_ref, data_ref, mask_ref, own_out, other_out):
    pad = jnp.zeros((HALF - NY, NZ), f32)

    def turned(values):
        return jnp.concatenate([values.astype(f32), pad], 0).T.astype(bf16)

    for k in range(2):
        for place, out in ((core_ref[0], own_out), (1 - core_ref[0], other_out)):
            for part in range(2):
                values = data_ref[k, place, part * NY : (part + 1) * NY, :]
                out[k, part * NZ : (part + 1) * NZ, :] = turned(values)
    own_out[2, :NZ, :] = turned(mask_ref[...])
    own_out[2, NZ:, :] = jnp.zeros((NZ, HALF), bf16)


def project_kernel(
    info_ref, col_ref, block_ref, xs_ref, pet_ref, mr_ref, tiles_ref,
    pay_ref, win_ref, low_ref, high_ref, picked,
):
    for t in range(16):
        picked[pl.ds(t, 1), :] = pet_ref[pl.ds(col_ref[t], 1), :]
    rows = picked[...].astype(bf16)
    pay_ref[:16, :] = jnp.zeros((16, 128), f32)
    for t in range(16):
        product = jnp.dot(rows, tiles_ref[t], preferred_element_type=f32)
        place = pl.ds(block_ref[t], 1)
        pay_ref[place, :] = pay_ref[place, :] + product[t : t + 1, :]
    win_ref[...] = jnp.zeros((12, ZS, HALF), f32)
    for r in range(4):
        for z in range(ZS):
            place = pl.ds(xs_ref[r] + z * NX, 1)
            win_ref[r, z : z + 1, :NY] = pet_ref[place, :]
            win_ref[4 + r, z : z + 1, :NY] = mr_ref[place, :NY]
            win_ref[8 + r, z : z + 1, :NY] = mr_ref[place, NY:]
    for b in range(4):
        for r in range(12):
            row = pl.ds(12 * b + r, 1)
            low_ref[row, :] = win_ref[r, 0:1, 128 * b : 128 * (b + 1)]
            high_ref[row, :] = win_ref[r, ZS - 1 : ZS, 128 * b : 128 * (b + 1)]
    pay_ref[16:, :] = jnp.where(info_ref[2] == 1, low_ref[...], high_ref[...])


def ratio_rows(block_ref, view_ref, pay_ref, got_ref, measured_ref, background_ref, ratio, gathered):
    for j in range(16):
        counts = measured_ref[pl.ds(view_ref[j], 1), :]
        back = background_ref[pl.ds(view_ref[j], 1), :]
        projection = (pay_ref[j : j + 1, :] + got_ref[j : j + 1, :]) / NY
        ratio[j : j + 1, :] = 1.0 - counts / (projection + back)
    for t in range(16):
        gathered[t : t + 1, :] = ratio[pl.ds(block_ref[t], 1), :]
    return gathered[...].astype(bf16)


def backproject(col_ref, rows, tiles_ref, acc, out_ref):
    acc[...] = jnp.zeros((4, ZS * NX, 128), f32)
    for t in range(16):
        spread = lax.dot_general(
            rows, tiles_ref[t], (((1,), (1,)), ((), ())), preferred_element_type=f32
        )
        place = pl.ds(col_ref[t], 1)
        for b in range(4):
            block = spread[t : t + 1, 128 * b : min(128 * (b + 1), NY)]
            lanes = slice(0, block.shape[1])
            acc[b, place, lanes] = acc[b, place, lanes] + block
    for p in range(16):
        rows_out = slice((2 + p // 8) * ZS, (3 + p // 8) * ZS)
        for k in range(2):
            for b in range(4):
                block = acc[b, pl.ds(2 * p + k, ZS, stride=NX), :] / NY
                first = k * HALF + 128 * b
                out_ref[p % 8, rows_out, first : first + 128] = block.astype(bf16)


def coupling_kernel(
    info_ref, win_ref, got_a, got_b, got_c, got_d, pet_out, mr_out, planes, mags, moved
):
    z_start, x_first = info_ref[0], info_ref[1]
    edges = []
    for which in (info_ref[6], info_ref[7]):
        edge = got_d[16:, :]
        for step, got in enumerate((got_a, got_b, got_c)):
            edge = jnp.where(which == step, got[16:, :], edge)
        edges.append(edge)
    planes[...] = jnp.zeros((12, 24, HALF), f32)
    for r in range(12):
        planes[r, 1 : ZS + 1, :] = win_ref[r]
        for b in range(4):
            lanes = slice(128 * b, 128 * (b + 1))
            planes[r, 0:1, lanes] = edges[0][12 * b + r : 12 * b + r + 1, :]
            planes[r, ZS + 1 : ZS + 2, lanes] = edges[1][12 * b + r : 12 * b + r + 1, :]
    for r in range(4):
        mags[r] = jnp.sqrt(planes[4 + r] ** 2 + planes[8 + r] ** 2 + mag_smooth**2)
    shape = (16, HALF)
    level = z_start - 1 + lax.broadcasted_iota(jnp.int32, shape, 0)
    lane = lax.broadcasted_iota(jnp.int32, shape, 1)
    step_z = level < NZ - 1
    step_y = lane < NY - 1
    term_z = (level >= 0) & (lane < NY)

    def differences(ref, r, step_x):
        here = ref[r, 0:16, :]
        along_z = jnp.where(step_z, ref[r, 1:17, :] - here, 0.0)
        along_x = jnp.where(step_x, ref[r + 1, 0:16, :] - here, 0.0)
        along_y = jnp.where(step_y, pltpu.roll(here, HALF - 1, 1) - here, 0.0)
        return along_z, along_x, along_y

    grads = []
    for r in range(3):
        place = x_first - 1 + r
        step_x = place < NX - 1
        a = differences(planes, r, step_x)
        b = differences(mags, r, step_x)
        a_sq = a[0] ** 2 + a[1] ** 2 + a[2] ** 2
        b_sq = b[0] ** 2 + b[1] ** 2 + b[2] ** 2
        cross = a[0] * b[0] + a[1] * b[1] + a[2] * b[2]
        weight = lax.rsqrt(eta_smooth**2 + a_sq * b_sq - cross * cross)
        weight = jnp.where(term_z & (place >= 0), weight, 0.0)
        grads.append(
            (
                [(p * b_sq - q * cross) * weight for p, q in zip(a, b)],
                [(q * a_sq - p * cross) * weight for p, q in zip(a, b)],
            )
        )

    for k in range(2):
        found = []
        for which in range(2):
            here, before = grads[k + 1][which], grads[k][which]
            total = before[1] - here[0] - here[1] - here[2]
            total = total + pltpu.roll(here[0], 1, 0) + pltpu.roll(here[2], 1, 1)
            found.append(coupling_weight * total)
        moved[0] = found[0]
        scaled = found[1] / mags[k + 1, 0:16, :]
        moved[1] = scaled * planes[5 + k, 0:16, :]
        moved[2] = scaled * planes[9 + k, 0:16, :]
        pet_out[k] = moved[0, 1 : ZS + 1, :]
        mr_out[k, :, :HALF] = moved[1, 1 : ZS + 1, :]
        mr_out[k, :, HALF:] = moved[2, 1 : ZS + 1, :]


def coil_kernel(core_ref, col_ref, block_ref, view_ref, recv_hbm, ytab_hbm, ztab_hbm, data_own_hbm,
                data_got_hbm, tiles_hbm, pay_hbm, got_hbm, measured_hbm, background_hbm,
                out_hbm, recv_ref, ytab_ref, ztab_ref, data_ref, mask_ref, tiles_ref, bins_ref, counts_ref,
                ratio, gathered, acc, sens, images, kyrows, out_ref, sems, out_sems):
    copies = []

    def fetch(source, target):
        copies.append(pltpu.make_async_copy(source, target, sems.at[len(copies)]))
        copies[-1].start()
        return copies[-1]

    small = [
        fetch(pay_hbm, bins_ref.at[0]), fetch(got_hbm, bins_ref.at[1]),
        fetch(measured_hbm, counts_ref.at[0]), fetch(background_hbm, counts_ref.at[1]),
    ]
    received = [fetch(recv_hbm.at[pl.ds(8 * n, 8)], recv_ref.at[pl.ds(8 * n, 8)]) for n in range(4)]
    tables = [
        fetch(ytab_hbm.at[pl.ds(256 * n, 256)], ytab_ref.at[pl.ds(256 * n, 256)]) for n in range(4)
    ]
    others = [
        fetch(ztab_hbm, ztab_ref),
        fetch(data_own_hbm.at[pl.ds(0, 2)], data_ref.at[core_ref[0]]),
        fetch(data_got_hbm, data_ref.at[1 - core_ref[0]]),
        fetch(data_own_hbm.at[2], mask_ref),
    ]
    tiles = [fetch(tiles_hbm.at[pl.ds(4 * n, 4)], tiles_ref.at[pl.ds(4 * n, 4)]) for n in range(4)]
    for copy in small:
        copy.wait()
    ratio_now = ratio_rows(
        block_ref, view_ref, bins_ref.at[0], bins_ref.at[1], counts_ref.at[0], counts_ref.at[1], ratio, gathered
    )
    for copy in received:
        copy.wait()

    def block(c, b):
        return recv_ref[16 * c : 16 * (c + 1), 16 * b : 16 * (b + 1), :].astype(f32)

    lane = lax.broadcasted_iota(jnp.int32, (NZ, 128), 1)

    def image_part(c):
        tail = recv_ref[16 * c : 16 * (c + 1), 128:, :].astype(f32)
        parts = [tail[:, ZS * b : ZS * (b + 1)].reshape(NZ, 128) for b in range(3)]
        real, imag = block(c, 3), block(c, 7)
        first = pltpu.roll(real[:, :ZS].reshape(NZ, 128), 32, 1)
        second = pltpu.roll(real[:, ZS:].reshape(NZ, 128), 64, 1)
        third = pltpu.roll(imag[:, :ZS].reshape(NZ, 128), 96, 1)
        last = jnp.where(lane < 32, first, jnp.where(lane < 64, second, third))
        return jnp.concatenate(parts + [jnp.where(lane < 96, last, 0.0)], -1)

    mr_re, mr_im = image_part(0), image_part(1)
    for c in range(2):
        for b in range(4):
            real, imag = block(c, b), block(c, 4 + b)
            lanes = slice(128 * b, 128 * (b + 1))
            lanes_im = slice(HALF + 128 * b, HALF + 128 * (b + 1))
            for k in range(2):
                rows = pl.ds((2 * c + k) * NZ, NZ)
                s_re = real[:, k * ZS : (k + 1) * ZS].reshape(NZ, 128)
                s_im = imag[:, k * ZS : (k + 1) * ZS].reshape(NZ, 128)
                sens[rows, lanes] = s_re
                sens[rows, lanes_im] = s_im
                images[rows, lanes] = (s_re * mr_re[:, lanes] - s_im * mr_im[:, lanes]).astype(bf16)
                images[rows, lanes_im] = (s_re * mr_im[:, lanes] + s_im * mr_re[:, lanes]).astype(bf16)
    for copy in tables:
        copy.wait()
    kyrows[...] = jnp.dot(images[...], ytab_ref[...], preferred_element_type=f32).astype(bf16)
    for copy in others:
        copy.wait()
    mask = mask_ref[:NZ, :].astype(f32)
    ztab = ztab_ref[...]
    for q in range(4):
        rows = pl.ds(q * NZ, NZ)
        volume = jnp.concatenate([kyrows[rows, :HALF], kyrows[rows, HALF:]], 0)
        kspace = jnp.dot(ztab, volume, preferred_element_type=f32)
        data = data_ref[q // 2, q % 2].astype(f32)
        misfit = jnp.concatenate(
            [mask * (kspace[:NZ] - data[:NZ]), mask * (data[NZ:] - kspace[NZ:])], 0
        ).astype(bf16)
        back = jnp.dot(ztab, misfit, preferred_element_type=f32).astype(bf16)
        images[rows, :HALF] = back[:NZ]
        images[rows, HALF:] = back[NZ:]
    for copy in tiles:
        copy.wait()
    backproject(col_ref, ratio_now, tiles_ref, acc, out_ref)
    for b in range(4):
        lanes = slice(128 * b, 128 * (b + 1))
        lanes_im = slice(HALF + 128 * b, HALF + 128 * (b + 1))
        table = jnp.concatenate([ytab_ref[:, lanes], ytab_ref[:, lanes_im]], 1)
        image = jnp.dot(images[...], table, preferred_element_type=f32)
        total_re = jnp.zeros((NZ, 128), f32)
        total_im = jnp.zeros((NZ, 128), f32)
        for q in range(4):
            rows = slice(q * NZ, (q + 1) * NZ)
            s_re, s_im = sens[rows, lanes], sens[rows, lanes_im]
            i_re, i_im = image[rows, :128], image[rows, 128:]
            total_re = total_re + (s_re * i_re - s_im * i_im)
            total_im = total_im - (s_re * i_im + s_im * i_re)
        for total, place in ((total_re, lanes), (total_im, lanes_im)):
            slabs = total.reshape(2, 8, ZS, 128)
            out_ref[:, : 2 * ZS, place] = jnp.concatenate([slabs[0], slabs[1]], 1).astype(bf16)
    out_copies = []
    for n in range(2):
        part = pl.ds(4 * n, 4)
        out_copies.append(pltpu.make_async_copy(out_ref.at[part], out_hbm.at[part], out_sems.at[n]))
        out_copies[-1].start()
    for copy in out_copies:
        copy.wait()


def sum_kernel(half_ref, recv_ref, mr_own, mr_other, pet_own, pet_other):
    upper = half_ref[0] == 1
    pet = jnp.zeros((2 * ZS, ROW), f32)
    for c in range(2):
        mr = jnp.zeros((2 * ZS, ROW), f32)
        for x in range(4):
            block = recv_ref[2 * x + c].astype(f32)
            mr = mr + block[: 2 * ZS]
            pet = pet + block[2 * ZS :]
        rows = pl.ds(c * ZS, ZS)
        mr_own[rows, :] = jnp.where(upper, mr[ZS:], mr[:ZS]).astype(bf16)
        mr_other[rows, :] = jnp.where(upper, mr[:ZS], mr[ZS:]).astype(bf16)
    pet_own[...] = jnp.where(upper, pet[ZS:], pet[:ZS])
    pet_other[...] = jnp.where(upper, pet[:ZS], pet[ZS:]).astype(bf16)


def final_kernel(mr_a, mr_b, pet_a, pet_b, couple_pet_ref, couple_mr_ref, pet_out, mr_out):
    for k in range(2):
        rows = pl.ds(k * ZS, ZS)
        lanes = pl.ds(k * HALF, HALF)
        pet = pet_a[:, lanes] + pet_b[:, lanes].astype(f32) + couple_pet_ref[k]
        mr = mr_a[rows, :].astype(f32) + mr_b[rows, :].astype(f32) + couple_mr_ref[k]
        pet_out[:, k, :] = pet[:, :NY]
        mr_out[:, k, :NY] = mr[:, :NY]
        mr_out[:, k, NY:] = mr[:, HALF : HALF + NY]


def sds(shape, dtype):
    return jax.ShapeDtypeStruct(shape, dtype)


def on_device(
    pet_image, mr_image, coil_sens, kspace_data, kspace_mask, system_tiles,
    tile_subset_block, tile_col, measured, background, subset_view_blocks,
):
    core = lax.axis_index("c")
    grp = lax.axis_index(GRP)
    gz = lax.axis_index(GZ)
    core_arr = core.astype(jnp.int32).reshape(1)
    pet_rows = pet_image.reshape(ZS * NX, NY)
    mr_rows = mr_image.reshape(ZS * NX, 2 * NY)
    tiles = system_tiles.swapaxes(1, 2)

    sent = call(
        pack_kernel, sds((32, CHUNK, 128), bf16), [SMEM] + [ANY] * 4,
        [pltpu.VMEM((2 * ZS * NX, 2 * NY), bf16), pltpu.VMEM((ZS * NX, 2 * NY), f32),
         pltpu.VMEM((512, 512), bf16), pltpu.VMEM((256, 256), bf16), pltpu.VMEM((512, ROW), bf16),
         pltpu.VMEM((256, 384), bf16), pltpu.VMEM((32, CHUNK, 128), bf16),
         pltpu.SemaphoreType.DMA((10,)), pltpu.SemaphoreType.DMA((5,))],
        10**6, 4 * 10**6, "pack", ANY, 60,
    )(core_arr, coil_sens.reshape(2 * ZS * NX, 2 * NY), mr_rows, *order_tables())
    sent, tile_col = lax.optimization_barrier((sent, tile_col))
    recv = lax.all_to_all(sent, ("c",) + GZ, split_axis=0, concat_axis=0, tiled=True)

    xs = jnp.clip(2 * grp - 1 + jnp.arange(4, dtype=jnp.int32), 0, NX - 1)
    bits = [(gz >> t) & 1 for t in range(4)]
    ones = [gz & 1, (gz & 3) == 3, (gz & 7) == 7]
    zeros = [(gz & 1) == 0, (gz & 3) == 0, (gz & 7) == 0]
    after = sum(jnp.asarray(v).astype(jnp.int32) for v in ones)
    before = sum(jnp.asarray(v).astype(jnp.int32) for v in zeros)
    info = jnp.stack([gz * ZS, 2 * grp] + bits + [before, after]).astype(jnp.int32)
    pay, win, low, high = call(
        project_kernel,
        (sds((64, 128), f32), sds((12, ZS, HALF), f32), sds((48, 128), f32), sds((48, 128), f32)),
        [SMEM] * 4 + [VMEM] * 3, [pltpu.VMEM((16, NY), f32)],
        10**7, 4 * 10**6, "project", VMEM, 8,
    )(info, tile_col, tile_subset_block, xs, pet_rows, mr_rows, tiles)
    got = []
    for step in range(4):
        got.append(lax.ppermute(pay, GZ, [(i, i ^ (2 ** (step + 1) - 1)) for i in range(16)]))
        if step == 0:
            kspace_data, got[0] = lax.optimization_barrier((kspace_data, got[0]))
        if step < 3:
            edge = jnp.where(bits[step + 1] == 1, low, high)
            pay = jnp.concatenate([pay[:16] + got[step][:16], edge], 0)
    data_own, data_out = call(
        prepare_kernel, (sds((3, 2 * NZ, HALF), bf16), sds((2, 2 * NZ, HALF), bf16)),
        [SMEM, VMEM, VMEM], [], 10**6, 3 * 10**6, "prepare", VMEM, 8,
    )(core_arr, kspace_data.transpose(0, 2, 3, 1), kspace_mask.T)
    data_got = lax.ppermute(data_out, "c", [(0, 1), (1, 0)])
    couple_pet, couple_mr = call(
        coupling_kernel, (sds((2, ZS, HALF), f32), sds((2, ZS, ROW), f32)),
        [SMEM] + [VMEM] * 5,
        [pltpu.VMEM((12, 24, HALF), f32), pltpu.VMEM((4, 24, HALF), f32),
         pltpu.VMEM((3, 16, HALF), f32)],
        10**6, 10**6, "coupling", VMEM, 8,
    )(info, win, *got)

    parts = call(
        coil_kernel, sds((8, 4 * ZS, ROW), bf16), [SMEM] * 4 + [ANY] * 10,
        [pltpu.VMEM((32, CHUNK, 128), bf16), pltpu.VMEM((ROW, ROW), bf16),
         pltpu.VMEM((2 * NZ, 2 * NZ), bf16), pltpu.VMEM((2, 2, 2 * NZ, HALF), bf16),
         pltpu.VMEM((2 * NZ, HALF), bf16), pltpu.VMEM((16, NY, 128), bf16),
         pltpu.VMEM((2, 64, 128), f32), pltpu.VMEM((2, 64, 128), f32),
         pltpu.VMEM((16, 128), f32), pltpu.VMEM((16, 128), f32), pltpu.VMEM((4, ZS * NX, 128), f32),
         pltpu.VMEM((4 * NZ, ROW), f32), pltpu.VMEM((4 * NZ, ROW), bf16),
         pltpu.VMEM((4 * NZ, ROW), bf16), pltpu.VMEM((8, 4 * ZS, ROW), bf16),
         pltpu.SemaphoreType.DMA((20,)), pltpu.SemaphoreType.DMA((2,))],
        5 * 10**9, 6 * 10**6, "coils", ANY, 61,
    )(core_arr, tile_col, tile_subset_block, subset_view_blocks, recv, y_table(), z_table(), data_own,
      data_got, tiles, pay, got[3], measured, background)

    both = lax.all_to_all(parts, ("x", "c"), split_axis=0, concat_axis=0, tiled=True)
    half = lax.axis_index("zh").astype(jnp.int32).reshape(1)
    mr_own, mr_other, pet_own, pet_other = call(
        sum_kernel,
        (sds((2 * ZS, ROW), bf16), sds((2 * ZS, ROW), bf16), sds((ZS, ROW), f32), sds((ZS, ROW), bf16)),
        [SMEM, VMEM], [], 10**6, 10**6, "sums",
    )(half, both)
    places = [(zh, p, j) for zh in range(2) for p in range(8) for j in range(16)]
    mr_a = lax.ppermute(
        mr_own, GRP + GZ, [((zh * 8 + p) * 16 + j, j * 16 + zh * 8 + p) for zh, p, j in places]
    )
    mr_b = lax.ppermute(
        mr_other, GRP + GZ, [((zh * 8 + p) * 16 + j, j * 16 + (1 - zh) * 8 + p) for zh, p, j in places]
    )
    pet_got = lax.ppermute(pet_other, "zh", [(0, 1), (1, 0)])
    return call(
        final_kernel, (sds((ZS, 2, NY), f32), sds((ZS, 2, 2 * NY), f32)), [VMEM] * 6, [],
        10**5, 10**6, "final",
    )(mr_a, mr_b, pet_own, pet_got, couple_pet, couple_mr)


def solution(mesh):
    fine = Mesh(mesh.devices.reshape(2, 4, 2, 4, 4), ("zh", "x", "c", "zl", "y"))
    placed = (
        P(GZ, None, None),
        P(GZ, None, None),
        P(GRP, GZ, None, None),
        P(GRP, None, GZ, None),
        P(),
        P(GRP + GZ, None, None),
        P(GRP + GZ),
        P(GRP + GZ),
        P(GRP, None),
        P(GRP, None),
        P(GRP),
    )
    return jax.shard_map(
        on_device,
        mesh=fine,
        in_specs=placed,
        out_specs=(P(GZ, GRP, None), P(GZ, GRP, None)),
        check_vma=False,
    )
```

time: 97 us -> 89.8 us (0.926)
  the two profiles are of different devices: /device:TPU:7 before, /device:TPU:6 now
where the time goes in v3:
time: 89.8 us; the launch traced here: 89.3 us
  starting transfers between devices  31.8 us (35%)
  waiting for transfers between devices  19.8 us (22%)
  Pallas kernels  16.5 us (18%)
  blocking collectives  13.1 us (15%)
  local copies, waits for them, and re-layouts  5.79 us (6%)
  other arithmetic  1.49 us (2%)
    ppermute x4, waiting for transfers between devices, on_device(): lax.ppermute(pay, GZ, [(i, i ^ 2 ** (step + 1) - 1) for i in range(16)])  13.9 us
    all_to_all x1, blocking collectives, on_device(): lax.all_to_all(parts, ('x', 'c'), split_axis=0, concat_axis=0, tiled=True)  13.1 us
    ppermute x4, starting transfers between devices, on_device(): lax.ppermute(pay, GZ, [(i, i ^ 2 ** (step + 1) - 1) for i in range(16)])  9.65 us
    all_to_all x1, starting transfers between devices, on_device(): lax.all_to_all(sent, ('c',) + GZ, split_axis=0, concat_axis=0, tiled=True)  9.18 us
    pallas_call x1, Pallas kernels, on_device(): call(coil_kernel, sds((8, 4 * ZS, ROW), bf16), [SMEM] * 4 + [ANY] * 10, [...  8.4 us
    ppermute x1, starting transfers between devices, on_device(): lax.ppermute(mr_other, GRP + GZ, [((zh * 8 + p) * 16 + j, j * 16 + (1 - z...  6.32 us
    unnamed x32, local copies, waits for them, and re-layouts  5.7 us
    ppermute x1, starting transfers between devices, on_device(): lax.ppermute(mr_own, GRP + GZ, [((zh * 8 + p) * 16 + j, j * 16 + zh * 8 +...  5.23 us
  transfers between devices with their start and end apart: 9, of which 6 were waited for; matrix products, arithmetic and copies ran while one was open for 2% of the time, Pallas kernels for 3%

profile of v3, /device:TPU:6, one launch (start us, length us, event | category | flops | bytes accessed | tf_op | source)
XLA Modules:
  0.0 89.3 jit_solution(829196440045233131)
XLA Ops:
  0.6 0.0 copy-start.1
  0.6 4.2 %pack.1 = bf16[32,152,128]{2,1,0:T(8,128)(2,1)} custom-call(s32[1]{0:T(128)} %bitcast.1.core_ref, bf16[512,960]{1,0:T(8,128)(2,1)} %bitcast.23, f32[256,960]{1,0:T(8,128)} %bitcast.16, bf16[512,512]{1,0:T(8,128)(2,1)} %constant.47.clone.order_hbm, bf16[256,256]{1,0:T(8,128)(2,1)} %constant.48.clone.short_hbm), custom_call_target="tpu_custom_call" | custom-call | flops 1000000 | bytes 4000000 | tf_op jit(solution)/shard_map/pack/pallas_call | solution.py:420
  4.8 0.0 copy-start
  4.8 0.0 copy-start.3
  4.8 0.0 copy-start.11
  4.8 0.0 copy-start.12
  4.9 9.2 %all-to-all-start = ((bf16[32,152,128]{2,1,0:T(8,128)(2,1)}), bf16[32,152,128]{2,1,0:T(8,128)(2,1)}, u32[]{:S(2)}, u32[]{:S(2)}) async-start(bf16[32,152,128]{2,1,0:T(8,128)(2,1)} %pack.1), calls=%async_computation | async-start | bytes 2490368 | tf_op jit(solution)/shard_map/all_to_all | solution.py:429
  14.1 0.1 stack.35.info_ref
  14.2 0.0 copy-done.1
  14.2 0.0 copy-done
  14.2 0.0 copy-done.3
  14.2 0.0 copy-done.11
  14.2 0.0 copy-done.12
  14.2 1.7 %project.1 = (f32[64,128]{1,0:T(8,128)}, f32[12,8,512]{2,1,0:T(8,128)S(1)}, f32[48,128]{1,0:T(8,128)S(1)}, f32[48,128]{1,0:T(8,128)S(1)}) custom-call(s32[8]{0:T(128)S(1)} %stack.35.info_ref, s32[16]{0:T(128)S(1)} %copy-done.11, s32[16]{0:T(128)S(1)} %copy-done.12, s32[4]{0:T(128)S(1)} %add_clamp_fusion.xs_ref, f32[256,480]{1,0:T(8,128)S(1)} %bitcast.21, ...), custom_call_target="tpu_custom_call" | custom-call | flops 10000000 | bytes 4000000 | tf_op jit(solution)/shard_map/project/pallas_call | solution.py:438
  15.9 0.7 copy-done.5
  16.6 0.6 copy-done.9
  17.2 0.6 copy-done.10
  17.8 1.7 %collective-permute-start = (f32[64,128]{1,0:T(8,128)}, f32[64,128]{1,0:T(8,128)S(1)}, u32[]{:S(2)}, u32[]{:S(2)}) collective-permute-start(f32[64,128]{1,0:T(8,128)} %get-tuple-element.20), channel_id=1, source_target_pairs={{0,1},{1,0},{2,3},{3,2},{4,5},{5,4},{6,7},{7,6},{8,9},{9,8},{10,11... | collective-permute-start | bytes 98312 | tf_op jit(solution)/shard_map/ppermute | solution.py:446
  19.5 0.8 broadcast_select_fusion.1
  20.3 5.6 %collective-permute-done.got_a = f32[64,128]{1,0:T(8,128)S(1)} collective-permute-done((f32[64,128]{1,0:T(8,128)}, f32[64,128]{1,0:T(8,128)S(1)}, u32[]{:S(2)}, u32[]{:S(2)}) %collective-permute-start) | collective-permute-done | bytes 32800 | tf_op jit(solution)/shard_map/ppermute | solution.py:446
  25.9 0.7 slice_add_fusion.2
  26.6 0.0 collective-permute-start.2
  26.6 0.0 copy-start.2
  26.6 1.2 %copy-done.2 = bf16[2,128,2,960]{1,3,2,0:T(8,128)(2,1)S(1)} copy-done((bf16[2,128,2,960]{1,3,2,0:T(8,128)(2,1)S(1)}, bf16[2,128,2,960]{1,3,2,0:T(8,128)(2,1)}, u32[]{:S(2)}) %copy-start.2) | copy-done | bytes 983064
  27.8 0.9 %copy-done.4 = s32[128,480]{0,1:T(8,128)S(1)} copy-done((s32[128,480]{0,1:T(8,128)S(1)}, s32[128,480]{0,1:T(8,128)}, u32[]{:S(2)}) %copy-start.4) | copy-done | bytes 245784
  28.7 0.4 prepare.1
  29.1 0.9 copy-done.13
  30.0 0.0 collective-permute-start.1
  30.0 1.8 %collective-permute-done.2.got_b = f32[64,128]{1,0:T(8,128)S(1)} collective-permute-done((f32[64,128]{1,0:T(8,128)S(1)}, f32[64,128]{1,0:T(8,128)S(1)}, u32[]{:S(2)}, u32[]{:S(2)}) %collective-permute-start.2) | collective-permute-done | bytes 32800 | tf_op jit(solution)/shard_map/ppermute | solution.py:446
  31.9 2.3 %collective-permute-start.3 = (f32[64,128]{1,0:T(8,128)S(1)}, f32[64,128]{1,0:T(8,128)S(1)}, u32[]{:S(2)}, u32[]{:S(2)}) collective-permute-start(f32[64,128]{1,0:T(8,128)S(1)} %pad_maximum_fusion.1), channel_id=1, source_target_pairs={{0,7},{1,6},{2,5},{3,4},{4,3},{5,2},{6,1},{7,0},{8,15},{9,14},{10,... | collective-permute-start | bytes 98312 | tf_op jit(solution)/shard_map/ppermute | solution.py:446
  34.2 4.1 %collective-permute-done.3.got_c = f32[64,128]{1,0:T(8,128)S(1)} collective-permute-done((f32[64,128]{1,0:T(8,128)S(1)}, f32[64,128]{1,0:T(8,128)S(1)}, u32[]{:S(2)}, u32[]{:S(2)}) %collective-permute-start.3) | collective-permute-done | bytes 32800 | tf_op jit(solution)/shard_map/ppermute | solution.py:446
  38.3 5.6 %collective-permute-start.4 = (f32[64,128]{1,0:T(8,128)S(1)}, f32[64,128]{1,0:T(8,128)S(1)}, u32[]{:S(2)}, u32[]{:S(2)}) collective-permute-start(f32[64,128]{1,0:T(8,128)S(1)} %pad_maximum_fusion.2.pay_hbm), channel_id=1, source_target_pairs={{0,15},{1,14},{2,13},{3,12},{4,11},{5,10},{6,9},{7,8},{8,7},{9,6},... | collective-permute-start | bytes 98312 | tf_op jit(solution)/shard_map/ppermute | solution.py:446
  44.0 2.4 %collective-permute-done.4.got_hbm.got_d = f32[64,128]{1,0:T(8,128)S(1)} collective-permute-done((f32[64,128]{1,0:T(8,128)S(1)}, f32[64,128]{1,0:T(8,128)S(1)}, u32[]{:S(2)}, u32[]{:S(2)}) %collective-permute-start.4) | collective-permute-done | bytes 32800 | tf_op jit(solution)/shard_map/ppermute | solution.py:446
  46.3 0.0 collective-permute-done.1.data_got_hbm
  46.3 1.4 %all-to-all-done.recv_hbm = bf16[32,152,128]{2,1,0:T(8,128)(2,1)} async-done(((bf16[32,152,128]{2,1,0:T(8,128)(2,1)}), bf16[32,152,128]{2,1,0:T(8,128)(2,1)}, u32[]{:S(2)}, u32[]{:S(2)}) %all-to-all-start) | async-done | bytes 1245216 | tf_op jit(solution)/shard_map/all_to_all | solution.py:429
  47.8 0.0 copy-start.6
  47.8 8.4 %coils.1 = bf16[8,32,1024]{2,1,0:T(8,128)(2,1)} custom-call(s32[1]{0:T(128)} %bitcast.1.core_ref, s32[16]{0:T(128)} %col_ref.1, s32[16]{0:T(128)} %block_ref.3, s32[16]{0:T(128)} %view_ref.1, bf16[32,152,128]{2,1,0:T(8,128)(2,1)} %all-to-all-done.recv_hbm, bf16[1024,1024]{1,0:T(8,128)(2,1)} %constant.49.clone.ytab_hbm, ...), custom_call_target="tpu_custom_call" | custom-call | flops 5000000000 | bytes 6000000 | tf_op jit(solution)/shard_map/coils/pallas_call | solution.py:465
  56.2 13.1 %all_to_all.10.recv_ref = bf16[8,32,1024]{2,1,0:T(8,128)(2,1)S(1)} all-to-all(bf16[8,32,1024]{2,1,0:T(8,128)(2,1)} %coils.1), channel_id=1, replica_groups=mesh['zh'=2,'x'=4,'c'=2,'zl'=4,'y'=4] {'x','c'}, dimensions={0} | all-to-all | bytes 1048576 | tf_op jit(solution)/shard_map/all_to_all | solution.py:479
  69.3 0.1 sums.1
  69.4 5.2 %collective-permute-start.5 = (bf16[16,1024]{1,0:T(8,128)(2,1)S(1)}, bf16[16,1024]{1,0:T(8,128)(2,1)S(1)}, u32[]{:S(2)}, u32[]{:S(2)}) collective-permute-start(bf16[16,1024]{1,0:T(8,128)(2,1)S(1)} %get-tuple-element.27), channel_id=1, source_target_pairs={{0,0},{1,16},{2,32},{3,48},{4,64},{5,80},{6,96},{7,112},{8,128},{9... | collective-permute-start | bytes 98312 | tf_op jit(solution)/shard_map/ppermute | solution.py:487
  74.6 6.3 %collective-permute-start.6 = (bf16[16,1024]{1,0:T(8,128)(2,1)S(1)}, bf16[16,1024]{1,0:T(8,128)(2,1)S(1)}, u32[]{:S(2)}, u32[]{:S(2)}) collective-permute-start(bf16[16,1024]{1,0:T(8,128)(2,1)S(1)} %get-tuple-element.28), channel_id=1, source_target_pairs={{0,8},{1,24},{2,40},{3,56},{4,72},{5,88},{6,104},{7,120},{8,136},{... | collective-permute-start | bytes 98312 | tf_op jit(solution)/shard_map/ppermute | solution.py:490
  80.9 1.5 %collective-permute-start.7 = (bf16[8,1024]{1,0:T(8,128)(2,1)S(1)}, bf16[8,1024]{1,0:T(8,128)(2,1)S(1)}, u32[]{:S(2)}, u32[]{:S(2)}) collective-permute-start(bf16[8,1024]{1,0:T(8,128)(2,1)S(1)} %get-tuple-element.30), channel_id=1, source_target_pairs={{0,128},{128,0},{1,129},{129,1},{2,130},{130,2},{3,131},{131,3},{4... | collective-permute-start | bytes 49160 | tf_op jit(solution)/shard_map/ppermute | solution.py:493
  82.4 0.8 copy-done.8
  83.1 1.0 %coupling.1 = (f32[2,8,512]{2,1,0:T(8,128)S(1)}, f32[2,8,1024]{2,1,0:T(8,128)S(1)}) custom-call(s32[8]{0:T(128)S(1)} %stack.35.info_ref, f32[12,8,512]{2,1,0:T(8,128)S(1)} %copy-done.6, f32[64,128]{1,0:T(8,128)S(1)} %collective-permute-done.got_a, f32[64,128]{1,0:T(8,128)S(1)} %collective-permute-done.2.got_b, f32[64,128]{1,0:T(8,128)S(1)} %collective-permute-done.3.got_c, ...), custom_call_target="tpu_custom_call" | custom-call | flops 1000000 | bytes 1000000 | tf_op jit(solution)/shard_map/coupling/pallas_call | solution.py:457
  84.1 4.4 %collective-permute-done.7.pet_b = bf16[8,1024]{1,0:T(8,128)(2,1)S(1)} collective-permute-done((bf16[8,1024]{1,0:T(8,128)(2,1)S(1)}, bf16[8,1024]{1,0:T(8,128)(2,1)S(1)}, u32[]{:S(2)}, u32[]{:S(2)}) %collective-permute-start.7) | collective-permute-done | bytes 16416 | tf_op jit(solution)/shard_map/ppermute | solution.py:493
  88.6 0.0 collective-permute-done.5.mr_a
  88.6 0.0 collective-permute-done.6.mr_b
  88.6 0.7 final.1
  (19 shorter events, 0.1 us)
Async XLA Ops:
  0.6 13.5 %copy-start.1 = (bf16[16,128,480]{1,2,0:T(8,128)(2,1)S(1)}, bf16[16,128,480]{1,2,0:T(8,128)(2,1)}, u32[]{:S(2)}) copy-start(bf16[16,128,480]{1,2,0:T(8,128)(2,1)} %param.20) | copy-start | bytes 5898244
  4.8 9.4 %copy-start = (f32[8,32,960]{2,1,0:T(8,128)S(1)}, f32[8,32,960]{2,1,0:T(8,128)}, u32[]{:S(2)}) copy-start(f32[8,32,960]{2,1,0:T(8,128)} %param.16) | copy-start | bytes 2949124
  4.8 9.4 %copy-start.3 = (f32[8,32,480]{2,1,0:T(8,128)S(1)}, f32[8,32,480]{2,1,0:T(8,128)}, u32[]{:S(2)}) copy-start(f32[8,32,480]{2,1,0:T(8,128)} %param.15) | copy-start | bytes 1474564
  4.8 9.4 %copy-start.11 = (s32[16]{0:T(128)S(1)}, s32[16]{0:T(128)}, u32[]{:S(2)}) copy-start(s32[16]{0:T(128)} %col_ref.1) | copy-start | bytes 196
  4.8 9.4 %copy-start.12 = (s32[16]{0:T(128)S(1)}, s32[16]{0:T(128)}, u32[]{:S(2)}) copy-start(s32[16]{0:T(128)} %block_ref.3) | copy-start | bytes 196
  4.9 42.9 %all-to-all-start = ((bf16[32,152,128]{2,1,0:T(8,128)(2,1)}), bf16[32,152,128]{2,1,0:T(8,128)(2,1)}, u32[]{:S(2)}, u32[]{:S(2)}) async-start(bf16[32,152,128]{2,1,0:T(8,128)(2,1)} %pack.1), calls=%async_computation | async-start | bytes 2490368 | tf_op jit(solution)/shard_map/all_to_all | solution.py:429
  15.9 0.7 copy-start.5
  16.6 0.6 copy-start.9
  17.2 0.6 copy-start.10
  17.8 8.1 %collective-permute-start = (f32[64,128]{1,0:T(8,128)}, f32[64,128]{1,0:T(8,128)S(1)}, u32[]{:S(2)}, u32[]{:S(2)}) collective-permute-start(f32[64,128]{1,0:T(8,128)} %get-tuple-element.20), channel_id=1, source_target_pairs={{0,1},{1,0},{2,3},{3,2},{4,5},{5,4},{6,7},{7,6},{8,9},{9,8},{10,11... | collective-permute-start | bytes 98312 | tf_op jit(solution)/shard_map/ppermute | solution.py:446
  26.6 5.3 %collective-permute-start.2 = (f32[64,128]{1,0:T(8,128)S(1)}, f32[64,128]{1,0:T(8,128)S(1)}, u32[]{:S(2)}, u32[]{:S(2)}) collective-permute-start(f32[64,128]{1,0:T(8,128)S(1)} %pad_maximum_fusion), channel_id=1, source_target_pairs={{0,3},{1,2},{2,1},{3,0},{4,7},{5,6},{6,5},{7,4},{8,11},{9,10},{10,... | collective-permute-start | bytes 98312 | tf_op jit(solution)/shard_map/ppermute | solution.py:446
  26.6 1.2 %copy-start.2 = (bf16[2,128,2,960]{1,3,2,0:T(8,128)(2,1)S(1)}, bf16[2,128,2,960]{1,3,2,0:T(8,128)(2,1)}, u32[]{:S(2)}) copy-start(bf16[2,128,2,960]{1,3,2,0:T(8,128)(2,1)} %param.18) | copy-start | bytes 2949124
  27.8 0.9 %copy-start.4 = (s32[128,480]{0,1:T(8,128)S(1)}, s32[128,480]{0,1:T(8,128)}, u32[]{:S(2)}) copy-start(s32[128,480]{0,1:T(8,128)} %param.19) | copy-start | bytes 737284
  29.1 0.9 copy-start.13
  30.0 16.3 %collective-permute-start.1 = (bf16[2,256,512]{2,1,0:T(8,128)(2,1)S(1)}, bf16[2,256,512]{2,1,0:T(8,128)(2,1)S(1)}, u32[]{:S(2)}, u32[]{:S(2)}) collective-permute-start(bf16[2,256,512]{2,1,0:T(8,128)(2,1)S(1)} %get-tuple-element.23), channel_id=1, source_target_pairs={{0,16},{16,0},{1,17},{17,1},{2,18},{18,2},{3,19},{19,3},{4,20},{20... | collective-permute-start | bytes 1572872 | tf_op jit(solution)/shard_map/ppermute | solution.py:456
  31.9 6.4 %collective-permute-start.3 = (f32[64,128]{1,0:T(8,128)S(1)}, f32[64,128]{1,0:T(8,128)S(1)}, u32[]{:S(2)}, u32[]{:S(2)}) collective-permute-start(f32[64,128]{1,0:T(8,128)S(1)} %pad_maximum_fusion.1), channel_id=1, source_target_pairs={{0,7},{1,6},{2,5},{3,4},{4,3},{5,2},{6,1},{7,0},{8,15},{9,14},{10,... | collective-permute-start | bytes 98312 | tf_op jit(solution)/shard_map/ppermute | solution.py:446
  38.3 9.4 %copy-start.14 = (f32[64,128]{1,0:T(8,128)}, f32[64,128]{1,0:T(8,128)S(1)}, u32[]{:S(2)}) copy-start(f32[64,128]{1,0:T(8,128)S(1)} %pad_maximum_fusion.2.pay_hbm) | copy-start | bytes 98308
  38.3 8.0 %collective-permute-start.4 = (f32[64,128]{1,0:T(8,128)S(1)}, f32[64,128]{1,0:T(8,128)S(1)}, u32[]{:S(2)}, u32[]{:S(2)}) collective-permute-start(f32[64,128]{1,0:T(8,128)S(1)} %pad_maximum_fusion.2.pay_hbm), channel_id=1, source_target_pairs={{0,15},{1,14},{2,13},{3,12},{4,11},{5,10},{6,9},{7,8},{8,7},{9,6},... | collective-permute-start | bytes 98312 | tf_op jit(solution)/shard_map/ppermute | solution.py:446
  46.3 1.4 %copy-start.7 = (f32[64,128]{1,0:T(8,128)}, f32[64,128]{1,0:T(8,128)S(1)}, u32[]{:S(2)}) copy-start(f32[64,128]{1,0:T(8,128)S(1)} %collective-permute-done.4.got_hbm.got_d) | copy-start | bytes 98308
  46.3 1.4 %copy-start.15 = (bf16[2,256,512]{2,1,0:T(8,128)(2,1)}, bf16[2,256,512]{2,1,0:T(8,128)(2,1)S(1)}, u32[]{:S(2)}) copy-start(bf16[2,256,512]{2,1,0:T(8,128)(2,1)S(1)} %collective-permute-done.1.data_got_hbm) | copy-start | bytes 1572868
  47.8 34.6 %copy-start.6 = (f32[12,8,512]{2,1,0:T(8,128)S(1)}, f32[12,8,512]{2,1,0:T(8,128)}, u32[]{:S(2)}) copy-start(f32[12,8,512]{2,1,0:T(8,128)} %copy-done.5) | copy-start | bytes 589828
  69.4 19.2 %collective-permute-start.5 = (bf16[16,1024]{1,0:T(8,128)(2,1)S(1)}, bf16[16,1024]{1,0:T(8,128)(2,1)S(1)}, u32[]{:S(2)}, u32[]{:S(2)}) collective-permute-start(bf16[16,1024]{1,0:T(8,128)(2,1)S(1)} %get-tuple-element.27), channel_id=1, source_target_pairs={{0,0},{1,16},{2,32},{3,48},{4,64},{5,80},{6,96},{7,112},{8,128},{9... | collective-permute-start | bytes 98312 | tf_op jit(solution)/shard_map/ppermute | solution.py:487
  74.6 14.0 %collective-permute-start.6 = (bf16[16,1024]{1,0:T(8,128)(2,1)S(1)}, bf16[16,1024]{1,0:T(8,128)(2,1)S(1)}, u32[]{:S(2)}, u32[]{:S(2)}) collective-permute-start(bf16[16,1024]{1,0:T(8,128)(2,1)S(1)} %get-tuple-element.28), channel_id=1, source_target_pairs={{0,8},{1,24},{2,40},{3,56},{4,72},{5,88},{6,104},{7,120},{8,136},{... | collective-permute-start | bytes 98312 | tf_op jit(solution)/shard_map/ppermute | solution.py:490
  80.9 7.6 %collective-permute-start.7 = (bf16[8,1024]{1,0:T(8,128)(2,1)S(1)}, bf16[8,1024]{1,0:T(8,128)(2,1)S(1)}, u32[]{:S(2)}, u32[]{:S(2)}) collective-permute-start(bf16[8,1024]{1,0:T(8,128)(2,1)S(1)} %get-tuple-element.30), channel_id=1, source_target_pairs={{0,128},{128,0},{1,129},{129,1},{2,130},{130,2},{3,131},{131,3},{4... | collective-permute-start | bytes 49160 | tf_op jit(solution)/shard_map/ppermute | solution.py:493
  82.4 0.8 copy-start.8

commit v4 on v3

--- a/solution.py
+++ b/solution.py
@@ -42,10 +42,17 @@
     return jnp.asarray(table.reshape(ROW, ROW).astype(jnp.bfloat16))
 
 
-def z_table():
+def arrived(slab):
+    return slab % 4 * 4 + slab // 4
+
+
+def z_tables():
     real_part, imag_part = dft_parts(NZ)
     table = np.block([[real_part, -imag_part], [imag_part, real_part]])
-    return jnp.asarray(table.astype(jnp.bfloat16))
+    place = np.arange(NZ)
+    order = arrived(place // ZS) * ZS + place % ZS
+    order = np.concatenate([order, NZ + order])
+    return jnp.asarray(np.stack([table[:, order], table[order]]).astype(jnp.bfloat16))
 
 
 def call(kernel, out_shape, in_specs, scratch, flops, moved, name, out_spec=VMEM, grant=40):
@@ -61,34 +68,41 @@
     )
 
 
-def order_tables():
-    tables = []
-    for count in (2 * ZS, ZS):
-        rows = np.arange(NX * count)
-        place, q = rows // count, rows % count
-        table = np.zeros((NX * count, NX * count), np.float32)
-        table[rows, q * NX + 2 * (place % 16) + place // 16] = 1.0
-        tables.append(jnp.asarray(table.astype(jnp.bfloat16)))
-    return tables
-
-
-def pack_kernel(core_ref, sens_hbm, mr_hbm, order_hbm, short_hbm, out_hbm, sens_ref, mr_ref, order_ref,
-                short_ref, rows_ref, mr_rows, out_ref, sems, out_sems):
+def pack_kernel(core_ref, sens_hbm, mr_hbm, out_hbm, sens_ref, mr_ref, order_ref, short_ref, rows_ref,
+                mr_rows, out_ref, sems, out_sems):
     copies = []
     for n in range(4):
+        part = pl.ds(128 * n, 128)
+        copies.append(pltpu.make_async_copy(sens_hbm.at[part], sens_ref.at[part], sems.at[n]))
+    for n in range(4):
         part = pl.ds(64 * n, 64)
-        copies.append(pltpu.make_async_copy(mr_hbm.at[part], mr_ref.at[part], sems.at[n]))
-    for n in range(4):
-        part = pl.ds(128 * n, 128)
-        copies.append(pltpu.make_async_copy(sens_hbm.at[part], sens_ref.at[part], sems.at[4 + n]))
-    copies.append(pltpu.make_async_copy(order_hbm, order_ref, sems.at[8]))
-    copies.append(pltpu.make_async_copy(short_hbm, short_ref, sems.at[9]))
+        copies.append(pltpu.make_async_copy(mr_hbm.at[part], mr_ref.at[part], sems.at[4 + n]))
     for copy in copies:
         copy.start()
+    for count, ref in ((2 * ZS, order_ref), (ZS, short_ref)):
+        size = NX * count
+        row = lax.broadcasted_iota(jnp.int32, (size, size), 0)
+        col = lax.broadcasted_iota(jnp.int32, (size, size), 1)
+        place, q = row // count, row % count
+        source = q * NX + 2 * (place % 4 * 4 + place % 16 // 4) + place // 16
+        ref[...] = jnp.where(col == source, 1.0, 0.0).astype(bf16)
     imag = core_ref[0] == 1
     rows_ref[256:, HALF + NY :] = jnp.zeros((256, HALF - NY), bf16)
+    out_copies = []
+
+    def send(rows):
+        place = (slice(None), rows)
+        copy = pltpu.make_async_copy(out_ref.at[place], out_hbm.at[place], out_sems.at[len(out_copies)])
+        copy.start()
+        out_copies.append(copy)
+
     for n in range(4):
         copies[n].wait()
+        part = pl.ds(128 * n, 128)
+        rows_ref[part, :NY] = sens_ref[part, :NY]
+        rows_ref[part, HALF : HALF + NY] = sens_ref[part, NY:]
+    for n in range(4):
+        copies[4 + n].wait()
         part = pl.ds(64 * n, 64)
         values = jnp.where(imag, mr_ref[part, NY:], mr_ref[part, :NY]).astype(bf16)
         mr_rows[part, :] = values[:, :384]
@@ -96,30 +110,15 @@
         rows_ref[pl.ds(256 + 64 * n, 64), NY:HALF] = values[:, 416:448]
         rows_ref[part, HALF + NY :] = values[:, 448:]
     for n in range(4):
-        copies[4 + n].wait()
-        part = pl.ds(128 * n, 128)
-        rows_ref[part, :NY] = sens_ref[part, :NY]
-        rows_ref[part, HALF : HALF + NY] = sens_ref[part, NY:]
-    copies[8].wait()
-    copies[9].wait()
-    out_copies = []
-
-    def send(rows):
-        place = (slice(None), rows)
-        copy = pltpu.make_async_copy(out_ref.at[place], out_hbm.at[place], out_sems.at[len(out_copies)])
-        copy.start()
-        out_copies.append(copy)
-
-    moved = jnp.dot(short_ref[...], mr_rows[...], preferred_element_type=f32)
-    blocks = [moved[:, 128 * b : 128 * (b + 1)].reshape(NX, ZS, 128) for b in range(3)]
-    out_ref[:, 128:, :] = jnp.concatenate(blocks, 1).astype(bf16)
-    for n in range(4):
         moved = jnp.dot(order_ref[...], rows_ref[:, 256 * n : 256 * (n + 1)], preferred_element_type=f32)
         for b in range(2):
             first = 16 * (2 * n + b)
             block = moved[:, 128 * b : 128 * (b + 1)].astype(bf16)
             out_ref[:, first : first + 16, :] = block.reshape(NX, 16, 128)
         send(pl.ds(32 * n, 32))
+    moved = jnp.dot(short_ref[...], mr_rows[...], preferred_element_type=f32)
+    blocks = [moved[:, 128 * b : 128 * (b + 1)].reshape(NX, ZS, 128) for b in range(3)]
+    out_ref[:, 128:, :] = jnp.concatenate(blocks, 1).astype(bf16)
     send(pl.ds(128, CHUNK - 128))
     for copy in out_copies:
         copy.wait()
@@ -334,21 +333,25 @@
     for copy in others:
         copy.wait()
     mask = mask_ref[:NZ, :].astype(f32)
-    ztab = ztab_ref[...]
     for q in range(4):
         rows = pl.ds(q * NZ, NZ)
         volume = jnp.concatenate([kyrows[rows, :HALF], kyrows[rows, HALF:]], 0)
-        kspace = jnp.dot(ztab, volume, preferred_element_type=f32)
+        kspace = jnp.dot(ztab_ref[0], volume, preferred_element_type=f32)
         data = data_ref[q // 2, q % 2].astype(f32)
         misfit = jnp.concatenate(
             [mask * (kspace[:NZ] - data[:NZ]), mask * (data[NZ:] - kspace[NZ:])], 0
         ).astype(bf16)
-        back = jnp.dot(ztab, misfit, preferred_element_type=f32).astype(bf16)
+        back = jnp.dot(ztab_ref[1], misfit, preferred_element_type=f32).astype(bf16)
         images[rows, :HALF] = back[:NZ]
         images[rows, HALF:] = back[NZ:]
     for copy in tiles:
         copy.wait()
     backproject(col_ref, ratio_now, tiles_ref, acc, out_ref)
+    out_copies = []
+    for n in (1, 0):
+        part = (slice(None), pl.ds(2 * ZS * n, 2 * ZS))
+        out_copies.append(pltpu.make_async_copy(out_ref.at[part], out_hbm.at[part], out_sems.at[n]))
+    out_copies[0].start()
     for b in range(4):
         lanes = slice(128 * b, 128 * (b + 1))
         lanes_im = slice(HALF + 128 * b, HALF + 128 * (b + 1))
@@ -363,13 +366,11 @@
             total_re = total_re + (s_re * i_re - s_im * i_im)
             total_im = total_im - (s_re * i_im + s_im * i_re)
         for total, place in ((total_re, lanes), (total_im, lanes_im)):
-            slabs = total.reshape(2, 8, ZS, 128)
-            out_ref[:, : 2 * ZS, place] = jnp.concatenate([slabs[0], slabs[1]], 1).astype(bf16)
-    out_copies = []
-    for n in range(2):
-        part = pl.ds(4 * n, 4)
-        out_copies.append(pltpu.make_async_copy(out_ref.at[part], out_hbm.at[part], out_sems.at[n]))
-        out_copies[-1].start()
+            slabs = total.reshape(16, ZS, 128)
+            for p in range(8):
+                both = jnp.concatenate([slabs[arrived(p)], slabs[arrived(p + 8)]], 0)
+                out_ref[p, : 2 * ZS, place] = both.astype(bf16)
+    out_copies[1].start()
     for copy in out_copies:
         copy.wait()
 
@@ -418,15 +419,15 @@
     tiles = system_tiles.swapaxes(1, 2)
 
     sent = call(
-        pack_kernel, sds((32, CHUNK, 128), bf16), [SMEM] + [ANY] * 4,
+        pack_kernel, sds((32, CHUNK, 128), bf16), [SMEM] + [ANY] * 2,
         [pltpu.VMEM((2 * ZS * NX, 2 * NY), bf16), pltpu.VMEM((ZS * NX, 2 * NY), f32),
          pltpu.VMEM((512, 512), bf16), pltpu.VMEM((256, 256), bf16), pltpu.VMEM((512, ROW), bf16),
          pltpu.VMEM((256, 384), bf16), pltpu.VMEM((32, CHUNK, 128), bf16),
-         pltpu.SemaphoreType.DMA((10,)), pltpu.SemaphoreType.DMA((5,))],
-        10**6, 4 * 10**6, "pack", ANY, 60,
-    )(core_arr, coil_sens.reshape(2 * ZS * NX, 2 * NY), mr_rows, *order_tables())
+         pltpu.SemaphoreType.DMA((8,)), pltpu.SemaphoreType.DMA((5,))],
+        10**9, 4 * 10**6, "pack", ANY, 60,
+    )(core_arr, coil_sens.reshape(2 * ZS * NX, 2 * NY), mr_rows)
     sent, tile_col = lax.optimization_barrier((sent, tile_col))
-    recv = lax.all_to_all(sent, ("c",) + GZ, split_axis=0, concat_axis=0, tiled=True)
+    recv = lax.all_to_all(sent, ("c", "y", "zl"), split_axis=0, concat_axis=0, tiled=True)
 
     xs = jnp.clip(2 * grp - 1 + jnp.arange(4, dtype=jnp.int32), 0, NX - 1)
     bits = [(gz >> t) & 1 for t in range(4)]
@@ -465,7 +466,7 @@
     parts = call(
         coil_kernel, sds((8, 4 * ZS, ROW), bf16), [SMEM] * 4 + [ANY] * 10,
         [pltpu.VMEM((32, CHUNK, 128), bf16), pltpu.VMEM((ROW, ROW), bf16),
-         pltpu.VMEM((2 * NZ, 2 * NZ), bf16), pltpu.VMEM((2, 2, 2 * NZ, HALF), bf16),
+         pltpu.VMEM((2, 2 * NZ, 2 * NZ), bf16), pltpu.VMEM((2, 2, 2 * NZ, HALF), bf16),
          pltpu.VMEM((2 * NZ, HALF), bf16), pltpu.VMEM((16, NY, 128), bf16),
          pltpu.VMEM((2, 64, 128), f32), pltpu.VMEM((2, 64, 128), f32),
          pltpu.VMEM((16, 128), f32), pltpu.VMEM((16, 128), f32), pltpu.VMEM((4, ZS * NX, 128), f32),
@@ -473,7 +474,7 @@
          pltpu.VMEM((4 * NZ, ROW), bf16), pltpu.VMEM((8, 4 * ZS, ROW), bf16),
          pltpu.SemaphoreType.DMA((20,)), pltpu.SemaphoreType.DMA((2,))],
         5 * 10**9, 6 * 10**6, "coils", ANY, 61,
-    )(core_arr, tile_col, tile_subset_block, subset_view_blocks, recv, y_table(), z_table(), data_own,
+    )(core_arr, tile_col, tile_subset_block, subset_view_blocks, recv, y_table(), z_tables(), data_own,
       data_got, tiles, pay, got[3], measured, background)
 
     both = lax.all_to_all(parts, ("x", "c"), split_axis=0, concat_axis=0, tiled=True)

time: 89.8 us -> 88.6 us (0.987); the launches traced: 89.3 us -> 87 us
  other arithmetic: 1.49 us -> 0.05 us
  starting transfers between devices: 31.8 us -> 33.1 us
  local copies, waits for them, and re-layouts: 5.79 us -> 4.66 us
  Pallas kernels: 16.5 us -> 15.5 us
    ppermute x1, starting transfers between devices: 5.23 us -> 7.24 us  [on_device(): lax.ppermute(mr_own, GRP + GZ, [((zh * 8 + p) * 16 + j, j * 16 + zh * 8 +...]
    ppermute x1, starting transfers between devices: 6.32 us -> 4.31 us  [on_device(): lax.ppermute(mr_other, GRP + GZ, [((zh * 8 + p) * 16 + j, j * 16 + (1 - z...]
    ppermute x4, starting transfers between devices: 9.65 us -> 10.9 us  [on_device(): lax.ppermute(pay, GZ, [(i, i ^ 2 ** (step + 1) - 1) for i in range(16)])]
    unnamed x32 -> x28, local copies, waits for them, and re-layouts: 5.7 us -> 4.58 us
  transfers between devices with their start and end apart: 9 -> 9, of which waited for: 6 -> 6; matrix products, arithmetic and copies ran while one was open for 2% -> 0% of each run, Pallas kernels for 3% -> 3%
where the time goes in v4:
time: 88.6 us; the launch traced here: 87 us
  starting transfers between devices  33.1 us (37%)
  waiting for transfers between devices  19.6 us (22%)
  Pallas kernels  15.5 us (17%)
  blocking collectives  13.1 us (15%)
  local copies, waits for them, and re-layouts  4.66 us (5%)
    ppermute x4, waiting for transfers between devices, on_device(): lax.ppermute(pay, GZ, [(i, i ^ 2 ** (step + 1) - 1) for i in range(16)])  13.8 us
    all_to_all x1, blocking collectives, on_device(): lax.all_to_all(parts, ('x', 'c'), split_axis=0, concat_axis=0, tiled=True)  13.1 us
    ppermute x4, starting transfers between devices, on_device(): lax.ppermute(pay, GZ, [(i, i ^ 2 ** (step + 1) - 1) for i in range(16)])  10.9 us
    all_to_all x1, starting transfers between devices, on_device(): lax.all_to_all(sent, ('c', 'y', 'zl'), split_axis=0, concat_axis=0, tiled...  9.18 us
    pallas_call x1, Pallas kernels, on_device(): call(coil_kernel, sds((8, 4 * ZS, ROW), bf16), [SMEM] * 4 + [ANY] * 10, [...  8.36 us
    ppermute x1, starting transfers between devices, on_device(): lax.ppermute(mr_own, GRP + GZ, [((zh * 8 + p) * 16 + j, j * 16 + zh * 8 +...  7.24 us
    unnamed x28, local copies, waits for them, and re-layouts  4.58 us
    ppermute x1, waiting for transfers between devices, on_device(): pet_got = lax.ppermute(pet_other, 'zh', [(0, 1), (1, 0)])  4.43 us
  transfers between devices with their start and end apart: 9, of which 6 were waited for; matrix products, arithmetic and copies ran while one was open for 0% of the time, Pallas kernels for 3%

profile of v4, /device:TPU:6, one launch (start us, length us, event | category | flops | bytes accessed | tf_op | source)
XLA Modules:
  0.0 87.0 jit_solution(13349044915825065210)
XLA Ops:
  0.6 0.0 copy-start.1
  0.6 3.8 %pack.1 = bf16[32,152,128]{2,1,0:T(8,128)(2,1)} custom-call(s32[1]{0:T(128)} %bitcast.1.core_ref, bf16[512,960]{1,0:T(8,128)(2,1)} %bitcast.23, f32[256,960]{1,0:T(8,128)} %bitcast.18), custom_call_target="tpu_custom_call" | custom-call | flops 1000000000 | bytes 4000000 | tf_op jit(solution)/shard_map/pack/pallas_call | solution.py:421
  4.5 0.0 copy-start
  4.5 0.0 copy-start.9
  4.5 0.0 copy-start.10
  4.5 0.0 copy-start.4
  4.5 9.2 %all-to-all-start = ((bf16[32,152,128]{2,1,0:T(8,128)(2,1)}), bf16[32,152,128]{2,1,0:T(8,128)(2,1)}, u32[]{:S(2)}, u32[]{:S(2)}) async-start(bf16[32,152,128]{2,1,0:T(8,128)(2,1)} %pack.1), calls=%async_computation | async-start | bytes 2490368 | tf_op jit(solution)/shard_map/all_to_all | solution.py:430
  13.8 0.1 stack.35.info_ref
  13.9 0.0 copy-done.1
  13.9 0.0 copy-done
  13.9 0.0 copy-done.9
  13.9 0.0 copy-done.10
  13.9 0.0 copy-start.3
  13.9 1.0 %copy-done.3 = f32[8,32,480]{2,1,0:T(8,128)S(1)} copy-done((f32[8,32,480]{2,1,0:T(8,128)S(1)}, f32[8,32,480]{2,1,0:T(8,128)}, u32[]{:S(2)}) %copy-start.3) | copy-done | bytes 491544
  15.0 1.1 %project.1 = (f32[64,128]{1,0:T(8,128)S(1)}, f32[12,8,512]{2,1,0:T(8,128)S(1)}, f32[48,128]{1,0:T(8,128)S(1)}, f32[48,128]{1,0:T(8,128)S(1)}) custom-call(s32[8]{0:T(128)S(1)} %stack.35.info_ref, s32[16]{0:T(128)S(1)} %copy-done.9, s32[16]{0:T(128)S(1)} %copy-done.10, s32[4]{0:T(128)S(1)} %add_clamp_fusion.xs_ref, f32[256,480]{1,0:T(8,128)S(1)} %bitcast.21, ...), custom_call_target="tpu_custom_call" | custom-call | flops 10000000 | bytes 4000000 | tf_op jit(solution)/shard_map/project/pallas_call | solution.py:439
  16.1 0.0 copy-start.5
  16.1 0.7 copy-done.5
  16.7 1.7 %collective-permute-start = (f32[64,128]{1,0:T(8,128)S(1)}, f32[64,128]{1,0:T(8,128)S(1)}, u32[]{:S(2)}, u32[]{:S(2)}) collective-permute-start(f32[64,128]{1,0:T(8,128)S(1)} %get-tuple-element.20), channel_id=1, source_target_pairs={{0,1},{1,0},{2,3},{3,2},{4,5},{5,4},{6,7},{7,6},{8,9},{9,8},{10,11... | collective-permute-start | bytes 98312 | tf_op jit(solution)/shard_map/ppermute | solution.py:447
  18.5 5.3 %collective-permute-done.got_a = f32[64,128]{1,0:T(8,128)S(1)} collective-permute-done((f32[64,128]{1,0:T(8,128)S(1)}, f32[64,128]{1,0:T(8,128)S(1)}, u32[]{:S(2)}, u32[]{:S(2)}) %collective-permute-start) | collective-permute-done | bytes 32800 | tf_op jit(solution)/shard_map/ppermute | solution.py:447
  23.8 2.0 %collective-permute-start.2 = (f32[64,128]{1,0:T(8,128)S(1)}, f32[64,128]{1,0:T(8,128)S(1)}, u32[]{:S(2)}, u32[]{:S(2)}) collective-permute-start(f32[64,128]{1,0:T(8,128)S(1)} %pad_maximum_fusion), channel_id=1, source_target_pairs={{0,3},{1,2},{2,1},{3,0},{4,7},{5,6},{6,5},{7,4},{8,11},{9,10},{10,... | collective-permute-start | bytes 98312 | tf_op jit(solution)/shard_map/ppermute | solution.py:447
  25.8 0.0 copy-done.4
  25.8 1.2 %copy-done.2 = bf16[2,128,2,960]{1,3,2,0:T(8,128)(2,1)S(1)} copy-done((bf16[2,128,2,960]{1,3,2,0:T(8,128)(2,1)S(1)}, bf16[2,128,2,960]{1,3,2,0:T(8,128)(2,1)}, u32[]{:S(2)}) %copy-start.2) | copy-done | bytes 983064
  27.0 0.4 prepare.1
  27.4 0.0 copy-start.11
  27.4 0.9 %copy-done.11 = bf16[3,256,512]{2,1,0:T(8,128)(2,1)} copy-done((bf16[3,256,512]{2,1,0:T(8,128)(2,1)}, bf16[3,256,512]{2,1,0:T(8,128)(2,1)S(1)}, u32[]{:S(2)}) %copy-start.11) | copy-done | bytes 786456
  28.3 0.0 collective-permute-start.1
  28.3 1.3 %collective-permute-done.2.got_b = f32[64,128]{1,0:T(8,128)S(1)} collective-permute-done((f32[64,128]{1,0:T(8,128)S(1)}, f32[64,128]{1,0:T(8,128)S(1)}, u32[]{:S(2)}, u32[]{:S(2)}) %collective-permute-start.2) | collective-permute-done | bytes 32800 | tf_op jit(solution)/shard_map/ppermute | solution.py:447
  29.6 1.4 %collective-permute-start.3 = (f32[64,128]{1,0:T(8,128)S(1)}, f32[64,128]{1,0:T(8,128)S(1)}, u32[]{:S(2)}, u32[]{:S(2)}) collective-permute-start(f32[64,128]{1,0:T(8,128)S(1)} %pad_maximum_fusion.1), channel_id=1, source_target_pairs={{0,7},{1,6},{2,5},{3,4},{4,3},{5,2},{6,1},{7,0},{8,15},{9,14},{10,... | collective-permute-start | bytes 98312 | tf_op jit(solution)/shard_map/ppermute | solution.py:447
  31.0 5.0 %collective-permute-done.3.got_c = f32[64,128]{1,0:T(8,128)S(1)} collective-permute-done((f32[64,128]{1,0:T(8,128)S(1)}, f32[64,128]{1,0:T(8,128)S(1)}, u32[]{:S(2)}, u32[]{:S(2)}) %collective-permute-start.3) | collective-permute-done | bytes 32800 | tf_op jit(solution)/shard_map/ppermute | solution.py:447
  36.0 5.9 %collective-permute-start.4 = (f32[64,128]{1,0:T(8,128)S(1)}, f32[64,128]{1,0:T(8,128)S(1)}, u32[]{:S(2)}, u32[]{:S(2)}) collective-permute-start(f32[64,128]{1,0:T(8,128)S(1)} %pad_maximum_fusion.2.pay_hbm), channel_id=1, source_target_pairs={{0,15},{1,14},{2,13},{3,12},{4,11},{5,10},{6,9},{7,8},{8,7},{9,6},... | collective-permute-start | bytes 98312 | tf_op jit(solution)/shard_map/ppermute | solution.py:447
  41.9 2.1 %collective-permute-done.4.got_hbm.got_d = f32[64,128]{1,0:T(8,128)S(1)} collective-permute-done((f32[64,128]{1,0:T(8,128)S(1)}, f32[64,128]{1,0:T(8,128)S(1)}, u32[]{:S(2)}, u32[]{:S(2)}) %collective-permute-start.4) | collective-permute-done | bytes 32800 | tf_op jit(solution)/shard_map/ppermute | solution.py:447
  44.0 0.0 collective-permute-done.1.data_got_hbm
  44.0 1.4 %all-to-all-done.recv_hbm = bf16[32,152,128]{2,1,0:T(8,128)(2,1)} async-done(((bf16[32,152,128]{2,1,0:T(8,128)(2,1)}), bf16[32,152,128]{2,1,0:T(8,128)(2,1)}, u32[]{:S(2)}, u32[]{:S(2)}) %all-to-all-start) | async-done | bytes 1245216 | tf_op jit(solution)/shard_map/all_to_all | solution.py:430
  45.4 0.0 copy-done.12
  45.4 0.0 copy-done.7
  45.5 8.4 %coils.1 = bf16[8,32,1024]{2,1,0:T(8,128)(2,1)} custom-call(s32[1]{0:T(128)} %bitcast.1.core_ref, s32[16]{0:T(128)} %col_ref.1, s32[16]{0:T(128)} %block_ref.3, s32[16]{0:T(128)} %view_ref.1, bf16[32,152,128]{2,1,0:T(8,128)(2,1)} %all-to-all-done.recv_hbm, bf16[1024,1024]{1,0:T(8,128)(2,1)} %constant.43.clone.ytab_hbm, ...), custom_call_target="tpu_custom_call" | custom-call | flops 5000000000 | bytes 6000000 | tf_op jit(solution)/shard_map/coils/pallas_call | solution.py:466
  53.8 13.1 %all_to_all.10.recv_ref = bf16[8,32,1024]{2,1,0:T(8,128)(2,1)S(1)} all-to-all(bf16[8,32,1024]{2,1,0:T(8,128)(2,1)} %coils.1), channel_id=1, replica_groups=mesh['zh'=2,'x'=4,'c'=2,'zl'=4,'y'=4] {'x','c'}, dimensions={0} | all-to-all | bytes 1048576 | tf_op jit(solution)/shard_map/all_to_all | solution.py:480
  66.9 0.1 sums.1
  67.0 7.2 %collective-permute-start.5 = (bf16[16,1024]{1,0:T(8,128)(2,1)S(1)}, bf16[16,1024]{1,0:T(8,128)(2,1)S(1)}, u32[]{:S(2)}, u32[]{:S(2)}) collective-permute-start(bf16[16,1024]{1,0:T(8,128)(2,1)S(1)} %get-tuple-element.27), channel_id=1, source_target_pairs={{0,0},{1,16},{2,32},{3,48},{4,64},{5,80},{6,96},{7,112},{8,128},{9... | collective-permute-start | bytes 98312 | tf_op jit(solution)/shard_map/ppermute | solution.py:488
  74.3 4.3 %collective-permute-start.6 = (bf16[16,1024]{1,0:T(8,128)(2,1)S(1)}, bf16[16,1024]{1,0:T(8,128)(2,1)S(1)}, u32[]{:S(2)}, u32[]{:S(2)}) collective-permute-start(bf16[16,1024]{1,0:T(8,128)(2,1)S(1)} %get-tuple-element.28), channel_id=1, source_target_pairs={{0,8},{1,24},{2,40},{3,56},{4,72},{5,88},{6,104},{7,120},{8,136},{... | collective-permute-start | bytes 98312 | tf_op jit(solution)/shard_map/ppermute | solution.py:491
  78.6 1.4 %collective-permute-start.7 = (bf16[8,1024]{1,0:T(8,128)(2,1)S(1)}, bf16[8,1024]{1,0:T(8,128)(2,1)S(1)}, u32[]{:S(2)}, u32[]{:S(2)}) collective-permute-start(bf16[8,1024]{1,0:T(8,128)(2,1)S(1)} %get-tuple-element.30), channel_id=1, source_target_pairs={{0,128},{128,0},{1,129},{129,1},{2,130},{130,2},{3,131},{131,3},{4... | collective-permute-start | bytes 49160 | tf_op jit(solution)/shard_map/ppermute | solution.py:494
  80.0 0.0 copy-done.6
  80.0 0.8 copy-done.8
  80.8 1.0 %coupling.1 = (f32[2,8,512]{2,1,0:T(8,128)S(1)}, f32[2,8,1024]{2,1,0:T(8,128)S(1)}) custom-call(s32[8]{0:T(128)S(1)} %stack.35.info_ref, f32[12,8,512]{2,1,0:T(8,128)S(1)} %copy-done.6, f32[64,128]{1,0:T(8,128)S(1)} %collective-permute-done.got_a, f32[64,128]{1,0:T(8,128)S(1)} %collective-permute-done.2.got_b, f32[64,128]{1,0:T(8,128)S(1)} %collective-permute-done.3.got_c, ...), custom_call_target="tpu_custom_call" | custom-call | flops 1000000 | bytes 1000000 | tf_op jit(solution)/shard_map/coupling/pallas_call | solution.py:458
  81.8 4.4 %collective-permute-done.7.pet_b = bf16[8,1024]{1,0:T(8,128)(2,1)S(1)} collective-permute-done((bf16[8,1024]{1,0:T(8,128)(2,1)S(1)}, bf16[8,1024]{1,0:T(8,128)(2,1)S(1)}, u32[]{:S(2)}, u32[]{:S(2)}) %collective-permute-start.7) | collective-permute-done | bytes 16416 | tf_op jit(solution)/shard_map/ppermute | solution.py:494
  86.2 0.0 collective-permute-done.5.mr_a
  86.2 0.0 collective-permute-done.6.mr_b
  86.2 0.7 final.1
  (15 shorter events, 0.1 us)
Async XLA Ops:
  0.6 13.2 %copy-start.1 = (f32[8,32,960]{2,1,0:T(8,128)S(1)}, f32[8,32,960]{2,1,0:T(8,128)}, u32[]{:S(2)}) copy-start(f32[8,32,960]{2,1,0:T(8,128)} %param.14) | copy-start | bytes 2949124
  4.5 9.4 %copy-start = (bf16[16,128,480]{1,2,0:T(8,128)(2,1)S(1)}, bf16[16,128,480]{1,2,0:T(8,128)(2,1)}, u32[]{:S(2)}) copy-start(bf16[16,128,480]{1,2,0:T(8,128)(2,1)} %param.18) | copy-start | bytes 5898244
  4.5 9.4 %copy-start.9 = (s32[16]{0:T(128)S(1)}, s32[16]{0:T(128)}, u32[]{:S(2)}) copy-start(s32[16]{0:T(128)} %col_ref.1) | copy-start | bytes 196
  4.5 9.4 %copy-start.10 = (s32[16]{0:T(128)S(1)}, s32[16]{0:T(128)}, u32[]{:S(2)}) copy-start(s32[16]{0:T(128)} %block_ref.3) | copy-start | bytes 196
  4.5 21.3 %copy-start.4 = (s32[128,480]{0,1:T(8,128)S(1)}, s32[128,480]{0,1:T(8,128)}, u32[]{:S(2)}) copy-start(s32[128,480]{0,1:T(8,128)} %param.17) | copy-start | bytes 737284
  4.5 40.9 %all-to-all-start = ((bf16[32,152,128]{2,1,0:T(8,128)(2,1)}), bf16[32,152,128]{2,1,0:T(8,128)(2,1)}, u32[]{:S(2)}, u32[]{:S(2)}) async-start(bf16[32,152,128]{2,1,0:T(8,128)(2,1)} %pack.1), calls=%async_computation | async-start | bytes 2490368 | tf_op jit(solution)/shard_map/all_to_all | solution.py:430
  13.9 1.0 %copy-start.3 = (f32[8,32,480]{2,1,0:T(8,128)S(1)}, f32[8,32,480]{2,1,0:T(8,128)}, u32[]{:S(2)}) copy-start(f32[8,32,480]{2,1,0:T(8,128)} %param.13) | copy-start | bytes 1474564
  16.1 0.7 copy-start.5
  16.7 7.1 %collective-permute-start = (f32[64,128]{1,0:T(8,128)S(1)}, f32[64,128]{1,0:T(8,128)S(1)}, u32[]{:S(2)}, u32[]{:S(2)}) collective-permute-start(f32[64,128]{1,0:T(8,128)S(1)} %get-tuple-element.20), channel_id=1, source_target_pairs={{0,1},{1,0},{2,3},{3,2},{4,5},{5,4},{6,7},{7,6},{8,9},{9,8},{10,11... | collective-permute-start | bytes 98312 | tf_op jit(solution)/shard_map/ppermute | solution.py:447
  23.8 5.8 %collective-permute-start.2 = (f32[64,128]{1,0:T(8,128)S(1)}, f32[64,128]{1,0:T(8,128)S(1)}, u32[]{:S(2)}, u32[]{:S(2)}) collective-permute-start(f32[64,128]{1,0:T(8,128)S(1)} %pad_maximum_fusion), channel_id=1, source_target_pairs={{0,3},{1,2},{2,1},{3,0},{4,7},{5,6},{6,5},{7,4},{8,11},{9,10},{10,... | collective-permute-start | bytes 98312 | tf_op jit(solution)/shard_map/ppermute | solution.py:447
  25.8 1.2 %copy-start.2 = (bf16[2,128,2,960]{1,3,2,0:T(8,128)(2,1)S(1)}, bf16[2,128,2,960]{1,3,2,0:T(8,128)(2,1)}, u32[]{:S(2)}) copy-start(bf16[2,128,2,960]{1,3,2,0:T(8,128)(2,1)} %param.16) | copy-start | bytes 2949124
  27.4 0.9 %copy-start.11 = (bf16[3,256,512]{2,1,0:T(8,128)(2,1)}, bf16[3,256,512]{2,1,0:T(8,128)(2,1)S(1)}, u32[]{:S(2)}) copy-start(bf16[3,256,512]{2,1,0:T(8,128)(2,1)S(1)} %get-tuple-element.22.data_own_hbm) | copy-start | bytes 2359300
  28.3 15.7 %collective-permute-start.1 = (bf16[2,256,512]{2,1,0:T(8,128)(2,1)S(1)}, bf16[2,256,512]{2,1,0:T(8,128)(2,1)S(1)}, u32[]{:S(2)}, u32[]{:S(2)}) collective-permute-start(bf16[2,256,512]{2,1,0:T(8,128)(2,1)S(1)} %get-tuple-element.23), channel_id=1, source_target_pairs={{0,16},{16,0},{1,17},{17,1},{2,18},{18,2},{3,19},{19,3},{4,20},{20... | collective-permute-start | bytes 1572872 | tf_op jit(solution)/shard_map/ppermute | solution.py:457
  29.6 6.4 %collective-permute-start.3 = (f32[64,128]{1,0:T(8,128)S(1)}, f32[64,128]{1,0:T(8,128)S(1)}, u32[]{:S(2)}, u32[]{:S(2)}) collective-permute-start(f32[64,128]{1,0:T(8,128)S(1)} %pad_maximum_fusion.1), channel_id=1, source_target_pairs={{0,7},{1,6},{2,5},{3,4},{4,3},{5,2},{6,1},{7,0},{8,15},{9,14},{10,... | collective-permute-start | bytes 98312 | tf_op jit(solution)/shard_map/ppermute | solution.py:447
  36.0 9.4 %copy-start.12 = (f32[64,128]{1,0:T(8,128)}, f32[64,128]{1,0:T(8,128)S(1)}, u32[]{:S(2)}) copy-start(f32[64,128]{1,0:T(8,128)S(1)} %pad_maximum_fusion.2.pay_hbm) | copy-start | bytes 98308
  36.0 8.0 %collective-permute-start.4 = (f32[64,128]{1,0:T(8,128)S(1)}, f32[64,128]{1,0:T(8,128)S(1)}, u32[]{:S(2)}, u32[]{:S(2)}) collective-permute-start(f32[64,128]{1,0:T(8,128)S(1)} %pad_maximum_fusion.2.pay_hbm), channel_id=1, source_target_pairs={{0,15},{1,14},{2,13},{3,12},{4,11},{5,10},{6,9},{7,8},{8,7},{9,6},... | collective-permute-start | bytes 98312 | tf_op jit(solution)/shard_map/ppermute | solution.py:447
  44.0 1.4 %copy-start.7 = (f32[64,128]{1,0:T(8,128)}, f32[64,128]{1,0:T(8,128)S(1)}, u32[]{:S(2)}) copy-start(f32[64,128]{1,0:T(8,128)S(1)} %collective-permute-done.4.got_hbm.got_d) | copy-start | bytes 98308
  44.0 1.4 %copy-start.13 = (bf16[2,256,512]{2,1,0:T(8,128)(2,1)}, bf16[2,256,512]{2,1,0:T(8,128)(2,1)S(1)}, u32[]{:S(2)}) copy-start(bf16[2,256,512]{2,1,0:T(8,128)(2,1)S(1)} %collective-permute-done.1.data_got_hbm) | copy-start | bytes 1572868
  45.4 34.6 %copy-start.6 = (f32[12,8,512]{2,1,0:T(8,128)S(1)}, f32[12,8,512]{2,1,0:T(8,128)}, u32[]{:S(2)}) copy-start(f32[12,8,512]{2,1,0:T(8,128)} %copy-done.5) | copy-start | bytes 589828
  67.0 19.2 %collective-permute-start.5 = (bf16[16,1024]{1,0:T(8,128)(2,1)S(1)}, bf16[16,1024]{1,0:T(8,128)(2,1)S(1)}, u32[]{:S(2)}, u32[]{:S(2)}) collective-permute-start(bf16[16,1024]{1,0:T(8,128)(2,1)S(1)} %get-tuple-element.27), channel_id=1, source_target_pairs={{0,0},{1,16},{2,32},{3,48},{4,64},{5,80},{6,96},{7,112},{8,128},{9... | collective-permute-start | bytes 98312 | tf_op jit(solution)/shard_map/ppermute | solution.py:488
  74.3 12.0 %collective-permute-start.6 = (bf16[16,1024]{1,0:T(8,128)(2,1)S(1)}, bf16[16,1024]{1,0:T(8,128)(2,1)S(1)}, u32[]{:S(2)}, u32[]{:S(2)}) collective-permute-start(bf16[16,1024]{1,0:T(8,128)(2,1)S(1)} %get-tuple-element.28), channel_id=1, source_target_pairs={{0,8},{1,24},{2,40},{3,56},{4,72},{5,88},{6,104},{7,120},{8,136},{... | collective-permute-start | bytes 98312 | tf_op jit(solution)/shard_map/ppermute | solution.py:491
  78.6 7.6 %collective-permute-start.7 = (bf16[8,1024]{1,0:T(8,128)(2,1)S(1)}, bf16[8,1024]{1,0:T(8,128)(2,1)S(1)}, u32[]{:S(2)}, u32[]{:S(2)}) collective-permute-start(bf16[8,1024]{1,0:T(8,128)(2,1)S(1)} %get-tuple-element.30), channel_id=1, source_target_pairs={{0,128},{128,0},{1,129},{129,1},{2,130},{130,2},{3,131},{131,3},{4... | collective-permute-start | bytes 49160 | tf_op jit(solution)/shard_map/ppermute | solution.py:494
  80.0 0.8 copy-start.8

commit v5 on v4

--- a/solution.py
+++ b/solution.py
@@ -368,7 +368,7 @@
         for total, place in ((total_re, lanes), (total_im, lanes_im)):
             slabs = total.reshape(16, ZS, 128)
             for p in range(8):
-                both = jnp.concatenate([slabs[arrived(p)], slabs[arrived(p + 8)]], 0)
+                both = jnp.concatenate([slabs[arrived(2 * p)], slabs[arrived(2 * p + 1)]], 0)
                 out_ref[p, : 2 * ZS, place] = both.astype(bf16)
     out_copies[1].start()
     for copy in out_copies:
@@ -486,10 +486,10 @@
     )(half, both)
     places = [(zh, p, j) for zh in range(2) for p in range(8) for j in range(16)]
     mr_a = lax.ppermute(
-        mr_own, GRP + GZ, [((zh * 8 + p) * 16 + j, j * 16 + zh * 8 + p) for zh, p, j in places]
+        mr_own, GRP + GZ, [((zh * 8 + p) * 16 + j, j * 16 + 2 * p + 1 * zh) for zh, p, j in places]
     )
     mr_b = lax.ppermute(
-        mr_other, GRP + GZ, [((zh * 8 + p) * 16 + j, j * 16 + (1 - zh) * 8 + p) for zh, p, j in places]
+        mr_other, GRP + GZ, [((zh * 8 + p) * 16 + j, j * 16 + 2 * p + 1 * (1 - zh)) for zh, p, j in places]
     )
     pet_got = lax.ppermute(pet_other, "zh", [(0, 1), (1, 0)])
     return call(

time: 88.6 us -> 88.1 us (level); the launches traced: 87 us -> 87.6 us
  waiting for transfers between devices: 19.6 us -> 22.2 us
  starting transfers between devices: 33.1 us -> 31.2 us
    ppermute x2, waiting for transfers between devices: 0.01 us -> 3.42 us  [the longest x1 3.41 us: on_device(): lax.ppermute(mr_other, GRP + GZ, [((zh * 8 + p) * 16 + j, j * 16 + 2 * p...]
    ppermute x2, starting transfers between devices: 11.6 us -> 8.77 us  [the longest x1 8.27 us: on_device(): lax.ppermute(mr_own, GRP + GZ, [((zh * 8 + p) * 16 + j, j * 16 + 2 * p +...]
  transfers between devices with their start and end apart: 9 -> 9, of which waited for: 6 -> 7; matrix products, arithmetic and copies ran while one was open for 0% -> 0% of each run, Pallas kernels for 3% -> 3%
where the time goes in v5:
time: 88.1 us; the launch traced here: 87.6 us
  starting transfers between devices  31.2 us (35%)
  waiting for transfers between devices  22.2 us (25%)
  Pallas kernels  15.5 us (18%)
  blocking collectives  13.1 us (15%)
  local copies, waits for them, and re-layouts  4.66 us (5%)
    ppermute x4, waiting for transfers between devices, on_device(): lax.ppermute(pay, GZ, [(i, i ^ 2 ** (step + 1) - 1) for i in range(16)])  13.8 us
    all_to_all x1, blocking collectives, on_device(): lax.all_to_all(parts, ('x', 'c'), split_axis=0, concat_axis=0, tiled=True)  13.1 us
    ppermute x4, starting transfers between devices, on_device(): lax.ppermute(pay, GZ, [(i, i ^ 2 ** (step + 1) - 1) for i in range(16)])  10.9 us
    all_to_all x1, starting transfers between devices, on_device(): lax.all_to_all(sent, ('c', 'y', 'zl'), split_axis=0, concat_axis=0, tiled...  9.18 us
    pallas_call x1, Pallas kernels, on_device(): call(coil_kernel, sds((8, 4 * ZS, ROW), bf16), [SMEM] * 4 + [ANY] * 10, [...  8.36 us
    ppermute x1, starting transfers between devices, on_device(): lax.ppermute(mr_own, GRP + GZ, [((zh * 8 + p) * 16 + j, j * 16 + 2 * p +...  8.27 us
    unnamed x28, local copies, waits for them, and re-layouts  4.58 us
    pallas_call x1, Pallas kernels, on_device(): call(pack_kernel, sds((32, CHUNK, 128), bf16), [SMEM] + [ANY] * 2, [pltpu...  3.85 us
  transfers between devices with their start and end apart: 9, of which 7 were waited for; matrix products, arithmetic and copies ran while one was open for 0% of the time, Pallas kernels for 3%

profile of v5, /device:TPU:6, one launch (start us, length us, event | category | flops | bytes accessed | tf_op | source)
XLA Modules:
  0.0 87.6 jit_solution(8805876857662209768)
XLA Ops:
  0.6 0.0 copy-start.1
  0.6 3.8 %pack.1 = bf16[32,152,128]{2,1,0:T(8,128)(2,1)} custom-call(s32[1]{0:T(128)} %bitcast.1.core_ref, bf16[512,960]{1,0:T(8,128)(2,1)} %bitcast.23, f32[256,960]{1,0:T(8,128)} %bitcast.18), custom_call_target="tpu_custom_call" | custom-call | flops 1000000000 | bytes 4000000 | tf_op jit(solution)/shard_map/pack/pallas_call | solution.py:421
  4.5 0.0 copy-start
  4.5 0.0 copy-start.9
  4.5 0.0 copy-start.10
  4.5 0.0 copy-start.4
  4.5 9.2 %all-to-all-start = ((bf16[32,152,128]{2,1,0:T(8,128)(2,1)}), bf16[32,152,128]{2,1,0:T(8,128)(2,1)}, u32[]{:S(2)}, u32[]{:S(2)}) async-start(bf16[32,152,128]{2,1,0:T(8,128)(2,1)} %pack.1), calls=%async_computation | async-start | bytes 2490368 | tf_op jit(solution)/shard_map/all_to_all | solution.py:430
  13.8 0.1 stack.35.info_ref
  13.9 0.0 copy-done.1
  13.9 0.0 copy-done
  13.9 0.0 copy-done.9
  13.9 0.0 copy-done.10
  13.9 0.0 copy-start.3
  13.9 1.0 %copy-done.3 = f32[8,32,480]{2,1,0:T(8,128)S(1)} copy-done((f32[8,32,480]{2,1,0:T(8,128)S(1)}, f32[8,32,480]{2,1,0:T(8,128)}, u32[]{:S(2)}) %copy-start.3) | copy-done | bytes 491544
  15.0 1.1 %project.1 = (f32[64,128]{1,0:T(8,128)S(1)}, f32[12,8,512]{2,1,0:T(8,128)S(1)}, f32[48,128]{1,0:T(8,128)S(1)}, f32[48,128]{1,0:T(8,128)S(1)}) custom-call(s32[8]{0:T(128)S(1)} %stack.35.info_ref, s32[16]{0:T(128)S(1)} %copy-done.9, s32[16]{0:T(128)S(1)} %copy-done.10, s32[4]{0:T(128)S(1)} %add_clamp_fusion.xs_ref, f32[256,480]{1,0:T(8,128)S(1)} %bitcast.21, ...), custom_call_target="tpu_custom_call" | custom-call | flops 10000000 | bytes 4000000 | tf_op jit(solution)/shard_map/project/pallas_call | solution.py:439
  16.1 0.0 copy-start.5
  16.1 0.7 copy-done.5
  16.7 1.7 %collective-permute-start = (f32[64,128]{1,0:T(8,128)S(1)}, f32[64,128]{1,0:T(8,128)S(1)}, u32[]{:S(2)}, u32[]{:S(2)}) collective-permute-start(f32[64,128]{1,0:T(8,128)S(1)} %get-tuple-element.20), channel_id=1, source_target_pairs={{0,1},{1,0},{2,3},{3,2},{4,5},{5,4},{6,7},{7,6},{8,9},{9,8},{10,11... | collective-permute-start | bytes 98312 | tf_op jit(solution)/shard_map/ppermute | solution.py:447
  18.5 5.3 %collective-permute-done.got_a = f32[64,128]{1,0:T(8,128)S(1)} collective-permute-done((f32[64,128]{1,0:T(8,128)S(1)}, f32[64,128]{1,0:T(8,128)S(1)}, u32[]{:S(2)}, u32[]{:S(2)}) %collective-permute-start) | collective-permute-done | bytes 32800 | tf_op jit(solution)/shard_map/ppermute | solution.py:447
  23.8 2.0 %collective-permute-start.2 = (f32[64,128]{1,0:T(8,128)S(1)}, f32[64,128]{1,0:T(8,128)S(1)}, u32[]{:S(2)}, u32[]{:S(2)}) collective-permute-start(f32[64,128]{1,0:T(8,128)S(1)} %pad_maximum_fusion), channel_id=1, source_target_pairs={{0,3},{1,2},{2,1},{3,0},{4,7},{5,6},{6,5},{7,4},{8,11},{9,10},{10,... | collective-permute-start | bytes 98312 | tf_op jit(solution)/shard_map/ppermute | solution.py:447
  25.8 0.0 copy-done.4
  25.8 1.2 %copy-done.2 = bf16[2,128,2,960]{1,3,2,0:T(8,128)(2,1)S(1)} copy-done((bf16[2,128,2,960]{1,3,2,0:T(8,128)(2,1)S(1)}, bf16[2,128,2,960]{1,3,2,0:T(8,128)(2,1)}, u32[]{:S(2)}) %copy-start.2) | copy-done | bytes 983064
  27.0 0.4 prepare.1
  27.4 0.0 copy-start.11
  27.4 0.9 copy-done.11
  28.3 0.0 collective-permute-start.1
  28.3 1.3 %collective-permute-done.2.got_b = f32[64,128]{1,0:T(8,128)S(1)} collective-permute-done((f32[64,128]{1,0:T(8,128)S(1)}, f32[64,128]{1,0:T(8,128)S(1)}, u32[]{:S(2)}, u32[]{:S(2)}) %collective-permute-start.2) | collective-permute-done | bytes 32800 | tf_op jit(solution)/shard_map/ppermute | solution.py:447
  29.6 1.4 %collective-permute-start.3 = (f32[64,128]{1,0:T(8,128)S(1)}, f32[64,128]{1,0:T(8,128)S(1)}, u32[]{:S(2)}, u32[]{:S(2)}) collective-permute-start(f32[64,128]{1,0:T(8,128)S(1)} %pad_maximum_fusion.1), channel_id=1, source_target_pairs={{0,7},{1,6},{2,5},{3,4},{4,3},{5,2},{6,1},{7,0},{8,15},{9,14},{10,... | collective-permute-start | bytes 98312 | tf_op jit(solution)/shard_map/ppermute | solution.py:447
  31.0 5.0 %collective-permute-done.3.got_c = f32[64,128]{1,0:T(8,128)S(1)} collective-permute-done((f32[64,128]{1,0:T(8,128)S(1)}, f32[64,128]{1,0:T(8,128)S(1)}, u32[]{:S(2)}, u32[]{:S(2)}) %collective-permute-start.3) | collective-permute-done | bytes 32800 | tf_op jit(solution)/shard_map/ppermute | solution.py:447
  36.0 5.9 %collective-permute-start.4 = (f32[64,128]{1,0:T(8,128)S(1)}, f32[64,128]{1,0:T(8,128)S(1)}, u32[]{:S(2)}, u32[]{:S(2)}) collective-permute-start(f32[64,128]{1,0:T(8,128)S(1)} %pad_maximum_fusion.2.pay_hbm), channel_id=1, source_target_pairs={{0,15},{1,14},{2,13},{3,12},{4,11},{5,10},{6,9},{7,8},{8,7},{9,6},... | collective-permute-start | bytes 98312 | tf_op jit(solution)/shard_map/ppermute | solution.py:447
  41.9 2.1 %collective-permute-done.4.got_hbm.got_d = f32[64,128]{1,0:T(8,128)S(1)} collective-permute-done((f32[64,128]{1,0:T(8,128)S(1)}, f32[64,128]{1,0:T(8,128)S(1)}, u32[]{:S(2)}, u32[]{:S(2)}) %collective-permute-start.4) | collective-permute-done | bytes 32800 | tf_op jit(solution)/shard_map/ppermute | solution.py:447
  44.0 0.0 collective-permute-done.1.data_got_hbm
  44.0 1.4 %all-to-all-done.recv_hbm = bf16[32,152,128]{2,1,0:T(8,128)(2,1)} async-done(((bf16[32,152,128]{2,1,0:T(8,128)(2,1)}), bf16[32,152,128]{2,1,0:T(8,128)(2,1)}, u32[]{:S(2)}, u32[]{:S(2)}) %all-to-all-start) | async-done | bytes 1245216 | tf_op jit(solution)/shard_map/all_to_all | solution.py:430
  45.4 0.0 copy-done.12
  45.4 0.0 copy-done.7
  45.4 0.0 copy-done.13
  45.5 8.4 %coils.1 = bf16[8,32,1024]{2,1,0:T(8,128)(2,1)} custom-call(s32[1]{0:T(128)} %bitcast.1.core_ref, s32[16]{0:T(128)} %col_ref.1, s32[16]{0:T(128)} %block_ref.3, s32[16]{0:T(128)} %view_ref.1, bf16[32,152,128]{2,1,0:T(8,128)(2,1)} %all-to-all-done.recv_hbm, bf16[1024,1024]{1,0:T(8,128)(2,1)} %constant.43.clone.ytab_hbm, ...), custom_call_target="tpu_custom_call" | custom-call | flops 5000000000 | bytes 6000000 | tf_op jit(solution)/shard_map/coils/pallas_call | solution.py:466
  53.8 13.1 %all_to_all.10.recv_ref = bf16[8,32,1024]{2,1,0:T(8,128)(2,1)S(1)} all-to-all(bf16[8,32,1024]{2,1,0:T(8,128)(2,1)} %coils.1), channel_id=1, replica_groups=mesh['zh'=2,'x'=4,'c'=2,'zl'=4,'y'=4] {'x','c'}, dimensions={0} | all-to-all | bytes 1048576 | tf_op jit(solution)/shard_map/all_to_all | solution.py:480
  66.9 0.1 sums.1
  67.0 8.3 %collective-permute-start.5 = (bf16[16,1024]{1,0:T(8,128)(2,1)S(1)}, bf16[16,1024]{1,0:T(8,128)(2,1)S(1)}, u32[]{:S(2)}, u32[]{:S(2)}) collective-permute-start(bf16[16,1024]{1,0:T(8,128)(2,1)S(1)} %get-tuple-element.27), channel_id=1, source_target_pairs={{0,0},{1,16},{2,32},{3,48},{4,64},{5,80},{6,96},{7,112},{8,128},{9... | collective-permute-start | bytes 98312 | tf_op jit(solution)/shard_map/ppermute | solution.py:488
  75.3 0.5 collective-permute-start.6
  75.8 2.3 %collective-permute-start.7 = (bf16[8,1024]{1,0:T(8,128)(2,1)S(1)}, bf16[8,1024]{1,0:T(8,128)(2,1)S(1)}, u32[]{:S(2)}, u32[]{:S(2)}) collective-permute-start(bf16[8,1024]{1,0:T(8,128)(2,1)S(1)} %get-tuple-element.30), channel_id=1, source_target_pairs={{0,128},{128,0},{1,129},{129,1},{2,130},{130,2},{3,131},{131,3},{4... | collective-permute-start | bytes 49160 | tf_op jit(solution)/shard_map/ppermute | solution.py:494
  78.1 0.8 copy-done.8
  78.8 1.0 %coupling.1 = (f32[2,8,512]{2,1,0:T(8,128)S(1)}, f32[2,8,1024]{2,1,0:T(8,128)S(1)}) custom-call(s32[8]{0:T(128)S(1)} %stack.35.info_ref, f32[12,8,512]{2,1,0:T(8,128)S(1)} %copy-done.6, f32[64,128]{1,0:T(8,128)S(1)} %collective-permute-done.got_a, f32[64,128]{1,0:T(8,128)S(1)} %collective-permute-done.2.got_b, f32[64,128]{1,0:T(8,128)S(1)} %collective-permute-done.3.got_c, ...), custom_call_target="tpu_custom_call" | custom-call | flops 1000000 | bytes 1000000 | tf_op jit(solution)/shard_map/coupling/pallas_call | solution.py:458
  79.8 3.6 %collective-permute-done.7.pet_b = bf16[8,1024]{1,0:T(8,128)(2,1)S(1)} collective-permute-done((bf16[8,1024]{1,0:T(8,128)(2,1)S(1)}, bf16[8,1024]{1,0:T(8,128)(2,1)S(1)}, u32[]{:S(2)}, u32[]{:S(2)}) %collective-permute-start.7) | collective-permute-done | bytes 16416 | tf_op jit(solution)/shard_map/ppermute | solution.py:494
  83.4 0.0 collective-permute-done.5.mr_a
  83.5 3.4 %collective-permute-done.6.mr_b = bf16[16,1024]{1,0:T(8,128)(2,1)S(1)} collective-permute-done((bf16[16,1024]{1,0:T(8,128)(2,1)S(1)}, bf16[16,1024]{1,0:T(8,128)(2,1)S(1)}, u32[]{:S(2)}, u32[]{:S(2)}) %collective-permute-start.6) | collective-permute-done | bytes 32800 | tf_op jit(solution)/shard_map/ppermute | solution.py:491
  86.9 0.7 final.1
  (15 shorter events, 0.1 us)
Async XLA Ops:
  0.6 13.2 %copy-start.1 = (f32[8,32,960]{2,1,0:T(8,128)S(1)}, f32[8,32,960]{2,1,0:T(8,128)}, u32[]{:S(2)}) copy-start(f32[8,32,960]{2,1,0:T(8,128)} %param.14) | copy-start | bytes 2949124
  4.5 9.4 %copy-start = (bf16[16,128,480]{1,2,0:T(8,128)(2,1)S(1)}, bf16[16,128,480]{1,2,0:T(8,128)(2,1)}, u32[]{:S(2)}) copy-start(bf16[16,128,480]{1,2,0:T(8,128)(2,1)} %param.18) | copy-start | bytes 5898244
  4.5 9.4 %copy-start.9 = (s32[16]{0:T(128)S(1)}, s32[16]{0:T(128)}, u32[]{:S(2)}) copy-start(s32[16]{0:T(128)} %col_ref.1) | copy-start | bytes 196
  4.5 9.4 %copy-start.10 = (s32[16]{0:T(128)S(1)}, s32[16]{0:T(128)}, u32[]{:S(2)}) copy-start(s32[16]{0:T(128)} %block_ref.3) | copy-start | bytes 196
  4.5 21.3 %copy-start.4 = (s32[128,480]{0,1:T(8,128)S(1)}, s32[128,480]{0,1:T(8,128)}, u32[]{:S(2)}) copy-start(s32[128,480]{0,1:T(8,128)} %param.17) | copy-start | bytes 737284
  4.5 40.9 %all-to-all-start = ((bf16[32,152,128]{2,1,0:T(8,128)(2,1)}), bf16[32,152,128]{2,1,0:T(8,128)(2,1)}, u32[]{:S(2)}, u32[]{:S(2)}) async-start(bf16[32,152,128]{2,1,0:T(8,128)(2,1)} %pack.1), calls=%async_computation | async-start | bytes 2490368 | tf_op jit(solution)/shard_map/all_to_all | solution.py:430
  13.9 1.0 %copy-start.3 = (f32[8,32,480]{2,1,0:T(8,128)S(1)}, f32[8,32,480]{2,1,0:T(8,128)}, u32[]{:S(2)}) copy-start(f32[8,32,480]{2,1,0:T(8,128)} %param.13) | copy-start | bytes 1474564
  16.1 0.7 copy-start.5
  16.7 7.1 %collective-permute-start = (f32[64,128]{1,0:T(8,128)S(1)}, f32[64,128]{1,0:T(8,128)S(1)}, u32[]{:S(2)}, u32[]{:S(2)}) collective-permute-start(f32[64,128]{1,0:T(8,128)S(1)} %get-tuple-element.20), channel_id=1, source_target_pairs={{0,1},{1,0},{2,3},{3,2},{4,5},{5,4},{6,7},{7,6},{8,9},{9,8},{10,11... | collective-permute-start | bytes 98312 | tf_op jit(solution)/shard_map/ppermute | solution.py:447
  23.8 5.8 %collective-permute-start.2 = (f32[64,128]{1,0:T(8,128)S(1)}, f32[64,128]{1,0:T(8,128)S(1)}, u32[]{:S(2)}, u32[]{:S(2)}) collective-permute-start(f32[64,128]{1,0:T(8,128)S(1)} %pad_maximum_fusion), channel_id=1, source_target_pairs={{0,3},{1,2},{2,1},{3,0},{4,7},{5,6},{6,5},{7,4},{8,11},{9,10},{10,... | collective-permute-start | bytes 98312 | tf_op jit(solution)/shard_map/ppermute | solution.py:447
  25.8 1.2 %copy-start.2 = (bf16[2,128,2,960]{1,3,2,0:T(8,128)(2,1)S(1)}, bf16[2,128,2,960]{1,3,2,0:T(8,128)(2,1)}, u32[]{:S(2)}) copy-start(bf16[2,128,2,960]{1,3,2,0:T(8,128)(2,1)} %param.16) | copy-start | bytes 2949124
  27.4 0.9 %copy-start.11 = (bf16[3,256,512]{2,1,0:T(8,128)(2,1)}, bf16[3,256,512]{2,1,0:T(8,128)(2,1)S(1)}, u32[]{:S(2)}) copy-start(bf16[3,256,512]{2,1,0:T(8,128)(2,1)S(1)} %get-tuple-element.22.data_own_hbm) | copy-start | bytes 2359300
  28.3 15.7 %collective-permute-start.1 = (bf16[2,256,512]{2,1,0:T(8,128)(2,1)S(1)}, bf16[2,256,512]{2,1,0:T(8,128)(2,1)S(1)}, u32[]{:S(2)}, u32[]{:S(2)}) collective-permute-start(bf16[2,256,512]{2,1,0:T(8,128)(2,1)S(1)} %get-tuple-element.23), channel_id=1, source_target_pairs={{0,16},{16,0},{1,17},{17,1},{2,18},{18,2},{3,19},{19,3},{4,20},{20... | collective-permute-start | bytes 1572872 | tf_op jit(solution)/shard_map/ppermute | solution.py:457
  29.6 6.4 %collective-permute-start.3 = (f32[64,128]{1,0:T(8,128)S(1)}, f32[64,128]{1,0:T(8,128)S(1)}, u32[]{:S(2)}, u32[]{:S(2)}) collective-permute-start(f32[64,128]{1,0:T(8,128)S(1)} %pad_maximum_fusion.1), channel_id=1, source_target_pairs={{0,7},{1,6},{2,5},{3,4},{4,3},{5,2},{6,1},{7,0},{8,15},{9,14},{10,... | collective-permute-start | bytes 98312 | tf_op jit(solution)/shard_map/ppermute | solution.py:447
  36.0 9.4 %copy-start.12 = (f32[64,128]{1,0:T(8,128)}, f32[64,128]{1,0:T(8,128)S(1)}, u32[]{:S(2)}) copy-start(f32[64,128]{1,0:T(8,128)S(1)} %pad_maximum_fusion.2.pay_hbm) | copy-start | bytes 98308
  36.0 8.0 %collective-permute-start.4 = (f32[64,128]{1,0:T(8,128)S(1)}, f32[64,128]{1,0:T(8,128)S(1)}, u32[]{:S(2)}, u32[]{:S(2)}) collective-permute-start(f32[64,128]{1,0:T(8,128)S(1)} %pad_maximum_fusion.2.pay_hbm), channel_id=1, source_target_pairs={{0,15},{1,14},{2,13},{3,12},{4,11},{5,10},{6,9},{7,8},{8,7},{9,6},... | collective-permute-start | bytes 98312 | tf_op jit(solution)/shard_map/ppermute | solution.py:447
  44.0 1.4 %copy-start.7 = (f32[64,128]{1,0:T(8,128)}, f32[64,128]{1,0:T(8,128)S(1)}, u32[]{:S(2)}) copy-start(f32[64,128]{1,0:T(8,128)S(1)} %collective-permute-done.4.got_hbm.got_d) | copy-start | bytes 98308
  44.0 1.4 %copy-start.13 = (bf16[2,256,512]{2,1,0:T(8,128)(2,1)}, bf16[2,256,512]{2,1,0:T(8,128)(2,1)S(1)}, u32[]{:S(2)}) copy-start(bf16[2,256,512]{2,1,0:T(8,128)(2,1)S(1)} %collective-permute-done.1.data_got_hbm) | copy-start | bytes 1572868
  45.4 32.6 %copy-start.6 = (f32[12,8,512]{2,1,0:T(8,128)S(1)}, f32[12,8,512]{2,1,0:T(8,128)}, u32[]{:S(2)}) copy-start(f32[12,8,512]{2,1,0:T(8,128)} %copy-done.5) | copy-start | bytes 589828
  67.0 16.4 %collective-permute-start.5 = (bf16[16,1024]{1,0:T(8,128)(2,1)S(1)}, bf16[16,1024]{1,0:T(8,128)(2,1)S(1)}, u32[]{:S(2)}, u32[]{:S(2)}) collective-permute-start(bf16[16,1024]{1,0:T(8,128)(2,1)S(1)} %get-tuple-element.27), channel_id=1, source_target_pairs={{0,0},{1,16},{2,32},{3,48},{4,64},{5,80},{6,96},{7,112},{8,128},{9... | collective-permute-start | bytes 98312 | tf_op jit(solution)/shard_map/ppermute | solution.py:488
  75.3 11.6 %collective-permute-start.6 = (bf16[16,1024]{1,0:T(8,128)(2,1)S(1)}, bf16[16,1024]{1,0:T(8,128)(2,1)S(1)}, u32[]{:S(2)}, u32[]{:S(2)}) collective-permute-start(bf16[16,1024]{1,0:T(8,128)(2,1)S(1)} %get-tuple-element.28), channel_id=1, source_target_pairs={{0,1},{1,17},{2,33},{3,49},{4,65},{5,81},{6,97},{7,113},{8,129},{9... | collective-permute-start | bytes 98312 | tf_op jit(solution)/shard_map/ppermute | solution.py:491
  75.8 7.6 %collective-permute-start.7 = (bf16[8,1024]{1,0:T(8,128)(2,1)S(1)}, bf16[8,1024]{1,0:T(8,128)(2,1)S(1)}, u32[]{:S(2)}, u32[]{:S(2)}) collective-permute-start(bf16[8,1024]{1,0:T(8,128)(2,1)S(1)} %get-tuple-element.30), channel_id=1, source_target_pairs={{0,128},{128,0},{1,129},{129,1},{2,130},{130,2},{3,131},{131,3},{4... | collective-permute-start | bytes 49160 | tf_op jit(solution)/shard_map/ppermute | solution.py:494
  78.1 0.8 copy-start.8

commit v6 on v5

--- a/solution.py
+++ b/solution.py
@@ -275,11 +275,11 @@
         copies[-1].start()
         return copies[-1]
 
+    received = [fetch(recv_hbm.at[pl.ds(8 * n, 8)], recv_ref.at[pl.ds(8 * n, 8)]) for n in range(4)]
     small = [
         fetch(pay_hbm, bins_ref.at[0]), fetch(got_hbm, bins_ref.at[1]),
         fetch(measured_hbm, counts_ref.at[0]), fetch(background_hbm, counts_ref.at[1]),
     ]
-    received = [fetch(recv_hbm.at[pl.ds(8 * n, 8)], recv_ref.at[pl.ds(8 * n, 8)]) for n in range(4)]
     tables = [
         fetch(ytab_hbm.at[pl.ds(256 * n, 256)], ytab_ref.at[pl.ds(256 * n, 256)]) for n in range(4)
     ]
@@ -290,11 +290,6 @@
         fetch(data_own_hbm.at[2], mask_ref),
     ]
     tiles = [fetch(tiles_hbm.at[pl.ds(4 * n, 4)], tiles_ref.at[pl.ds(4 * n, 4)]) for n in range(4)]
-    for copy in small:
-        copy.wait()
-    ratio_now = ratio_rows(
-        block_ref, view_ref, bins_ref.at[0], bins_ref.at[1], counts_ref.at[0], counts_ref.at[1], ratio, gathered
-    )
     for copy in received:
         copy.wait()
 
@@ -327,6 +322,11 @@
                 sens[rows, lanes_im] = s_im
                 images[rows, lanes] = (s_re * mr_re[:, lanes] - s_im * mr_im[:, lanes]).astype(bf16)
                 images[rows, lanes_im] = (s_re * mr_im[:, lanes] + s_im * mr_re[:, lanes]).astype(bf16)
+    for copy in small:
+        copy.wait()
+    ratio_now = ratio_rows(
+        block_ref, view_ref, bins_ref.at[0], bins_ref.at[1], counts_ref.at[0], counts_ref.at[1], ratio, gathered
+    )
     for copy in tables:
         copy.wait()
     kyrows[...] = jnp.dot(images[...], ytab_ref[...], preferred_element_type=f32).astype(bf16)

time: 88.1 us -> 88 us (level)
  no operation moved by 1% of the time
where the time goes in v6:
time: 88 us; the launch traced here: 87.6 us
  starting transfers between devices  31.2 us (35%)
  waiting for transfers between devices  22.2 us (25%)
  Pallas kernels  15.5 us (18%)
  blocking collectives  13.1 us (15%)
  local copies, waits for them, and re-layouts  4.66 us (5%)
    ppermute x4, waiting for transfers between devices, on_device(): lax.ppermute(pay, GZ, [(i, i ^ 2 ** (step + 1) - 1) for i in range(16)])  13.8 us
    all_to_all x1, blocking collectives, on_device(): lax.all_to_all(parts, ('x', 'c'), split_axis=0, concat_axis=0, tiled=True)  13.1 us
    ppermute x4, starting transfers between devices, on_device(): lax.ppermute(pay, GZ, [(i, i ^ 2 ** (step + 1) - 1) for i in range(16)])  10.9 us
    all_to_all x1, starting transfers between devices, on_device(): lax.all_to_all(sent, ('c', 'y', 'zl'), split_axis=0, concat_axis=0, tiled...  9.18 us
    pallas_call x1, Pallas kernels, on_device(): call(coil_kernel, sds((8, 4 * ZS, ROW), bf16), [SMEM] * 4 + [ANY] * 10, [...  8.35 us
    ppermute x1, starting transfers between devices, on_device(): lax.ppermute(mr_own, GRP + GZ, [((zh * 8 + p) * 16 + j, j * 16 + 2 * p +...  8.26 us
    unnamed x28, local copies, waits for them, and re-layouts  4.58 us
    pallas_call x1, Pallas kernels, on_device(): call(pack_kernel, sds((32, CHUNK, 128), bf16), [SMEM] + [ANY] * 2, [pltpu...  3.85 us
  transfers between devices with their start and end apart: 9, of which 7 were waited for; matrix products, arithmetic and copies ran while one was open for 0% of the time, Pallas kernels for 3%

profile of v6, /device:TPU:6, one launch (start us, length us, event | category | flops | bytes accessed | tf_op | source)
XLA Modules:
  0.0 87.6 jit_solution(2191539645963243305)
XLA Ops:
  0.6 0.0 copy-start.1
  0.6 3.8 %pack.1 = bf16[32,152,128]{2,1,0:T(8,128)(2,1)} custom-call(s32[1]{0:T(128)} %bitcast.1.core_ref, bf16[512,960]{1,0:T(8,128)(2,1)} %bitcast.23, f32[256,960]{1,0:T(8,128)} %bitcast.18), custom_call_target="tpu_custom_call" | custom-call | flops 1000000000 | bytes 4000000 | tf_op jit(solution)/shard_map/pack/pallas_call | solution.py:421
  4.5 0.0 copy-start
  4.5 0.0 copy-start.9
  4.5 0.0 copy-start.10
  4.5 0.0 copy-start.4
  4.5 9.2 %all-to-all-start = ((bf16[32,152,128]{2,1,0:T(8,128)(2,1)}), bf16[32,152,128]{2,1,0:T(8,128)(2,1)}, u32[]{:S(2)}, u32[]{:S(2)}) async-start(bf16[32,152,128]{2,1,0:T(8,128)(2,1)} %pack.1), calls=%async_computation | async-start | bytes 2490368 | tf_op jit(solution)/shard_map/all_to_all | solution.py:430
  13.8 0.1 stack.35.info_ref
  13.9 0.0 copy-done.1
  13.9 0.0 copy-done
  13.9 0.0 copy-done.9
  13.9 0.0 copy-done.10
  13.9 0.0 copy-start.3
  13.9 1.0 %copy-done.3 = f32[8,32,480]{2,1,0:T(8,128)S(1)} copy-done((f32[8,32,480]{2,1,0:T(8,128)S(1)}, f32[8,32,480]{2,1,0:T(8,128)}, u32[]{:S(2)}) %copy-start.3) | copy-done | bytes 491544
  15.0 1.1 %project.1 = (f32[64,128]{1,0:T(8,128)S(1)}, f32[12,8,512]{2,1,0:T(8,128)S(1)}, f32[48,128]{1,0:T(8,128)S(1)}, f32[48,128]{1,0:T(8,128)S(1)}) custom-call(s32[8]{0:T(128)S(1)} %stack.35.info_ref, s32[16]{0:T(128)S(1)} %copy-done.9, s32[16]{0:T(128)S(1)} %copy-done.10, s32[4]{0:T(128)S(1)} %add_clamp_fusion.xs_ref, f32[256,480]{1,0:T(8,128)S(1)} %bitcast.21, ...), custom_call_target="tpu_custom_call" | custom-call | flops 10000000 | bytes 4000000 | tf_op jit(solution)/shard_map/project/pallas_call | solution.py:439
  16.1 0.0 copy-start.5
  16.1 0.7 copy-done.5
  16.7 1.7 %collective-permute-start = (f32[64,128]{1,0:T(8,128)S(1)}, f32[64,128]{1,0:T(8,128)S(1)}, u32[]{:S(2)}, u32[]{:S(2)}) collective-permute-start(f32[64,128]{1,0:T(8,128)S(1)} %get-tuple-element.20), channel_id=1, source_target_pairs={{0,1},{1,0},{2,3},{3,2},{4,5},{5,4},{6,7},{7,6},{8,9},{9,8},{10,11... | collective-permute-start | bytes 98312 | tf_op jit(solution)/shard_map/ppermute | solution.py:447
  18.5 5.3 %collective-permute-done.got_a = f32[64,128]{1,0:T(8,128)S(1)} collective-permute-done((f32[64,128]{1,0:T(8,128)S(1)}, f32[64,128]{1,0:T(8,128)S(1)}, u32[]{:S(2)}, u32[]{:S(2)}) %collective-permute-start) | collective-permute-done | bytes 32800 | tf_op jit(solution)/shard_map/ppermute | solution.py:447
  23.8 2.0 %collective-permute-start.2 = (f32[64,128]{1,0:T(8,128)S(1)}, f32[64,128]{1,0:T(8,128)S(1)}, u32[]{:S(2)}, u32[]{:S(2)}) collective-permute-start(f32[64,128]{1,0:T(8,128)S(1)} %pad_maximum_fusion), channel_id=1, source_target_pairs={{0,3},{1,2},{2,1},{3,0},{4,7},{5,6},{6,5},{7,4},{8,11},{9,10},{10,... | collective-permute-start | bytes 98312 | tf_op jit(solution)/shard_map/ppermute | solution.py:447
  25.8 0.0 copy-done.4
  25.8 1.2 %copy-done.2 = bf16[2,128,2,960]{1,3,2,0:T(8,128)(2,1)S(1)} copy-done((bf16[2,128,2,960]{1,3,2,0:T(8,128)(2,1)S(1)}, bf16[2,128,2,960]{1,3,2,0:T(8,128)(2,1)}, u32[]{:S(2)}) %copy-start.2) | copy-done | bytes 983064
  27.0 0.4 prepare.1
  27.4 0.0 copy-start.11
  27.4 0.9 copy-done.11
  28.3 0.0 collective-permute-start.1
  28.3 1.3 %collective-permute-done.2.got_b = f32[64,128]{1,0:T(8,128)S(1)} collective-permute-done((f32[64,128]{1,0:T(8,128)S(1)}, f32[64,128]{1,0:T(8,128)S(1)}, u32[]{:S(2)}, u32[]{:S(2)}) %collective-permute-start.2) | collective-permute-done | bytes 32800 | tf_op jit(solution)/shard_map/ppermute | solution.py:447
  29.6 1.4 %collective-permute-start.3 = (f32[64,128]{1,0:T(8,128)S(1)}, f32[64,128]{1,0:T(8,128)S(1)}, u32[]{:S(2)}, u32[]{:S(2)}) collective-permute-start(f32[64,128]{1,0:T(8,128)S(1)} %pad_maximum_fusion.1), channel_id=1, source_target_pairs={{0,7},{1,6},{2,5},{3,4},{4,3},{5,2},{6,1},{7,0},{8,15},{9,14},{10,... | collective-permute-start | bytes 98312 | tf_op jit(solution)/shard_map/ppermute | solution.py:447
  31.0 5.0 %collective-permute-done.3.got_c = f32[64,128]{1,0:T(8,128)S(1)} collective-permute-done((f32[64,128]{1,0:T(8,128)S(1)}, f32[64,128]{1,0:T(8,128)S(1)}, u32[]{:S(2)}, u32[]{:S(2)}) %collective-permute-start.3) | collective-permute-done | bytes 32800 | tf_op jit(solution)/shard_map/ppermute | solution.py:447
  36.0 5.9 %collective-permute-start.4 = (f32[64,128]{1,0:T(8,128)S(1)}, f32[64,128]{1,0:T(8,128)S(1)}, u32[]{:S(2)}, u32[]{:S(2)}) collective-permute-start(f32[64,128]{1,0:T(8,128)S(1)} %pad_maximum_fusion.2.pay_hbm), channel_id=1, source_target_pairs={{0,15},{1,14},{2,13},{3,12},{4,11},{5,10},{6,9},{7,8},{8,7},{9,6},... | collective-permute-start | bytes 98312 | tf_op jit(solution)/shard_map/ppermute | solution.py:447
  41.9 2.1 %collective-permute-done.4.got_hbm.got_d = f32[64,128]{1,0:T(8,128)S(1)} collective-permute-done((f32[64,128]{1,0:T(8,128)S(1)}, f32[64,128]{1,0:T(8,128)S(1)}, u32[]{:S(2)}, u32[]{:S(2)}) %collective-permute-start.4) | collective-permute-done | bytes 32800 | tf_op jit(solution)/shard_map/ppermute | solution.py:447
  44.0 0.0 collective-permute-done.1.data_got_hbm
  44.0 1.4 %all-to-all-done.recv_hbm = bf16[32,152,128]{2,1,0:T(8,128)(2,1)} async-done(((bf16[32,152,128]{2,1,0:T(8,128)(2,1)}), bf16[32,152,128]{2,1,0:T(8,128)(2,1)}, u32[]{:S(2)}, u32[]{:S(2)}) %all-to-all-start) | async-done | bytes 1245216 | tf_op jit(solution)/shard_map/all_to_all | solution.py:430
  45.4 0.0 copy-done.12
  45.4 0.0 copy-done.7
  45.4 0.0 copy-done.13
  45.5 8.4 %coils.1 = bf16[8,32,1024]{2,1,0:T(8,128)(2,1)} custom-call(s32[1]{0:T(128)} %bitcast.1.core_ref, s32[16]{0:T(128)} %col_ref.1, s32[16]{0:T(128)} %block_ref.3, s32[16]{0:T(128)} %view_ref.1, bf16[32,152,128]{2,1,0:T(8,128)(2,1)} %all-to-all-done.recv_hbm, bf16[1024,1024]{1,0:T(8,128)(2,1)} %constant.43.clone.ytab_hbm, ...), custom_call_target="tpu_custom_call" | custom-call | flops 5000000000 | bytes 6000000 | tf_op jit(solution)/shard_map/coils/pallas_call | solution.py:466
  53.8 13.1 %all_to_all.10.recv_ref = bf16[8,32,1024]{2,1,0:T(8,128)(2,1)S(1)} all-to-all(bf16[8,32,1024]{2,1,0:T(8,128)(2,1)} %coils.1), channel_id=1, replica_groups=mesh['zh'=2,'x'=4,'c'=2,'zl'=4,'y'=4] {'x','c'}, dimensions={0} | all-to-all | bytes 1048576 | tf_op jit(solution)/shard_map/all_to_all | solution.py:480
  66.9 0.1 sums.1
  67.0 8.3 %collective-permute-start.5 = (bf16[16,1024]{1,0:T(8,128)(2,1)S(1)}, bf16[16,1024]{1,0:T(8,128)(2,1)S(1)}, u32[]{:S(2)}, u32[]{:S(2)}) collective-permute-start(bf16[16,1024]{1,0:T(8,128)(2,1)S(1)} %get-tuple-element.27), channel_id=1, source_target_pairs={{0,0},{1,16},{2,32},{3,48},{4,64},{5,80},{6,96},{7,112},{8,128},{9... | collective-permute-start | bytes 98312 | tf_op jit(solution)/shard_map/ppermute | solution.py:488
  75.3 0.5 collective-permute-start.6
  75.8 2.3 %collective-permute-start.7 = (bf16[8,1024]{1,0:T(8,128)(2,1)S(1)}, bf16[8,1024]{1,0:T(8,128)(2,1)S(1)}, u32[]{:S(2)}, u32[]{:S(2)}) collective-permute-start(bf16[8,1024]{1,0:T(8,128)(2,1)S(1)} %get-tuple-element.30), channel_id=1, source_target_pairs={{0,128},{128,0},{1,129},{129,1},{2,130},{130,2},{3,131},{131,3},{4... | collective-permute-start | bytes 49160 | tf_op jit(solution)/shard_map/ppermute | solution.py:494
  78.0 0.8 copy-done.8
  78.8 1.0 %coupling.1 = (f32[2,8,512]{2,1,0:T(8,128)S(1)}, f32[2,8,1024]{2,1,0:T(8,128)S(1)}) custom-call(s32[8]{0:T(128)S(1)} %stack.35.info_ref, f32[12,8,512]{2,1,0:T(8,128)S(1)} %copy-done.6, f32[64,128]{1,0:T(8,128)S(1)} %collective-permute-done.got_a, f32[64,128]{1,0:T(8,128)S(1)} %collective-permute-done.2.got_b, f32[64,128]{1,0:T(8,128)S(1)} %collective-permute-done.3.got_c, ...), custom_call_target="tpu_custom_call" | custom-call | flops 1000000 | bytes 1000000 | tf_op jit(solution)/shard_map/coupling/pallas_call | solution.py:458
  79.8 3.6 %collective-permute-done.7.pet_b = bf16[8,1024]{1,0:T(8,128)(2,1)S(1)} collective-permute-done((bf16[8,1024]{1,0:T(8,128)(2,1)S(1)}, bf16[8,1024]{1,0:T(8,128)(2,1)S(1)}, u32[]{:S(2)}, u32[]{:S(2)}) %collective-permute-start.7) | collective-permute-done | bytes 16416 | tf_op jit(solution)/shard_map/ppermute | solution.py:494
  83.4 0.0 collective-permute-done.5.mr_a
  83.4 3.4 %collective-permute-done.6.mr_b = bf16[16,1024]{1,0:T(8,128)(2,1)S(1)} collective-permute-done((bf16[16,1024]{1,0:T(8,128)(2,1)S(1)}, bf16[16,1024]{1,0:T(8,128)(2,1)S(1)}, u32[]{:S(2)}, u32[]{:S(2)}) %collective-permute-start.6) | collective-permute-done | bytes 32800 | tf_op jit(solution)/shard_map/ppermute | solution.py:491
  86.8 0.7 final.1
  (15 shorter events, 0.1 us)
Async XLA Ops:
  0.6 13.2 %copy-start.1 = (f32[8,32,960]{2,1,0:T(8,128)S(1)}, f32[8,32,960]{2,1,0:T(8,128)}, u32[]{:S(2)}) copy-start(f32[8,32,960]{2,1,0:T(8,128)} %param.14) | copy-start | bytes 2949124
  4.5 9.4 %copy-start = (bf16[16,128,480]{1,2,0:T(8,128)(2,1)S(1)}, bf16[16,128,480]{1,2,0:T(8,128)(2,1)}, u32[]{:S(2)}) copy-start(bf16[16,128,480]{1,2,0:T(8,128)(2,1)} %param.18) | copy-start | bytes 5898244
  4.5 9.4 %copy-start.9 = (s32[16]{0:T(128)S(1)}, s32[16]{0:T(128)}, u32[]{:S(2)}) copy-start(s32[16]{0:T(128)} %col_ref.1) | copy-start | bytes 196
  4.5 9.4 %copy-start.10 = (s32[16]{0:T(128)S(1)}, s32[16]{0:T(128)}, u32[]{:S(2)}) copy-start(s32[16]{0:T(128)} %block_ref.3) | copy-start | bytes 196
  4.5 21.3 %copy-start.4 = (s32[128,480]{0,1:T(8,128)S(1)}, s32[128,480]{0,1:T(8,128)}, u32[]{:S(2)}) copy-start(s32[128,480]{0,1:T(8,128)} %param.17) | copy-start | bytes 737284
  4.5 40.9 %all-to-all-start = ((bf16[32,152,128]{2,1,0:T(8,128)(2,1)}), bf16[32,152,128]{2,1,0:T(8,128)(2,1)}, u32[]{:S(2)}, u32[]{:S(2)}) async-start(bf16[32,152,128]{2,1,0:T(8,128)(2,1)} %pack.1), calls=%async_computation | async-start | bytes 2490368 | tf_op jit(solution)/shard_map/all_to_all | solution.py:430
  13.9 1.0 %copy-start.3 = (f32[8,32,480]{2,1,0:T(8,128)S(1)}, f32[8,32,480]{2,1,0:T(8,128)}, u32[]{:S(2)}) copy-start(f32[8,32,480]{2,1,0:T(8,128)} %param.13) | copy-start | bytes 1474564
  16.1 0.7 copy-start.5
  16.7 7.1 %collective-permute-start = (f32[64,128]{1,0:T(8,128)S(1)}, f32[64,128]{1,0:T(8,128)S(1)}, u32[]{:S(2)}, u32[]{:S(2)}) collective-permute-start(f32[64,128]{1,0:T(8,128)S(1)} %get-tuple-element.20), channel_id=1, source_target_pairs={{0,1},{1,0},{2,3},{3,2},{4,5},{5,4},{6,7},{7,6},{8,9},{9,8},{10,11... | collective-permute-start | bytes 98312 | tf_op jit(solution)/shard_map/ppermute | solution.py:447
  23.8 5.8 %collective-permute-start.2 = (f32[64,128]{1,0:T(8,128)S(1)}, f32[64,128]{1,0:T(8,128)S(1)}, u32[]{:S(2)}, u32[]{:S(2)}) collective-permute-start(f32[64,128]{1,0:T(8,128)S(1)} %pad_maximum_fusion), channel_id=1, source_target_pairs={{0,3},{1,2},{2,1},{3,0},{4,7},{5,6},{6,5},{7,4},{8,11},{9,10},{10,... | collective-permute-start | bytes 98312 | tf_op jit(solution)/shard_map/ppermute | solution.py:447
  25.8 1.2 %copy-start.2 = (bf16[2,128,2,960]{1,3,2,0:T(8,128)(2,1)S(1)}, bf16[2,128,2,960]{1,3,2,0:T(8,128)(2,1)}, u32[]{:S(2)}) copy-start(bf16[2,128,2,960]{1,3,2,0:T(8,128)(2,1)} %param.16) | copy-start | bytes 2949124
  27.4 0.9 %copy-start.11 = (bf16[3,256,512]{2,1,0:T(8,128)(2,1)}, bf16[3,256,512]{2,1,0:T(8,128)(2,1)S(1)}, u32[]{:S(2)}) copy-start(bf16[3,256,512]{2,1,0:T(8,128)(2,1)S(1)} %get-tuple-element.22.data_own_hbm) | copy-start | bytes 2359300
  28.3 15.7 %collective-permute-start.1 = (bf16[2,256,512]{2,1,0:T(8,128)(2,1)S(1)}, bf16[2,256,512]{2,1,0:T(8,128)(2,1)S(1)}, u32[]{:S(2)}, u32[]{:S(2)}) collective-permute-start(bf16[2,256,512]{2,1,0:T(8,128)(2,1)S(1)} %get-tuple-element.23), channel_id=1, source_target_pairs={{0,16},{16,0},{1,17},{17,1},{2,18},{18,2},{3,19},{19,3},{4,20},{20... | collective-permute-start | bytes 1572872 | tf_op jit(solution)/shard_map/ppermute | solution.py:457
  29.6 6.4 %collective-permute-start.3 = (f32[64,128]{1,0:T(8,128)S(1)}, f32[64,128]{1,0:T(8,128)S(1)}, u32[]{:S(2)}, u32[]{:S(2)}) collective-permute-start(f32[64,128]{1,0:T(8,128)S(1)} %pad_maximum_fusion.1), channel_id=1, source_target_pairs={{0,7},{1,6},{2,5},{3,4},{4,3},{5,2},{6,1},{7,0},{8,15},{9,14},{10,... | collective-permute-start | bytes 98312 | tf_op jit(solution)/shard_map/ppermute | solution.py:447
  36.0 9.4 %copy-start.12 = (f32[64,128]{1,0:T(8,128)}, f32[64,128]{1,0:T(8,128)S(1)}, u32[]{:S(2)}) copy-start(f32[64,128]{1,0:T(8,128)S(1)} %pad_maximum_fusion.2.pay_hbm) | copy-start | bytes 98308
  36.0 8.0 %collective-permute-start.4 = (f32[64,128]{1,0:T(8,128)S(1)}, f32[64,128]{1,0:T(8,128)S(1)}, u32[]{:S(2)}, u32[]{:S(2)}) collective-permute-start(f32[64,128]{1,0:T(8,128)S(1)} %pad_maximum_fusion.2.pay_hbm), channel_id=1, source_target_pairs={{0,15},{1,14},{2,13},{3,12},{4,11},{5,10},{6,9},{7,8},{8,7},{9,6},... | collective-permute-start | bytes 98312 | tf_op jit(solution)/shard_map/ppermute | solution.py:447
  44.0 1.4 %copy-start.7 = (f32[64,128]{1,0:T(8,128)}, f32[64,128]{1,0:T(8,128)S(1)}, u32[]{:S(2)}) copy-start(f32[64,128]{1,0:T(8,128)S(1)} %collective-permute-done.4.got_hbm.got_d) | copy-start | bytes 98308
  44.0 1.4 %copy-start.13 = (bf16[2,256,512]{2,1,0:T(8,128)(2,1)}, bf16[2,256,512]{2,1,0:T(8,128)(2,1)S(1)}, u32[]{:S(2)}) copy-start(bf16[2,256,512]{2,1,0:T(8,128)(2,1)S(1)} %collective-permute-done.1.data_got_hbm) | copy-start | bytes 1572868
  45.4 32.6 %copy-start.6 = (f32[12,8,512]{2,1,0:T(8,128)S(1)}, f32[12,8,512]{2,1,0:T(8,128)}, u32[]{:S(2)}) copy-start(f32[12,8,512]{2,1,0:T(8,128)} %copy-done.5) | copy-start | bytes 589828
  67.0 16.4 %collective-permute-start.5 = (bf16[16,1024]{1,0:T(8,128)(2,1)S(1)}, bf16[16,1024]{1,0:T(8,128)(2,1)S(1)}, u32[]{:S(2)}, u32[]{:S(2)}) collective-permute-start(bf16[16,1024]{1,0:T(8,128)(2,1)S(1)} %get-tuple-element.27), channel_id=1, source_target_pairs={{0,0},{1,16},{2,32},{3,48},{4,64},{5,80},{6,96},{7,112},{8,128},{9... | collective-permute-start | bytes 98312 | tf_op jit(solution)/shard_map/ppermute | solution.py:488
  75.3 11.6 %collective-permute-start.6 = (bf16[16,1024]{1,0:T(8,128)(2,1)S(1)}, bf16[16,1024]{1,0:T(8,128)(2,1)S(1)}, u32[]{:S(2)}, u32[]{:S(2)}) collective-permute-start(bf16[16,1024]{1,0:T(8,128)(2,1)S(1)} %get-tuple-element.28), channel_id=1, source_target_pairs={{0,1},{1,17},{2,33},{3,49},{4,65},{5,81},{6,97},{7,113},{8,129},{9... | collective-permute-start | bytes 98312 | tf_op jit(solution)/shard_map/ppermute | solution.py:491
  75.8 7.6 %collective-permute-start.7 = (bf16[8,1024]{1,0:T(8,128)(2,1)S(1)}, bf16[8,1024]{1,0:T(8,128)(2,1)S(1)}, u32[]{:S(2)}, u32[]{:S(2)}) collective-permute-start(bf16[8,1024]{1,0:T(8,128)(2,1)S(1)} %get-tuple-element.30), channel_id=1, source_target_pairs={{0,128},{128,0},{1,129},{129,1},{2,130},{130,2},{3,131},{131,3},{4... | collective-permute-start | bytes 49160 | tf_op jit(solution)/shard_map/ppermute | solution.py:494
  78.0 0.8 copy-start.8
